TPU v7x, 32 devices: a whole 2x2x4 slice. The times are simulated.
32 devices in a mesh: dp: 16 (over z, x, core), tensor: 2 (over y).
Axes of the slice: x: 2, y: 2, z: 4, core: 2. Of those that a mesh axis runs over, the one named last changes fastest.
Arguments:
- tokens: bfloat16 [12288, 1152], P(('dp', 'tensor')), may hold values from -6 to 6
- conditions: bfloat16 [48, 1152], P('dp'), may hold values from -6 to 6
- item_grids: int32 [48, 2], P('dp'), may hold values from 8 to 32, as said below
- mod_weight: bfloat16 [1152, 6912], P('dp'), may hold values from -0.25 to 0.25
- query_weight: bfloat16 [1152, 1152], P(None, 'tensor'), may hold values from -0.1875 to 0.1875
- key_weight: bfloat16 [1152, 1152], P(None, 'tensor'), may hold values from -0.1875 to 0.1875
- value_weight: bfloat16 [1152, 1152], P(None, 'tensor'), may hold values from -0.1875 to 0.1875
- proj_weight: bfloat16 [1152, 1152], P('tensor'), may hold values from -0.75 to 0.75
- query_gain: float32 [72], replicated, may hold values from 0.8 to 2
- key_gain: float32 [72], replicated, may hold values from 0.8 to 2
- gate_weight: bfloat16 [1152, 3072], P(None, 'tensor'), may hold values from -0.1875 to 0.1875
- up_weight: bfloat16 [1152, 3072], P(None, 'tensor'), may hold values from -0.1875 to 0.1875
- down_weight: bfloat16 [3072, 1152], P('tensor'), may hold values from -0.21875 to 0.21875
- out_grad: bfloat16 [12288, 1152], P(('dp', 'tensor')), may hold values from -6 to 6
Outputs:
- block_out: bfloat16 [12288, 1152], P(('dp', 'tensor'))
- grad_tokens: bfloat16 [12288, 1152], P(('dp', 'tensor'))
- grad_conditions: float32 [48, 1152], P('dp')
- grad_mod_weight: float32 [1152, 6912], P('dp')
- grad_query_weight: float32 [1152, 1152], P('dp', 'tensor')
- grad_key_weight: float32 [1152, 1152], P('dp', 'tensor')
- grad_value_weight: float32 [1152, 1152], P('dp', 'tensor')
- grad_proj_weight: float32 [1152, 1152], P('tensor', 'dp')
- grad_query_gain: float32 [72], replicated
- grad_key_gain: float32 [72], replicated
- grad_gate_weight: float32 [1152, 3072], P('dp', 'tensor')
- grad_up_weight: float32 [1152, 3072], P('dp', 'tensor')
- grad_down_weight: float32 [3072, 1152], P('tensor', 'dp')
Inputs may be any that keep to these rules, and one draw needn't show every extreme that they name: `item_grids`: every item is (12, 20), (16, 16) or (8, 32) patches; each packed row holds exactly 3 items laid end to end from its first token in order, and the rest of the row is padding.
All inputs are finite; a program needn't handle non-finite values.
Results may differ from a plain program's by a relative error of at most 0.02.
Values may be sent and summed in bfloat16 or wider, within the bound.
A program may use at most 256 MiB of HBM per device.

v0:
```python
import jax
import jax.numpy as jnp
from jax import lax
from jax.sharding import PartitionSpec as P

HD = 72


EPSILON = 1e-06
HIGH = lax.Precision.HIGHEST


def silu_grad(values):
    sigma = jax.nn.sigmoid(values)
    return sigma * (1.0 + values * (1.0 - sigma))


def geometry(row_grids, length):
    heights = row_grids[:, 0]
    widths = row_grids[:, 1]
    item_sizes = heights * widths
    item_ends = jnp.cumsum(item_sizes)
    starts = item_ends - item_sizes
    positions = jnp.arange(length, dtype=jnp.int32)
    member = (positions[:, None] >= starts[None, :]) & (positions[:, None] < item_ends[None, :])
    member_int = member.astype(jnp.int32)
    item_count = row_grids.shape[0]
    valid_tok = jnp.sum(member_int, axis=1) > 0
    item_index = jnp.sum(member_int * jnp.arange(item_count, dtype=jnp.int32)[None, :], axis=1)
    segment = jnp.where(valid_tok, item_index, item_count)
    local_index = positions - jnp.sum(member_int * starts[None, :], axis=1)
    width_tok = jnp.maximum(jnp.sum(member_int * widths[None, :], axis=1), 1)
    row_pos = local_index // width_tok
    col_pos = local_index % width_tok
    allowed = (segment[:, None] == segment[None, :]) & valid_tok[None, :] | (
        positions[:, None] == positions[None, :]
    )
    return (member.astype(jnp.float32), allowed, row_pos, col_pos)


def rope_tables(row_pos, col_pos, head_dim):
    quarter = head_dim // 4
    frequency = 10000.0 ** (-jnp.arange(quarter, dtype=jnp.float32) / quarter)
    along_rows = row_pos.astype(jnp.float32)[:, None] * frequency[None, :]
    along_cols = col_pos.astype(jnp.float32)[:, None] * frequency[None, :]
    angles = jnp.concatenate([along_rows, along_rows, along_cols, along_cols], axis=1)
    return (jnp.cos(angles)[:, None, :], jnp.sin(angles)[:, None, :])


def rotate(values):
    dims_in = values.shape
    quarter = dims_in[2] // 4
    halves_view = values.reshape(dims_in[0], dims_in[1], 2, 2, quarter)
    turned = jnp.concatenate([-halves_view[:, :, :, 1:2], halves_view[:, :, :, 0:1]], axis=3)
    return turned.reshape(dims_in)


def layer_norm(values):
    centred = values - jnp.mean(values, axis=1, keepdims=True)
    inv_std = lax.rsqrt(jnp.mean(centred * centred, axis=1, keepdims=True) + EPSILON)
    return (centred * inv_std, inv_std)


def norm_back(grad_norm, normed, inv_std):
    return inv_std * (
        grad_norm
        - jnp.mean(grad_norm, axis=1, keepdims=True)
        - normed * jnp.mean(grad_norm * normed, axis=1, keepdims=True)
    )


def head_norm(values, gain):
    inv_rms = lax.rsqrt(jnp.mean(values * values, axis=2, keepdims=True) + EPSILON)
    return (values * inv_rms * gain, inv_rms)


def head_norm_back(grad_out, values, inv_rms, gain):
    scaled = grad_out * gain
    grad_in = inv_rms * scaled - values * inv_rms**3 * jnp.mean(
        scaled * values, axis=2, keepdims=True
    )
    grad_gain = jnp.sum(grad_out * values * inv_rms, axis=(0, 1))
    return (grad_in, grad_gain)


def head_columns(matrix, head_index):
    return lax.dynamic_slice_in_dim(matrix, head_index * HD, HD, 1)


def shards(
    tokens,
    conditions,
    item_grids,
    mod_weight,
    query_weight,
    key_weight,
    value_weight,
    proj_weight,
    query_gain,
    key_gain,
    gate_weight,
    up_weight,
    down_weight,
    out_grad,
):
    half_rows = tokens.shape[0]
    length = half_rows * lax.axis_size("tensor")
    first_row = lax.axis_index("tensor") * half_rows
    head_count = query_weight.shape[1] // HD
    score_scale = HD ** (-0.5)
    member, allowed, row_pos, col_pos = geometry(item_grids, length)
    cosine, sine = rope_tables(row_pos, col_pos, HD)
    own_member = lax.dynamic_slice_in_dim(member, first_row, half_rows, 0)
    mod_full = lax.all_gather(mod_weight, "dp", axis=0, tiled=True)
    cond_float = conditions.astype(jnp.float32)
    mod_input = jax.nn.silu(cond_float).astype(jnp.bfloat16)
    modulation = jnp.dot(mod_input, mod_full, preferred_element_type=jnp.float32)
    per_token = jnp.dot(own_member, modulation, precision=HIGH, preferred_element_type=jnp.float32)
    shift_one, scale_one, gate_one, shift_two, scale_two, gate_two = jnp.split(per_token, 6, axis=1)
    tokens_float = tokens.astype(jnp.float32)
    norm_one, inv_one = layer_norm(tokens_float)
    attn_in = (norm_one * (1.0 + scale_one) + shift_one).astype(jnp.bfloat16)
    attn_in_all = lax.all_gather(attn_in, "tensor", axis=0, tiled=True)
    query_pre = jnp.dot(attn_in_all, query_weight, preferred_element_type=jnp.float32).reshape(
        length, head_count, HD
    )
    key_pre = jnp.dot(attn_in_all, key_weight, preferred_element_type=jnp.float32).reshape(
        length, head_count, HD
    )
    values = jnp.dot(attn_in_all, value_weight, preferred_element_type=jnp.float32).astype(
        jnp.bfloat16
    )
    query_normed, query_inv = head_norm(query_pre, query_gain)
    key_normed, key_inv = head_norm(key_pre, key_gain)
    queries = (
        (query_normed * cosine + rotate(query_normed) * sine)
        .reshape(length, head_count * HD)
        .astype(jnp.bfloat16)
    )
    keys = (
        (key_normed * cosine + rotate(key_normed) * sine)
        .reshape(length, head_count * HD)
        .astype(jnp.bfloat16)
    )

    def head_forward(head_index):
        query_head = head_columns(queries, head_index)
        key_head = head_columns(keys, head_index)
        value_head = head_columns(values, head_index)
        scores = (
            jnp.einsum("qd,kd->qk", query_head, key_head, preferred_element_type=jnp.float32)
            * score_scale
        )
        scores = jnp.where(allowed, scores, -1e30)
        row_max = jnp.max(scores, axis=1, keepdims=True)
        exp_scores = jnp.exp(scores - row_max)
        row_total = jnp.sum(exp_scores, axis=1, keepdims=True)
        probs_low = (exp_scores / row_total).astype(jnp.bfloat16)
        head_out = jnp.dot(probs_low, value_head, preferred_element_type=jnp.float32)
        return (head_out, (row_max + jnp.log(row_total))[:, 0])

    head_outs, log_sums = lax.map(head_forward, jnp.arange(head_count))
    heads_out = head_outs.transpose(1, 0, 2).reshape(length, head_count * HD).astype(jnp.bfloat16)
    attn_out = lax.psum_scatter(
        jnp.dot(heads_out, proj_weight, preferred_element_type=jnp.float32).astype(jnp.bfloat16),
        "tensor",
        scatter_dimension=0,
        tiled=True,
    ).astype(jnp.float32)
    resid = tokens_float + gate_one * attn_out
    norm_two, inv_two = layer_norm(resid)
    mlp_in = (norm_two * (1.0 + scale_two) + shift_two).astype(jnp.bfloat16)
    mlp_in_all = lax.all_gather(mlp_in, "tensor", axis=0, tiled=True)
    gate_pre = jnp.dot(mlp_in_all, gate_weight, preferred_element_type=jnp.float32)
    up_pre = jnp.dot(mlp_in_all, up_weight, preferred_element_type=jnp.float32)
    silu_gate = jax.nn.silu(gate_pre)
    hidden = (silu_gate * up_pre).astype(jnp.bfloat16)
    mlp_out = lax.psum_scatter(
        jnp.dot(hidden, down_weight, preferred_element_type=jnp.float32).astype(jnp.bfloat16),
        "tensor",
        scatter_dimension=0,
        tiled=True,
    ).astype(jnp.float32)
    block_out = (resid + gate_two * mlp_out).astype(jnp.bfloat16)
    grad_out = out_grad.astype(jnp.float32)
    grad_mlp = (gate_two * grad_out).astype(jnp.bfloat16)
    grad_gate_two = grad_out * mlp_out
    grad_mlp_all = lax.all_gather(grad_mlp, "tensor", axis=0, tiled=True)
    grad_hidden = jnp.einsum(
        "rd,fd->rf", grad_mlp_all, down_weight, preferred_element_type=jnp.float32
    )
    part_down = jnp.einsum("rf,rd->fd", hidden, grad_mlp_all, preferred_element_type=jnp.float32)
    grad_gate_pre = (grad_hidden * up_pre * silu_grad(gate_pre)).astype(jnp.bfloat16)
    grad_up_pre = (grad_hidden * silu_gate).astype(jnp.bfloat16)
    part_gate = jnp.einsum(
        "rd,rf->df", mlp_in_all, grad_gate_pre, preferred_element_type=jnp.float32
    )
    part_up = jnp.einsum("rd,rf->df", mlp_in_all, grad_up_pre, preferred_element_type=jnp.float32)
    first_term = jnp.einsum(
        "rf,df->rd", grad_gate_pre, gate_weight, preferred_element_type=jnp.float32
    )
    grad_mlp_in = lax.psum_scatter(
        (
            first_term
            + jnp.einsum("rf,df->rd", grad_up_pre, up_weight, preferred_element_type=jnp.float32)
        ).astype(jnp.bfloat16),
        "tensor",
        scatter_dimension=0,
        tiled=True,
    ).astype(jnp.float32)
    grad_scale_two = grad_mlp_in * norm_two
    grad_resid = grad_out + norm_back(grad_mlp_in * (1.0 + scale_two), norm_two, inv_two)
    grad_gate_one = grad_resid * attn_out
    grad_attn = (gate_one * grad_resid).astype(jnp.bfloat16)
    grad_attn_all = lax.all_gather(grad_attn, "tensor", axis=0, tiled=True)
    part_proj = jnp.einsum(
        "rc,rd->cd", heads_out, grad_attn_all, preferred_element_type=jnp.float32
    )
    grad_heads = jnp.einsum(
        "rd,cd->rc", grad_attn_all, proj_weight, preferred_element_type=jnp.float32
    ).astype(jnp.bfloat16)

    def head_backward(head_index):
        query_head = head_columns(queries, head_index)
        key_head = head_columns(keys, head_index)
        value_head = head_columns(values, head_index)
        grad_head = head_columns(grad_heads, head_index)
        log_total = lax.dynamic_index_in_dim(log_sums, head_index, 0, keepdims=False)
        scores = (
            jnp.einsum("qd,kd->qk", query_head, key_head, preferred_element_type=jnp.float32)
            * score_scale
        )
        attn_probs = jnp.exp(jnp.where(allowed, scores, -1e30) - log_total[:, None])
        grad_probs = jnp.einsum(
            "qd,kd->qk", grad_head, value_head, preferred_element_type=jnp.float32
        )
        inner_sum = jnp.sum(attn_probs * grad_probs, axis=1, keepdims=True)
        grad_scores = (attn_probs * (grad_probs - inner_sum)).astype(jnp.bfloat16)
        grad_query_head = (
            jnp.einsum("qk,kd->qd", grad_scores, key_head, preferred_element_type=jnp.float32)
            * score_scale
        )
        grad_key_head = (
            jnp.einsum("qk,qd->kd", grad_scores, query_head, preferred_element_type=jnp.float32)
            * score_scale
        )
        grad_value_head = jnp.einsum(
            "qk,qd->kd",
            attn_probs.astype(jnp.bfloat16),
            grad_head,
            preferred_element_type=jnp.float32,
        )
        return (grad_query_head, grad_key_head, grad_value_head)

    grad_query_heads, grad_key_heads, grad_value_heads = lax.map(
        head_backward, jnp.arange(head_count)
    )
    grad_query_rot = grad_query_heads.transpose(1, 0, 2)
    grad_key_rot = grad_key_heads.transpose(1, 0, 2)
    grad_values = (
        grad_value_heads.transpose(1, 0, 2).reshape(length, head_count * HD).astype(jnp.bfloat16)
    )
    grad_query_normed = grad_query_rot * cosine - rotate(grad_query_rot * sine)
    grad_key_normed = grad_key_rot * cosine - rotate(grad_key_rot * sine)
    grad_query_pre, part_query_gain = head_norm_back(
        grad_query_normed, query_pre, query_inv, query_gain
    )
    grad_key_pre, part_key_gain = head_norm_back(grad_key_normed, key_pre, key_inv, key_gain)
    grad_query_low = grad_query_pre.reshape(length, head_count * HD).astype(jnp.bfloat16)
    grad_key_low = grad_key_pre.reshape(length, head_count * HD).astype(jnp.bfloat16)
    part_query = jnp.einsum(
        "rd,rc->dc", attn_in_all, grad_query_low, preferred_element_type=jnp.float32
    )
    part_key = jnp.einsum(
        "rd,rc->dc", attn_in_all, grad_key_low, preferred_element_type=jnp.float32
    )
    part_value = jnp.einsum(
        "rd,rc->dc", attn_in_all, grad_values, preferred_element_type=jnp.float32
    )
    summed = jnp.einsum(
        "rc,dc->rd", grad_query_low, query_weight, preferred_element_type=jnp.float32
    )
    summed = summed + jnp.einsum(
        "rc,dc->rd", grad_key_low, key_weight, preferred_element_type=jnp.float32
    )
    grad_attn_in = lax.psum_scatter(
        (
            summed
            + jnp.einsum("rc,dc->rd", grad_values, value_weight, preferred_element_type=jnp.float32)
        ).astype(jnp.bfloat16),
        "tensor",
        scatter_dimension=0,
        tiled=True,
    ).astype(jnp.float32)
    grad_scale_one = grad_attn_in * norm_one
    grad_tokens = (
        grad_resid + norm_back(grad_attn_in * (1.0 + scale_one), norm_one, inv_one)
    ).astype(jnp.bfloat16)
    grad_per_token = jnp.concatenate(
        [grad_attn_in, grad_scale_one, grad_gate_one, grad_mlp_in, grad_scale_two, grad_gate_two],
        axis=1,
    )
    part_modulation = jnp.einsum(
        "rs,rc->sc", own_member, grad_per_token, precision=HIGH, preferred_element_type=jnp.float32
    )
    grad_modulation, tensor_query_gain, tensor_key_gain = (
        lax.psum(part_modulation.astype(jnp.bfloat16), "tensor").astype(jnp.float32),
        lax.psum(part_query_gain.astype(jnp.bfloat16), "tensor").astype(jnp.float32),
        lax.psum(part_key_gain.astype(jnp.bfloat16), "tensor").astype(jnp.float32),
    )
    grad_mod_low = grad_modulation.astype(jnp.bfloat16)
    grad_conditions = silu_grad(cond_float) * jnp.einsum(
        "sc,dc->sd", grad_mod_low, mod_full, preferred_element_type=jnp.float32
    )
    grad_query_gain, grad_key_gain = lax.psum((tensor_query_gain, tensor_key_gain), "dp")
    inputs_all, grads_items = (
        lax.all_gather(mod_input, "dp", axis=0, tiled=True),
        lax.all_gather(grad_mod_low, "dp", axis=0, tiled=True),
    )
    owned_rows = mod_weight.shape[0]
    own_inputs = lax.dynamic_slice_in_dim(
        inputs_all, lax.axis_index("dp") * owned_rows, owned_rows, 1
    )
    sum_mod = jnp.einsum("sd,sc->dc", own_inputs, grads_items, preferred_element_type=jnp.float32)
    sum_query, sum_key, sum_value, sum_proj, sum_gate, sum_up, sum_down = (
        lax.psum_scatter(part_query, "dp", scatter_dimension=0, tiled=True),
        lax.psum_scatter(part_key, "dp", scatter_dimension=0, tiled=True),
        lax.psum_scatter(part_value, "dp", scatter_dimension=0, tiled=True),
        lax.psum_scatter(part_proj, "dp", scatter_dimension=1, tiled=True),
        lax.psum_scatter(part_gate, "dp", scatter_dimension=0, tiled=True),
        lax.psum_scatter(part_up, "dp", scatter_dimension=0, tiled=True),
        lax.psum_scatter(part_down, "dp", scatter_dimension=1, tiled=True),
    )
    return (
        block_out,
        grad_tokens,
        grad_conditions,
        sum_mod,
        sum_query,
        sum_key,
        sum_value,
        sum_proj,
        grad_query_gain,
        grad_key_gain,
        sum_gate,
        sum_up,
        sum_down,
    )


def solution(mesh):
    return jax.shard_map(
        shards,
        mesh=mesh,
        in_specs=(
            P(("dp", "tensor"), None),
            P("dp", None),
            P("dp", None),
            P("dp", None),
            P(None, "tensor"),
            P(None, "tensor"),
            P(None, "tensor"),
            P("tensor", None),
            P(),
            P(),
            P(None, "tensor"),
            P(None, "tensor"),
            P("tensor", None),
            P(("dp", "tensor"), None),
        ),
        out_specs=(
            P(("dp", "tensor"), None),
            P(("dp", "tensor"), None),
            P("dp", None),
            P("dp", None),
            P("dp", "tensor"),
            P("dp", "tensor"),
            P("dp", "tensor"),
            P("tensor", "dp"),
            P(),
            P(),
            P("dp", "tensor"),
            P("dp", "tensor"),
            P("tensor", "dp"),
        ),
        check_vma=False,
    )
```

profile of v0, /device:TPU:0, one launch (start us, length us, event | category | flops | bytes accessed | tf_op | source)
XLA Modules:
  0.0 1322.8 jit_solution(7781278319035976459)
XLA Ops:
  14.3 120.2 %all-gather.8.cloned.1.call-done = bf16[1152,6912]{1,0:T(8,128)(2,1)} async-done(((bf16[72,6912]{1,0:T(8,128)(2,1)}), bf16[1152,6912]{1,0:T(8,128)(2,1)}) %all-gather.8.cloned.1.call-update) | async-done | bytes 15925264 | tf_op jit(solution)/shard_map/all_gather | solution.py:114
  134.5 7.7 fusion.92
  142.2 4.4 fusion.85
  146.6 4.0 copy-done.2
  157.0 22.8 %all-gather.10.cloned.1.call-done = bf16[768,1152]{1,0:T(8,128)(2,1)} async-done(((bf16[384,1152]{1,0:T(8,128)(2,1)}), bf16[768,1152]{1,0:T(8,128)(2,1)}) %all-gather.10.cloned.1.call-update) | async-done | bytes 1769488 | tf_op jit(solution)/shard_map/all_gather | solution.py:123
  179.8 4.1 convolution_convert_fusion.4
  186.1 4.4 fusion.97
  195.7 3.8 fusion.96
  218.6 5.1 fusion.64
  229.1 57.7 %while.28 = (s32[]{:T(128)}, bf16[8,768,72]{1,2,0:T(8,128)(2,1)}, f32[8,768]{1,0:T(8,128)}, s32[8]{0:T(128)S(1)}, bf16[768,576]{1,0:T(8,128)(2,1)}, /*index=5*/b...) while((s32[]{:T(128)}, bf16[8,768,72]{1,2,0:T(8,128)(2,1)}, ...), condition=%wide.region_12.13_spmd.clone, body=%wide.region_9.12_spmd.clone.sunk | while | flops 176946432 | bytes 7936203 | solution.py:162
  286.9 4.6 convolution_convert_fusion.2
  291.7 28.1 %reduce-scatter.20.cloned.1.call-done = bf16[384,1152]{1,0:T(8,128)(2,1)} async-done(((bf16[768,1152]{1,0:T(8,128)(2,1)}), bf16[384,1152]{1,0:T(8,128)(2,1)}) %reduce-scatter.20.cloned.1.call-update) | async-done | bytes 884752 | tf_op jit(solution)/shard_map/reduce_scatter | solution.py:164
  324.0 4.2 fusion.57
  328.9 28.9 %all-gather.12.cloned.1.call-done = bf16[768,1152]{1,0:T(8,128)(2,1)} async-done(((bf16[384,1152]{1,0:T(8,128)(2,1)}), bf16[768,1152]{1,0:T(8,128)(2,1)}) %all-gather.12.cloned.1.call-update) | async-done | bytes 1769488 | tf_op jit(solution)/shard_map/all_gather | solution.py:173
  357.8 8.0 fusion.99
  365.8 5.0 fusion.98
  370.8 18.5 %all-gather.14.cloned.1.call-done = bf16[768,1152]{1,0:T(8,128)(2,1)} async-done(((bf16[384,1152]{1,0:T(8,128)(2,1)}), bf16[768,1152]{1,0:T(8,128)(2,1)}) %all-gather.14.cloned.1.call-update) | async-done | bytes 1769488 | tf_op jit(solution)/shard_map/all_gather | solution.py:188
  389.3 8.8 multiply_convert_fusion.1
  398.2 3.2 fusion.100
  401.9 4.4 fusion.39
  406.4 6.2 convolution_convert_fusion.1
  413.1 21.7 %reduce-scatter.24.cloned.1.call-done = bf16[384,1152]{1,0:T(8,128)(2,1)} async-done(((bf16[768,1152]{1,0:T(8,128)(2,1)}), bf16[384,1152]{1,0:T(8,128)(2,1)}) %reduce-scatter.24.cloned.1.call-update) | async-done | bytes 884752 | tf_op jit(solution)/shard_map/reduce_scatter | solution.py:202
  437.2 28.1 %reduce-scatter.22.cloned.1.call-done = bf16[384,1152]{1,0:T(8,128)(2,1)} async-done(((bf16[768,1152]{1,0:T(8,128)(2,1)}), bf16[384,1152]{1,0:T(8,128)(2,1)}) %reduce-scatter.22.cloned.1.call-update) | async-done | bytes 884752 | tf_op jit(solution)/shard_map/reduce_scatter | solution.py:178
  465.3 4.6 multiply_convert_fusion.4
  470.0 29.5 %all-gather.16.cloned.1.call-done = bf16[768,1152]{1,0:T(8,128)(2,1)} async-done(((bf16[384,1152]{1,0:T(8,128)(2,1)}), bf16[768,1152]{1,0:T(8,128)(2,1)}) %all-gather.16.cloned.1.call-update) | async-done | bytes 1769488 | tf_op jit(solution)/shard_map/all_gather | solution.py:215
  499.5 4.1 convolution_convert_fusion.3
  504.5 203.0 %while.29 = (s32[]{:T(128)}, f32[8,768,72]{1,0,2:T(8,128)}, f32[8,768,72]{1,0,2:T(8,128)}, bf16[8,768,72]{1,2,0:T(8,128)(2,1)}, s32[8]{0:T(128)S(1)}, /*index=5*...) while((s32[]{:T(128)}, f32[8,768,72]{1,0,2:T(8,128)}, ...), condition=%wide.region_22.23_spmd.clone, body=%wide.region_20.22_spmd.clone.sunk | while | flops 432450816 | bytes 21359900 | solution.py:255
  519.0 5.5 dynamic_update_slice.33
  524.4 5.5 dynamic_update_slice.32
  544.3 5.5 dynamic_update_slice.33
  549.8 5.5 dynamic_update_slice.32
  569.7 5.5 dynamic_update_slice.33
  575.2 5.5 dynamic_update_slice.32
  595.1 5.5 dynamic_update_slice.33
  600.6 5.5 dynamic_update_slice.32
  620.5 5.5 dynamic_update_slice.33
  626.0 5.5 dynamic_update_slice.32
  645.8 5.5 dynamic_update_slice.33
  651.3 5.5 dynamic_update_slice.32
  671.2 5.5 dynamic_update_slice.33
  676.7 5.5 dynamic_update_slice.32
  696.6 5.5 dynamic_update_slice.33
  702.1 5.5 dynamic_update_slice.32
  713.5 3.9 multiply_reduce_fusion.1
  729.0 4.7 fusion.105
  735.7 3.2 fusion.104
  740.1 3.2 fusion.102
  744.5 3.2 fusion.103
  749.1 7.5 fusion.108
  758.1 7.4 fusion.107
  765.6 7.6 fusion.106
  773.9 22.3 %all-gather = bf16[16,3,1152]{2,1,0:T(4,128)(2,1)S(1)} all-gather(bf16[1,3,1152]{2,1,0:T(4,128)(2,1)S(1)} %fusion.91), channel_id=1, replica_groups=mesh['dp'=16,'tensor'=2] {'dp'}, dimensions={0}, use_global_device_ids=true | all-gather | bytes 117504 | tf_op jit(solution)/shard_map/all_gather | solution.py:317
  800.9 3.3 fusion.54
  807.9 3.6 convolution_convert_fusion
  811.5 7.4 all-reduce.5
  819.5 20.9 %all-gather.1 = bf16[16,3,6912]{2,1,0:T(4,128)(2,1)S(1)} all-gather(bf16[1,3,6912]{2,1,0:T(4,128)(2,1)S(1)} %bitcast.176), channel_id=1, replica_groups=mesh['dp'=16,'tensor'=2] {'dp'}, dimensions={0}, use_global_device_ids=true | all-gather | bytes 705024 | tf_op jit(solution)/shard_map/all_gather | solution.py:318
  841.0 32.0 %all-reduce.4 = (f32[72]{0:T(128)}, f32[72]{0:T(128)}) all-reduce(bf16[72]{0:T(256)(128)(2,1)S(1)} %get-tuple-element.332, bf16[72]{0:T(256)(128)(2,1)S(1)} %get-tuple-element.333), channel_id=1, replica_groups=mesh['dp'=16,'tensor'=2] {'dp'}, use_global_device_ids=true, to_apply=%region_35.36 | all-reduce | flops 144 | bytes 864 | tf_op jit(solution)/shard_map/psum | solution.py:315
  875.6 10.5 convolution_multiply_fusion.2
  886.1 10.1 reduce-scatter.38.cloned.1.call-done
  896.2 68.7 %reduce-scatter.34.cloned.1.call-done = f32[72,576]{1,0:T(8,128)} async-done(((f32[1152,576]{1,0:T(8,128)}), f32[72,576]{1,0:T(8,128)}) %reduce-scatter.34.cloned.1.call-update) | async-done | bytes 165904
  964.9 68.8 %reduce-scatter.36.cloned.1.call-done = f32[72,576]{1,0:T(8,128)} async-done(((f32[1152,576]{1,0:T(8,128)}), f32[72,576]{1,0:T(8,128)}) %reduce-scatter.36.cloned.1.call-update) | async-done | bytes 165904
  1033.7 93.5 %reduce-scatter.32.cloned.1.call-done = f32[1536,72]{0,1:T(8,128)} async-done(((f32[1536,1152]{0,1:T(8,128)}), f32[1536,72]{0,1:T(8,128)}) %reduce-scatter.32.cloned.1.call-update) | async-done | bytes 442384 | tf_op jit(solution)/shard_map/reduce_scatter | solution.py:332
  1127.3 94.5 %reduce-scatter.30.cloned.1.call-done = f32[72,1536]{1,0:T(8,128)} async-done(((f32[1152,1536]{1,0:T(8,128)}), f32[72,1536]{1,0:T(8,128)}) %reduce-scatter.30.cloned.1.call-update) | async-done | bytes 442384 | tf_op jit(solution)/shard_map/reduce_scatter | solution.py:331
  1221.8 94.0 %reduce-scatter.28.cloned.1.call-done = f32[72,1536]{1,0:T(8,128)} async-done(((f32[1152,1536]{1,0:T(8,128)}), f32[72,1536]{1,0:T(8,128)}) %reduce-scatter.28.cloned.1.call-update) | async-done | bytes 442384 | tf_op jit(solution)/shard_map/reduce_scatter | solution.py:330
  (397 shorter events, 238.3 us)
Async XLA Ops:
  7.2 382.2 %copy-start = (bf16[1536,1152]{1,0:T(8,128)(2,1)S(1)}, bf16[1536,1152]{1,0:T(8,128)(2,1)}, u32[]{:S(2)}) copy-start(bf16[1536,1152]{1,0:T(8,128)(2,1)} %param.30) | copy-start | bytes 10616836
  7.2 127.3 %copy-start.35 = (bf16[3,1152]{1,0:T(4,128)(2,1)S(1)}, bf16[3,1152]{1,0:T(4,128)(2,1)}, u32[]{:S(2)}) copy-start(bf16[3,1152]{1,0:T(4,128)(2,1)} %param.19) | copy-start | bytes 20740
  7.2 127.3 %all-gather.8.cloned.1.call-start = ((), (), s32[]{:S(2)}) async-start(), calls=%async_computation.11 | async-start | bytes 16920576 | tf_op jit(solution)/shard_map/all_gather | solution.py:114
  7.9 171.8 %all-gather.10.cloned.1.call-start = ((), (), s32[]{:S(2)}) async-start(), calls=%async_computation.12 | async-start | bytes 2654208 | tf_op jit(solution)/shard_map/all_gather | solution.py:123
  10.0 2.9 copy-start.55
  10.0 3.0 copy-start.59
  11.4 135.1 %copy-start.42 = (f32[384]{0:T(512)}, f32[384]{0:T(512)S(1)}, u32[]{:S(2)}) copy-start(f32[384]{0:T(512)S(1)} %broadcast_multiply_fusion.11) | copy-start | bytes 4612
  134.5 7.7 copy-start.48
  142.2 8.4 copy-start.8
  142.2 8.4 copy-start.45
  146.6 4.0 copy-start.2
  150.6 2.3 copy-start.50
  152.0 167.9 %reduce-scatter.20.cloned.1.call-start = ((), (), s32[]{:S(2)}) async-start(), calls=%async_computation.13 | async-start | bytes 2654208 | tf_op jit(solution)/shard_map/reduce_scatter | solution.py:164
  193.3 2.4 copy-start.67
  202.4 2.9 copy-start.54
  225.9 3.2 copy-start.57
  225.9 3.2 copy-start.62
  291.5 66.3 %all-gather.12.cloned.1.call-start = ((), (), s32[]{:S(2)}) async-start(), calls=%async_computation.14 | async-start | bytes 2654208 | tf_op jit(solution)/shard_map/all_gather | solution.py:173
  322.2 6.0 copy-start.3
  324.0 141.3 %copy-start.40 = (f32[384]{0:T(512)}, f32[384]{0:T(512)S(1)}, u32[]{:S(2)}) copy-start(f32[384]{0:T(512)S(1)} %add_rsqrt_fusion.2) | copy-start | bytes 4612
  328.3 61.1 %all-gather.14.cloned.1.call-start = ((), (), s32[]{:S(2)}) async-start(), calls=%async_computation.16 | async-start | bytes 2654208 | tf_op jit(solution)/shard_map/all_gather | solution.py:188
  328.8 105.9 %reduce-scatter.24.cloned.1.call-start = ((), (), s32[]{:S(2)}) async-start(), calls=%async_computation.17 | async-start | bytes 2654208 | tf_op jit(solution)/shard_map/reduce_scatter | solution.py:202
  357.8 8.0 copy-start.64
  357.8 8.0 copy-start.69
  389.3 8.9 copy-start.65
  398.2 3.3 copy-start.74
  398.2 3.3 copy-start.75
  398.2 3.7 copy-start.66
  406.4 58.9 %reduce-scatter.22.cloned.1.call-start = ((), (), s32[]{:S(2)}) async-start(), calls=%async_computation.15 | async-start | bytes 2654208 | tf_op jit(solution)/shard_map/reduce_scatter | solution.py:178
  412.6 22.2 %copy-start.4 = (f32[384,1152]{1,0:T(8,128)S(1)}, f32[384,1152]{1,0:T(8,128)}, u32[]{:S(2)}) copy-start(f32[384,1152]{1,0:T(8,128)} %copy-done.3) | copy-start | bytes 5308420
  412.6 52.7 %copy-start.13 = (bf16[384,1152]{1,0:T(8,128)(2,1)S(1)}, bf16[384,1152]{1,0:T(8,128)(2,1)}, u32[]{:S(2)}) copy-start(bf16[384,1152]{1,0:T(8,128)(2,1)} %param.31) | copy-start | bytes 2654212
  412.6 86.8 %all-gather.16.cloned.1.call-start = ((), (), s32[]{:S(2)}) async-start(), calls=%async_computation.18 | async-start | bytes 2654208 | tf_op jit(solution)/shard_map/all_gather | solution.py:215
  434.8 30.5 %copy-start.10 = (bf16[384,1152]{1,0:T(8,128)(2,1)S(1)}, bf16[384,1152]{1,0:T(8,128)(2,1)}, u32[]{:S(2)}) copy-start(bf16[384,1152]{1,0:T(8,128)(2,1)} %reduce-scatter.24.cloned.1.call-done) | copy-start | bytes 2654212
  469.9 327.1 %reduce-scatter.26.cloned.1.call-start = ((), (), s32[]{:S(2)}) async-start(), calls=%async_computation.19 | async-start | bytes 2654208 | tf_op jit(solution)/shard_map/reduce_scatter | solution.py:286
  470.0 34.6 %copy-start.58 = (s32[768]{0:T(1024)S(1)}, s32[768]{0:T(1024)}, u32[]{:S(2)}) copy-start(s32[768]{0:T(1024)} %get-tuple-element.569) | copy-start | bytes 9220
  470.0 34.6 %copy-start.63 = (pred[768]{0:T(1024)(128)(4,1)S(1)}, pred[768]{0:T(1024)(128)(4,1)}, u32[]{:S(2)}) copy-start(pred[768]{0:T(1024)(128)(4,1)} %get-tuple-element.570) | copy-start | bytes 2308
  710.4 2.0 copy-start.18
  710.5 2.4 copy-start.6
  710.5 3.0 copy-start.7
  713.5 3.9 copy-start.38
  718.4 4.7 copy-start.19
  719.9 3.2 copy-start.25
  723.1 1.8 copy-start.27
  723.1 1.8 copy-start.73
  727.9 158.2 %reduce-scatter.40.cloned.1.call-start = ((), (), s32[]{:S(2)}) async-start(), calls=%async_computation.26 | async-start | bytes 3133440
  733.7 2.0 copy-start.68
  733.7 162.5 %reduce-scatter.38.cloned.1.call-start = ((), (), s32[]{:S(2)}) async-start(), calls=%async_computation.25 | async-start | bytes 3133440
  739.0 225.9 %reduce-scatter.34.cloned.1.call-start = ((), (), s32[]{:S(2)}) async-start(), calls=%async_computation.23 | async-start | bytes 3133440
  743.3 290.4 %reduce-scatter.36.cloned.1.call-start = ((), (), s32[]{:S(2)}) async-start(), calls=%async_computation.24 | async-start | bytes 3133440
  747.7 379.6 %reduce-scatter.32.cloned.1.call-start = ((), (), s32[]{:S(2)}) async-start(), calls=%async_computation.22 | async-start | bytes 7520256 | tf_op jit(solution)/shard_map/reduce_scatter | solution.py:332
  756.6 465.2 %reduce-scatter.30.cloned.1.call-start = ((), (), s32[]{:S(2)}) async-start(), calls=%async_computation.21 | async-start | bytes 7520256 | tf_op jit(solution)/shard_map/reduce_scatter | solution.py:331
  765.5 550.3 %reduce-scatter.28.cloned.1.call-start = ((), (), s32[]{:S(2)}) async-start(), calls=%async_computation.20 | async-start | bytes 7520256 | tf_op jit(solution)/shard_map/reduce_scatter | solution.py:330
  773.2 25.2 %copy-start.9 = (bf16[384,1152]{1,0:T(8,128)(2,1)S(1)}, bf16[384,1152]{1,0:T(8,128)(2,1)}, u32[]{:S(2)}) copy-start(bf16[384,1152]{1,0:T(8,128)(2,1)} %param.18) | copy-start | bytes 2654212
  773.2 25.2 %copy-start.43 = (f32[384]{0:T(512)S(1)}, f32[384]{0:T(512)}, u32[]{:S(2)}) copy-start(f32[384]{0:T(512)} %copy-done.42) | copy-start | bytes 4612
  773.2 25.2 %copy-start.46 = (f32[384]{0:T(512)S(1)}, f32[384]{0:T(512)}, u32[]{:S(2)}) copy-start(f32[384]{0:T(512)} %add_rsqrt_fusion.3) | copy-start | bytes 4612
  798.4 2.4 copy-start.16
  798.4 2.4 copy-start.22
  798.4 2.5 copy-start.44
  798.4 2.5 copy-start.47
  800.9 3.4 copy-start.11
  807.9 3.6 copy-start.60
  807.9 3.6 copy-start.61
  873.0 2.5 copy-start.34
  875.6 440.2 %copy-start.1 = (bf16[1536,1152]{1,0:T(8,128)(2,1)S(1)}, bf16[1536,1152]{1,0:T(8,128)(2,1)}, u32[]{:S(2)}) copy-start(bf16[1536,1152]{1,0:T(8,128)(2,1)} %param.30) | copy-start | bytes 10616836
  (28 other events, 33.4 us)
Sparse Core Ops, SparseCore 0:
  10.2 124.2 all-gather.7
  152.1 27.5 all-gather.9
  291.6 28.2 reduce-scatter.19
  328.4 29.3 all-gather.11
  359.9 29.4 all-gather.13
  406.5 28.2 reduce-scatter.23
  437.0 28.2 reduce-scatter.21
  470.0 29.4 all-gather.15
  728.0 28.2 reduce-scatter.25
  760.6 66.3 reduce-scatter.39
  831.5 64.6 reduce-scatter.37
  900.5 64.2 reduce-scatter.33
  969.4 64.2 reduce-scatter.35
  1038.1 89.0 reduce-scatter.31
  1132.2 89.5 reduce-scatter.29
  1226.2 89.5 reduce-scatter.27
where the time goes:
time: 1340 us; the launch traced here: 1320 us
  waiting for transfers between devices  729 us (54%)
  matrix products  239 us (18%)
  local copies, waits for them, and re-layouts  165 us (12%)
  blocking collectives  82.7 us (6%)
  other arithmetic  64 us (5%)
  loops' own time  26.5 us (2%)
  between operations  15.2 us (1%)
    unnamed x20, waiting for transfers between devices  149 us
    all_gather x1, waiting for transfers between devices, shards(): mod_full = lax.all_gather(mod_weight, 'dp', axis=0, tiled=True)  120 us
    dynamic_update_slice x40, local copies, waits for them, and re-layouts, shards(): head_outs, log_sums = lax.map(head_forward, jnp.arange(head_count))  102 us
    reduce_scatter x1, waiting for transfers between devices, shards(): lax.psum_scatter(part_up, 'dp', scatter_dimension=0, tiled=True)  94.5 us
    reduce_scatter x1, waiting for transfers between devices, shards(): lax.psum_scatter(part_gate, 'dp', scatter_dimension=0, tiled=True)  94 us
    reduce_scatter x1, waiting for transfers between devices, shards(): lax.psum_scatter(part_down, 'dp', scatter_dimension=1, tiled=True)  93.5 us
    psum x1, blocking collectives, shards(): lax.psum((tensor_query_gain, tensor_key_gain), 'dp')  32 us
    unnamed x157, local copies, waits for them, and re-layouts  31.7 us
  transfers between devices with their start and end apart: 16, of which 14 were waited for; matrix products, arithmetic and copies ran while one was open for 7% of the time, Pallas kernels for 0%

commit v1 on v0

v1 whole, which is shorter than its diff:
```python
import functools

import jax
import jax.numpy as jnp
from jax import lax
from jax.experimental import pallas as pl
from jax.experimental.pallas import tpu as pltpu
from jax.sharding import PartitionSpec as P

HD = 72
QUARTER = HD // 4
LANES = 128
SPAN = 256
TILE = 256
EPSILON = 1e-06
F32 = jnp.float32
BF16 = jnp.bfloat16
HIGH = lax.Precision.HIGHEST


def silu_grad(values):
    sigma = jax.nn.sigmoid(values)
    return sigma * (1.0 + values * (1.0 - sigma))


def dot(left, right):
    return jnp.dot(left, right, preferred_element_type=F32)


def dot_t(left, right):
    return lax.dot_general(left, right, (((1,), (1,)), ((), ())), preferred_element_type=F32)


def t_dot(left, right):
    return lax.dot_general(left, right, (((0,), (0,)), ((), ())), preferred_element_type=F32)


def geometry(row_grids, length):
    heights = row_grids[:, 0]
    widths = row_grids[:, 1]
    count = row_grids.shape[0]
    sizes = heights * widths
    ends = [sizes[0]]
    for item in range(1, count):
        ends.append(ends[-1] + sizes[item])
    starts = [ends[item] - sizes[item] for item in range(count)]
    positions = jnp.arange(length, dtype=jnp.int32)
    member = jnp.stack(
        [(positions >= starts[item]) & (positions < ends[item]) for item in range(count)], axis=1
    )
    origin = sum(jnp.where(member[:, item], starts[item], 0) for item in range(count))
    width = jnp.maximum(
        sum(jnp.where(member[:, item], widths[item], 0) for item in range(count)), 1
    )
    local = positions - origin
    spans = jnp.stack([jnp.stack(starts), sizes])
    return member.astype(F32), local // width, local % width, spans


def rope_tables(row_pos, col_pos):
    lane = jnp.arange(LANES)
    frequency = 10000.0 ** (-(lane % QUARTER).astype(F32) / QUARTER)
    along = jnp.where(lane[None, :] < 2 * QUARTER, row_pos[:, None], col_pos[:, None])
    angles = along.astype(F32) * frequency[None, :]
    valid = lane[None, :] < HD
    return jnp.where(valid, jnp.cos(angles), 0.0), jnp.where(valid, jnp.sin(angles), 0.0)


def turn(values):
    lane = lax.broadcasted_iota(jnp.int32, values.shape, 1)
    return jnp.where(
        lane % (2 * QUARTER) < QUARTER,
        -pltpu.roll(values, LANES - QUARTER, 1),
        pltpu.roll(values, QUARTER, 1),
    )


def only_head(values):
    lane = lax.broadcasted_iota(jnp.int32, values.shape, 1)
    return jnp.where(lane < HD, values, jnp.zeros_like(values))


def split_heads(wide, store, heads):
    rows = wide.shape[0]
    wide = jnp.concatenate([wide, jnp.zeros((rows, LANES), wide.dtype)], axis=1)
    for head in range(heads):
        store(head, only_head(wide[:, head * HD : head * HD + LANES]))


def attend_kernel(
    heads,
    items,
    spans,
    x_ref,
    wq_ref,
    wk_ref,
    wv_ref,
    gq_ref,
    gk_ref,
    cos_ref,
    sin_ref,
    out_ref,
    qpre_ref,
    kpre_ref,
    q_ref,
    k_ref,
    v_ref,
    probs_ref,
    qraw,
    kraw,
    vraw,
    oraw,
    wide,
):
    length = x_ref.shape[0]
    head = pl.program_id(0)

    @pl.when(head == 0)
    def _():
        for first in range(0, length, TILE):
            rows = pl.ds(first, TILE)
            x = x_ref[rows, :]
            for w_ref, raw in ((wq_ref, qraw), (wk_ref, kraw), (wv_ref, vraw)):

                def store(h, part, raw=raw):
                    raw[h, rows, :] = part.astype(raw.dtype)

                split_heads(dot(x, w_ref[...]), store, heads)

    for raw, pre_ref, low_ref, gain_ref in (
        (qraw, qpre_ref, q_ref, gq_ref),
        (kraw, kpre_ref, k_ref, gk_ref),
    ):
        for first in range(0, length, TILE):
            rows = pl.ds(first, TILE)
            pre = raw[head, rows, :]
            pre_ref[0, rows, :] = pre
            inv = lax.rsqrt(jnp.sum(pre * pre, axis=1, keepdims=True) / HD + EPSILON)
            normed = pre * inv * gain_ref[...]
            low_ref[0, rows, :] = (
                normed * cos_ref[rows, :] + turn(normed) * sin_ref[rows, :]
            ).astype(BF16)
    v_ref[0] = vraw[head]
    oraw[head] = vraw[head].astype(F32)
    row = lax.broadcasted_iota(jnp.int32, (SPAN, SPAN), 0)
    col = lax.broadcasted_iota(jnp.int32, (SPAN, SPAN), 1)
    row_out = lax.broadcasted_iota(jnp.int32, (SPAN, LANES), 0)
    for item in range(items):
        start = pl.multiple_of(spans[0, item], 16)
        size = spans[1, item]
        rows = pl.ds(start, SPAN)
        scores = dot_t(q_ref[0, rows, :], k_ref[0, rows, :]) * HD**-0.5
        scores = jnp.where(col < size, scores, -1e30)
        top = jnp.max(scores, axis=1, keepdims=True)
        weights = jnp.exp(scores - top)
        total = jnp.sum(weights, axis=1, keepdims=True)
        probs = jnp.where(row < size, weights / total, 0.0).astype(BF16)
        probs_ref[0, item] = probs
        mixed = dot(probs, v_ref[0, rows, :])
        oraw[head, rows, :] = jnp.where(row_out < size, mixed, oraw[head, rows, :])

    @pl.when(head == heads - 1)
    def _():
        for h in range(heads):
            wide[:, h * HD : h * HD + HD] = oraw[h][:, :HD]
        out_ref[...] = wide[...].astype(BF16)


def attend_back_kernel(
    heads,
    items,
    spans,
    grad_ref,
    qpre_ref,
    kpre_ref,
    q_ref,
    k_ref,
    v_ref,
    probs_ref,
    gq_ref,
    gk_ref,
    cos_ref,
    sin_ref,
    dq_ref,
    dk_ref,
    dv_ref,
    gain_ref,
    graw,
    dqraw,
    dkraw,
    dvraw,
    wide,
):
    length = grad_ref.shape[0]
    head = pl.program_id(0)

    @pl.when(head == 0)
    def _():
        gain_ref[...] = jnp.zeros_like(gain_ref)
        for first in range(0, length, TILE):
            rows = pl.ds(first, TILE)

            def store(h, part):
                graw[h, rows, :] = part.astype(BF16)

            split_heads(grad_ref[rows, :].astype(F32), store, heads)

    dqraw[head] = jnp.zeros((length, LANES), F32)
    dkraw[head] = jnp.zeros((length, LANES), F32)
    row_all = lax.broadcasted_iota(jnp.int32, (length, LANES), 0)
    used = spans[0, items - 1] + spans[1, items - 1]
    dvraw[head] = jnp.where(row_all >= used, graw[head].astype(F32), 0.0)
    for item in range(items):
        start = pl.multiple_of(spans[0, item], 16)
        rows = pl.ds(start, SPAN)
        probs_low = probs_ref[0, item]
        probs = probs_low.astype(F32)
        grad = graw[head, rows, :]
        grad_probs = dot_t(grad, v_ref[0, rows, :])
        inner = jnp.sum(probs * grad_probs, axis=1, keepdims=True) / jnp.maximum(
            jnp.sum(probs, axis=1, keepdims=True), 0.5
        )
        grad_scores = (probs * (grad_probs - inner)).astype(BF16)
        dqraw[head, rows, :] += dot(grad_scores, k_ref[0, rows, :])
        dkraw[head, rows, :] += t_dot(grad_scores, q_ref[0, rows, :])
        dvraw[head, rows, :] += t_dot(probs_low, grad)

    for raw, pre_ref, g_ref, which in (
        (dqraw, qpre_ref, gq_ref, 0),
        (dkraw, kpre_ref, gk_ref, 1),
    ):
        for first in range(0, length, TILE):
            rows = pl.ds(first, TILE)
            turned = raw[head, rows, :] * HD**-0.5
            normed = turned * cos_ref[rows, :] - turn(turned * sin_ref[rows, :])
            pre = pre_ref[0, rows, :]
            inv = lax.rsqrt(jnp.sum(pre * pre, axis=1, keepdims=True) / HD + EPSILON)
            unit = pre * inv
            gain_ref[which : which + 1, :] += jnp.sum(normed * unit, axis=0, keepdims=True)
            scaled = normed * g_ref[...]
            along = jnp.sum(scaled * unit, axis=1, keepdims=True) / HD
            raw[head, rows, :] = inv * (scaled - unit * along)

    @pl.when(head == heads - 1)
    def _():
        for raw, o_ref in ((dqraw, dq_ref), (dkraw, dk_ref), (dvraw, dv_ref)):
            for h in range(heads):
                wide[:, h * HD : h * HD + HD] = raw[h][:, :HD]
            o_ref[...] = wide[...].astype(BF16)


def whole(shape):
    return pl.BlockSpec(shape, lambda h, spans: (0,) * len(shape))


def per_head(shape):
    return pl.BlockSpec((1,) + shape, lambda h, spans: (h,) + (0,) * len(shape))


def attend(spans, x, wq, wk, wv, gain_q, gain_k, cosine, sine):
    length, width = x.shape
    heads = wq.shape[1] // HD
    items = spans.shape[1]
    head_f32 = jax.ShapeDtypeStruct((heads, length, LANES), F32)
    head_low = jax.ShapeDtypeStruct((heads, length, LANES), BF16)
    return pl.pallas_call(
        functools.partial(attend_kernel, heads, items),
        grid_spec=pltpu.PrefetchScalarGridSpec(
            num_scalar_prefetch=1,
            grid=(heads,),
            in_specs=[
                whole(x.shape),
                whole(wq.shape),
                whole(wk.shape),
                whole(wv.shape),
                whole((1, LANES)),
                whole((1, LANES)),
                whole((length, LANES)),
                whole((length, LANES)),
            ],
            out_specs=[
                whole((length, heads * HD)),
                per_head((length, LANES)),
                per_head((length, LANES)),
                per_head((length, LANES)),
                per_head((length, LANES)),
                per_head((length, LANES)),
                per_head((items, SPAN, SPAN)),
            ],
            scratch_shapes=[
                pltpu.VMEM((heads, length, LANES), F32),
                pltpu.VMEM((heads, length, LANES), F32),
                pltpu.VMEM((heads, length, LANES), BF16),
                pltpu.VMEM((heads, length, LANES), F32),
                pltpu.VMEM((length, heads * HD), F32),
            ],
        ),
        out_shape=[
            jax.ShapeDtypeStruct((length, heads * HD), BF16),
            head_f32,
            head_f32,
            head_low,
            head_low,
            head_low,
            jax.ShapeDtypeStruct((heads, items, SPAN, SPAN), BF16),
        ],
        compiler_params=pltpu.CompilerParams(vmem_limit_bytes=56 * 2**20),
        cost_estimate=pl.CostEstimate(
            flops=2 * length * width * heads * HD * 3 + 4 * heads * items * SPAN * SPAN * LANES,
            bytes_accessed=24 * 2**20,
            transcendentals=heads * items * SPAN * SPAN,
        ),
        name="attend",
    )(spans, x, wq, wk, wv, gain_q, gain_k, cosine, sine)


def attend_back(spans, grad, saved, gain_q, gain_k, cosine, sine):
    length, width = grad.shape
    heads = width // HD
    items = spans.shape[1]
    out = jax.ShapeDtypeStruct((length, width), BF16)
    return pl.pallas_call(
        functools.partial(attend_back_kernel, heads, items),
        grid_spec=pltpu.PrefetchScalarGridSpec(
            num_scalar_prefetch=1,
            grid=(heads,),
            in_specs=[
                whole(grad.shape),
                per_head((length, LANES)),
                per_head((length, LANES)),
                per_head((length, LANES)),
                per_head((length, LANES)),
                per_head((length, LANES)),
                per_head((items, SPAN, SPAN)),
                whole((1, LANES)),
                whole((1, LANES)),
                whole((length, LANES)),
                whole((length, LANES)),
            ],
            out_specs=[
                whole((length, width)),
                whole((length, width)),
                whole((length, width)),
                whole((8, LANES)),
            ],
            scratch_shapes=[
                pltpu.VMEM((heads, length, LANES), BF16),
                pltpu.VMEM((heads, length, LANES), F32),
                pltpu.VMEM((heads, length, LANES), F32),
                pltpu.VMEM((heads, length, LANES), F32),
                pltpu.VMEM((length, width), F32),
            ],
        ),
        out_shape=[out, out, out, jax.ShapeDtypeStruct((8, LANES), F32)],
        compiler_params=pltpu.CompilerParams(vmem_limit_bytes=56 * 2**20),
        cost_estimate=pl.CostEstimate(
            flops=8 * heads * items * SPAN * SPAN * LANES,
            bytes_accessed=24 * 2**20,
            transcendentals=0,
        ),
        name="attend_back",
    )(spans, grad, *saved, gain_q, gain_k, cosine, sine)


def layer_norm(values):
    centred = values - jnp.mean(values, axis=1, keepdims=True)
    inv_std = lax.rsqrt(jnp.mean(centred * centred, axis=1, keepdims=True) + EPSILON)
    return (centred * inv_std, inv_std)


def norm_back(grad_norm, normed, inv_std):
    return inv_std * (
        grad_norm
        - jnp.mean(grad_norm, axis=1, keepdims=True)
        - normed * jnp.mean(grad_norm * normed, axis=1, keepdims=True)
    )


def per_token(member, rows):
    return sum(member[:, item, None] * rows[item][None, :] for item in range(rows.shape[0]))


def per_item(member, values):
    return jnp.stack(
        [jnp.sum(member[:, item, None] * values, axis=0) for item in range(member.shape[1])]
    )


def swap(values):
    return lax.ppermute(values, "tensor", [(0, 1), (1, 0)])


def in_order(own, other, second):
    return jnp.concatenate([jnp.where(second, other, own), jnp.where(second, own, other)])


def halving_rows(values, bits):
    dp = 2**bits
    depth = values.shape[1] // dp
    blocks = values.T.reshape((2,) * bits + (depth, values.shape[0]))
    me = lax.axis_index("dp")
    for bit in range(bits):
        axis = bits - 1 - bit
        blocks = jnp.where((me >> bit) & 1 == 1, jnp.flip(blocks, axis), blocks)
    blocks = blocks.transpose(tuple(range(bits - 1, -1, -1)) + (bits, bits + 1))
    return blocks.reshape(dp * depth, values.shape[0])


def first_halving(rows, grads):
    half = rows.shape[0] // 2
    sent = lax.ppermute(dot(rows[half:], grads).astype(BF16), "dp", partners(0))
    return (dot(rows[:half], grads) + sent.astype(F32)).astype(BF16)


def partners(bit):
    return [(i, i ^ (1 << bit)) for i in range(lax.axis_size("dp"))]


def rest_of_halving(part, bits):
    for bit in range(1, bits):
        half = part.shape[0] // 2
        sent = lax.ppermute(part[half:], "dp", partners(bit))
        part = part[:half].astype(F32) + sent.astype(F32)
        if bit < bits - 1:
            part = part.astype(BF16)
    return part.astype(F32)


def shards(
    tokens,
    conditions,
    item_grids,
    mod_weight,
    query_weight,
    key_weight,
    value_weight,
    proj_weight,
    query_gain,
    key_gain,
    gate_weight,
    up_weight,
    down_weight,
    out_grad,
):
    half, width = tokens.shape
    length = 2 * half
    dp = lax.axis_size("dp")
    bits = dp.bit_length() - 1
    me = lax.axis_index("dp")
    second = lax.axis_index("tensor") == 1
    own_first = lax.axis_index("tensor") * half
    other_first = half - own_first
    items = conditions.shape[0]
    owned = mod_weight.shape[0]

    tokens_other = swap(tokens)
    out_grad_other = swap(out_grad)

    member, row_pos, col_pos, spans = geometry(item_grids, length)
    cosine, sine = rope_tables(row_pos, col_pos)
    gain_q = jnp.pad(query_gain, (0, LANES - HD))[None, :]
    gain_k = jnp.pad(key_gain, (0, LANES - HD))[None, :]
    member_own = lax.dynamic_slice_in_dim(member, own_first, half, 0)
    member_other = lax.dynamic_slice_in_dim(member, other_first, half, 0)

    cond_all = lax.all_gather(conditions, "dp", axis=0, tiled=True)
    mod_in_all = jax.nn.silu(cond_all.astype(F32)).astype(BF16)
    mod_in_own = lax.dynamic_slice_in_dim(mod_in_all, me * owned, owned, 1)
    mod_part = dot(mod_in_own, mod_weight)
    mod_parts = lax.all_to_all(
        mod_part.reshape(dp, items, 6 * width), "dp", split_axis=0, concat_axis=0, tiled=True
    )
    modulation = jnp.sum(mod_parts.astype(F32), axis=0)
    shift_one, scale_one, gate_one, shift_two, scale_two, gate_two = jnp.split(
        modulation, 6, axis=1
    )

    tokens_float = tokens.astype(F32)
    tokens_all = in_order(tokens, tokens_other, second).astype(F32)
    norm_all, _ = layer_norm(tokens_all)
    attn_in = (
        norm_all * (1.0 + per_token(member, scale_one)) + per_token(member, shift_one)
    ).astype(BF16)

    heads_out, *saved = attend(
        spans, attn_in, query_weight, key_weight, value_weight, gain_q, gain_k, cosine, sine
    )
    heads_other = lax.dynamic_slice_in_dim(heads_out, other_first, half, 0)
    heads_own = lax.dynamic_slice_in_dim(heads_out, own_first, half, 0)
    attn_recv = swap(dot(heads_other, proj_weight).astype(BF16))
    attn_out = dot(heads_own, proj_weight) + attn_recv.astype(F32)

    gate_one_own = per_token(member_own, gate_one)
    scale_two_own = per_token(member_own, scale_two)
    resid = tokens_float + gate_one_own * attn_out
    norm_two, inv_two = layer_norm(resid)
    mlp_in = (norm_two * (1.0 + scale_two_own) + per_token(member_own, shift_two)).astype(BF16)
    mlp_in_all = jnp.concatenate([mlp_in, swap(mlp_in)])

    grad_out = out_grad.astype(F32)
    gate_two_own = per_token(member_own, gate_two)
    grad_mlp_all = jnp.concatenate(
        [
            (gate_two_own * grad_out).astype(BF16),
            (per_token(member_other, gate_two) * out_grad_other.astype(F32)).astype(BF16),
        ]
    )
    grad_hidden = dot_t(grad_mlp_all, down_weight)

    gate_pre = dot(mlp_in_all, gate_weight)
    up_pre = dot(mlp_in_all, up_weight)
    silu_gate = jax.nn.silu(gate_pre)
    hidden = (silu_gate * up_pre).astype(BF16)
    grad_gate_pre = (grad_hidden * up_pre * silu_grad(gate_pre)).astype(BF16)
    grad_up_pre = (grad_hidden * silu_gate).astype(BF16)

    back_other = dot_t(grad_gate_pre[half:], gate_weight) + dot_t(grad_up_pre[half:], up_weight)
    back_recv = swap(back_other.astype(BF16))
    mlp_recv = swap(dot(hidden[half:], down_weight).astype(BF16))
    grad_mlp_in = (
        dot_t(grad_gate_pre[:half], gate_weight)
        + dot_t(grad_up_pre[:half], up_weight)
        + back_recv.astype(F32)
    )

    grad_mlp_rows = halving_rows(grad_mlp_all, bits)
    mlp_in_rows = halving_rows(mlp_in_all, bits)
    down_part = first_halving(grad_mlp_rows, hidden)
    gate_part = first_halving(mlp_in_rows, grad_gate_pre)
    up_part = first_halving(mlp_in_rows, grad_up_pre)

    mlp_out = dot(hidden[:half], down_weight) + mlp_recv.astype(F32)
    block_out = (resid + gate_two_own * mlp_out).astype(BF16)

    grad_resid = grad_out + norm_back(grad_mlp_in * (1.0 + scale_two_own), norm_two, inv_two)
    grad_attn = (gate_one_own * grad_resid).astype(BF16)
    grad_attn_all = in_order(grad_attn, swap(grad_attn), second)
    grad_heads = dot_t(grad_attn_all, proj_weight).astype(BF16)
    dq, dk, dv, gain_parts = attend_back(spans, grad_heads, saved, gain_q, gain_k, cosine, sine)

    def attn_back(first):
        def rows(array):
            return lax.dynamic_slice_in_dim(array, first, half, 0)

        return (
            dot_t(rows(dq), query_weight)
            + dot_t(rows(dk), key_weight)
            + dot_t(rows(dv), value_weight)
        )

    attn_back_recv = swap(attn_back(other_first).astype(BF16))
    grad_attn_in = attn_back(own_first) + attn_back_recv.astype(F32)
    attn_in_rows = halving_rows(attn_in, bits)
    grad_attn_rows = halving_rows(grad_attn_all, bits)
    attn_parts = jnp.concatenate(
        [
            first_halving(attn_in_rows, dq),
            first_halving(attn_in_rows, dk),
            first_halving(attn_in_rows, dv),
            first_halving(grad_attn_rows, heads_out),
        ],
        axis=1,
    )

    norm_one, inv_one = layer_norm(tokens_float)
    scale_one_own = per_token(member_own, scale_one)
    grad_tokens = (
        grad_resid + norm_back(grad_attn_in * (1.0 + scale_one_own), norm_one, inv_one)
    ).astype(BF16)

    part_mod = jnp.concatenate(
        [
            per_item(member_own, grad_attn_in),
            per_item(member_own, grad_attn_in * norm_one),
            per_item(member_own, grad_resid * attn_out),
            per_item(member_own, grad_mlp_in),
            per_item(member_own, grad_mlp_in * norm_two),
            per_item(member_own, grad_out * mlp_out),
        ],
        axis=1,
    )
    gains = jnp.pad(gain_parts[:2].reshape(1, 2 * LANES), ((0, 0), (0, 6 * width - 2 * LANES)))
    part_small = jnp.concatenate([part_mod, gains]).astype(BF16)
    small = part_small.astype(F32) + swap(part_small).astype(F32)
    small_all = lax.all_gather(small.astype(BF16), "dp", axis=0, tiled=False)
    grad_mod_all = small_all[:, :items].reshape(dp * items, 6 * width)
    grad_gains = jnp.sum(small_all[:, items, : 2 * LANES].astype(F32), axis=0)
    grad_mod_weight = t_dot(mod_in_own, grad_mod_all)
    cond_part = dot_t(grad_mod_all, mod_weight)
    cond_parts = lax.all_to_all(
        cond_part.reshape(dp, items, owned), "dp", split_axis=0, concat_axis=0, tiled=True
    )
    grad_mod_in = cond_parts.transpose(1, 0, 2).reshape(items, dp * owned)
    grad_conditions = silu_grad(conditions.astype(F32)) * grad_mod_in

    grad_down = rest_of_halving(down_part, bits).T
    grad_gate = rest_of_halving(gate_part, bits)
    grad_up = rest_of_halving(up_part, bits)
    attn_sum = rest_of_halving(attn_parts, bits)
    grad_q, grad_k, grad_v, grad_proj = jnp.split(attn_sum, 4, axis=1)
    return (
        block_out,
        grad_tokens,
        grad_conditions,
        grad_mod_weight,
        grad_q,
        grad_k,
        grad_v,
        grad_proj.T,
        grad_gains[:HD],
        grad_gains[LANES : LANES + HD],
        grad_gate,
        grad_up,
        grad_down,
    )


def solution(mesh):
    tokens = P(("dp", "tensor"), None)
    rows = P("dp", None)
    columns = P(None, "tensor")
    inner = P("tensor", None)
    both = P("dp", "tensor")
    turned = P("tensor", "dp")
    return jax.shard_map(
        shards,
        mesh=mesh,
        in_specs=(
            tokens,
            rows,
            rows,
            rows,
            columns,
            columns,
            columns,
            inner,
            P(),
            P(),
            columns,
            columns,
            inner,
            tokens,
        ),
        out_specs=(
            tokens,
            tokens,
            rows,
            rows,
            both,
            both,
            both,
            turned,
            P(),
            P(),
            both,
            both,
            turned,
        ),
        check_vma=False,
    )
```

time: 1340 us -> 525 us (0.39)
  waiting for transfers between devices: 729 us -> 110 us
  matrix products: 239 us -> 96 us
  local copies, waits for them, and re-layouts: 165 us -> 69.8 us
  Pallas kernels: 0 us -> 51 us
  starting transfers between devices: 1.66 us -> 44.7 us
  loops' own time: 26.5 us -> 0 us
  blocking collectives: 82.7 us -> 63.3 us
    reduce_scatter x7 -> x0, waiting for transfers between devices: 360 us -> none  [the longest x1 94.5 us: shards(): lax.psum_scatter(part_up, 'dp', scatter_dimension=0, tiled=True)]
    all_gather x5 -> x0, waiting for transfers between devices: 220 us -> none  [the longest x1 120 us: shards(): mod_full = lax.all_gather(mod_weight, 'dp', axis=0, tiled=True)]
    unnamed x20 -> x0, waiting for transfers between devices: 149 us -> none
    dot_general x82 -> x35, matrix products: 239 us -> 96 us  [the longest x21 57.7 us: dot(): return jnp.dot(left, right, preferred_element_type=F32)]
    ppermute x0 -> x28, waiting for transfers between devices: none -> 104 us  [the longest x12 59.8 us: rest_of_halving(): sent = lax.ppermute(part[half:], 'dp', partners(bit))]
    dynamic_update_slice x40 -> x0, local copies, waits for them, and re-layouts: 102 us -> none  [shards(): head_outs, log_sums = lax.map(head_forward, jnp.arange(head_count))]
    pallas_call x0 -> x2, Pallas kernels: none -> 51 us  [the longest x1 25.7 us: attend_back(): pl.pallas_call(functools.partial(attend_back_kernel, heads, items), grid_...]
    psum x2 -> x0, blocking collectives: 39.4 us -> none  [the longest x1 32 us: shards(): lax.psum((tensor_query_gain, tensor_key_gain), 'dp')]
  transfers between devices with their start and end apart: 16 -> 30, of which waited for: 14 -> 13; matrix products, arithmetic and copies ran while one was open for 7% -> 35% of each run, Pallas kernels for 0% -> 10%
where the time goes in v1:
time: 525 us; the launch traced here: 516 us
  waiting for transfers between devices  110 us (21%)
  matrix products  96 us (18%)
  other arithmetic  76.3 us (15%)
  local copies, waits for them, and re-layouts  69.8 us (13%)
  blocking collectives  63.3 us (12%)
  Pallas kernels  51 us (10%)
  starting transfers between devices  44.7 us (9%)
    ppermute x12, waiting for transfers between devices, rest_of_halving(): sent = lax.ppermute(part[half:], 'dp', partners(bit))  59.8 us
    dot_general x21, matrix products, dot(): return jnp.dot(left, right, preferred_element_type=F32)  57.7 us
    ppermute x9, waiting for transfers between devices, swap(): return lax.ppermute(values, 'tensor', [(0, 1), (1, 0)])  43.9 us
    all_gather x1, blocking collectives, shards(): small_all = lax.all_gather(small.astype(BF16), 'dp', axis=0, tiled=False)  38.1 us
    dot_general x13, matrix products, dot_t(): lax.dot_general(left, right, (((1,), (1,)), ((), ())), preferred_element_...  35.7 us
    pallas_call x1, Pallas kernels, attend_back(): pl.pallas_call(functools.partial(attend_back_kernel, heads, items), grid_...  25.7 us
    pallas_call x1, Pallas kernels, attend(): pl.pallas_call(functools.partial(attend_kernel, heads, items), grid_spec=...  25.3 us
    all_gather x1, blocking collectives, shards(): cond_all = lax.all_gather(conditions, 'dp', axis=0, tiled=True)  25.2 us
  transfers between devices with their start and end apart: 30, of which 13 were waited for; matrix products, arithmetic and copies ran while one was open for 35% of the time, Pallas kernels for 10%

profile of v1, /device:TPU:0, one launch (start us, length us, event | category | flops | bytes accessed | tf_op | source)
XLA Modules:
  0.0 516.0 jit_solution(2268941481808775129)
XLA Ops:
  0.7 25.2 %all-gather.1 = bf16[16,3,1152]{2,1,0:T(4,128)(2,1)} all-gather(bf16[1,3,1152]{2,1,0:T(4,128)(2,1)} %bitcast.131), channel_id=1, replica_groups=mesh['dp'=16,'tensor'=2] {'dp'}, dimensions={0}, use_global_device_ids=true | all-gather | bytes 117504 | tf_op jit(solution)/shard_map/all_gather | solution.py:466
  27.6 2.7 fusion.93
  30.3 2.6 reshape.251
  32.9 4.6 all-to-all-start
  48.7 2.6 copy.88.wq_ref
  51.3 2.6 copy.89.wk_ref
  53.9 2.6 copy.90.wv_ref
  57.2 2.7 add_select_fusion
  62.5 3.4 sine_select_fusion
  69.6 3.2 all-to-all-done
  72.8 2.4 reduce_sum.270
  77.1 10.3 %fusion.6.x_ref = bf16[768,1152]{1,0:T(8,128)(2,1)} fusion(f32[1152]{0:T(1024)S(1)} %get-tuple-element.66, f32[1152]{0:T(1024)S(1)} %get-tuple-element.67, f32[1152]{0:T(1024)S(1)} %get-tuple-element.68, f32[1152]{0:T(1024)S(1)} %get-tuple-element.69, f32[768]{0:T(1024)} %get-tuple-element.82, f32[1152]{0:T(1024)S(1)} %get-tuple-element.70, ...), kind=kLoop, calls=%fused_computation.12 | loop fusion | flops 17694720 | bytes 3581952 | tf_op jit(solution)/shard_map/convert_element_type | solution.py:483
  87.5 25.3 %attend.1 = (bf16[768,576]{1,0:T(8,128)(2,1)}, f32[8,768,128]{2,1,0:T(8,128)}, f32[8,768,128]{2,1,0:T(8,128)}, bf16[8,768,128]{2,1,0:T(8,128)(2,1)}, bf16[8,768,...) custom-call(s32[2,3]{1,0:T(2,128)} %pad_add_fusion.spans, ...), custom_call_target="tpu_custom_call" | custom-call | flops 3862953984 | bytes 25165824 | tf_op jit(solution)/shard_map/attend/pallas_call | solution.py:266
  112.8 2.9 convolution_convert_fusion.4
  117.1 4.2 copy.96
  121.4 2.4 reverse_select_fusion.15
  127.1 11.2 %collective-permute-done.1 = bf16[384,1152]{1,0:T(8,128)(2,1)} collective-permute-done((bf16[384,1152]{1,0:T(8,128)(2,1)}, bf16[384,1152]{1,0:T(8,128)(2,1)}, u32[]{:S(2)}, u32[]{:S(2)}) %collective-permute-start.1) | collective-permute-done | bytes 884768 | tf_op jit(solution)/shard_map/ppermute | solution.py:390
  138.4 5.3 %fusion.97 = (f32[384]{0:T(512)S(1)}, f32[384,1152]{1,0:T(8,128)S(1)}, f32[384]{0:T(512)}, bf16[384,1152]{1,0:T(8,128)(2,1)S(1)}, bf16[384,1152]{1,0:T(8,128)(2,1)S(1)}, /*index=5*/f32[384,1152]{1,0:T(8,128)}) fusion(bf16[384,1152]{1,0:T(8,128)(2,1)} %collective-permute-done.1, f32[1152]{0:T(1024)S(1)} %copy-done.75, f32[384]{0:T(512)S(1)} %copy-done.67, ...), kind=kOutput, calls=%fused_computation.276 | convolution fusion | flops 522878208 | bytes 10732548 | tf_op jit(solution)/shard_map/dot_general | solution.py:27
  144.7 4.8 add_convert_fusion.8
  152.4 3.8 copy.105
  156.2 2.4 reverse_select_fusion.3
  162.3 9.0 %collective-permute-done.2 = bf16[384,1152]{1,0:T(8,128)(2,1)} collective-permute-done((bf16[384,1152]{1,0:T(8,128)(2,1)}, bf16[384,1152]{1,0:T(8,128)(2,1)}, u32[]{:S(2)}, u32[]{:S(2)}) %collective-permute-start.2) | collective-permute-done | bytes 884768 | tf_op jit(solution)/shard_map/ppermute | solution.py:390
  171.3 6.3 %fusion.47 = f32[768,1536]{1,0:T(8,128)} fusion(bf16[1152,1536]{1,0:T(8,128)(2,1)S(1)} %copy-done.107, bf16[384,1152]{1,0:T(8,128)(2,1)} %collective-permute-done.2, bf16[384,1152]{1,0:T(8,128)(2,1)} %add_convert_fusion.8), kind=kOutput, calls=%fused_computation.146 | convolution fusion | flops 2721447936 | bytes 10027008 | tf_op jit(solution)/shard_map/dot_general | solution.py:27
  177.6 6.5 %fusion.46 = f32[768,1536]{1,0:T(8,128)} fusion(bf16[1152,1536]{1,0:T(8,128)(2,1)S(1)} %copy-done.109, bf16[384,1152]{1,0:T(8,128)(2,1)} %collective-permute-done.2, bf16[384,1152]{1,0:T(8,128)(2,1)} %add_convert_fusion.8), kind=kOutput, calls=%fused_computation.145 | convolution fusion | flops 2721447936 | bytes 10027008 | tf_op jit(solution)/shard_map/dot_general | solution.py:27
  184.1 8.0 %multiply_convert_fusion = (bf16[768,1536]{1,0:T(8,128)(2,1)S(1)}, bf16[768,1536]{1,0:T(8,128)(2,1)S(1)}, bf16[768,1536]{1,0:T(8,128)(2,1)S(1)}) fusion(f32[768,1536]{1,0:T(8,128)} %fusion.47, f32[768,1536]{1,0:T(8,128)} %fusion.46, bf16[1536,1152]{1,0:T(8,128)(2,1)S(1)} %copy-done, bf16[384,1152]{1,0:T(8,128)(2,1)S(1)} %copy-done.44, ...), kind=kOutput, calls=%fused_computation | convolution fusion | flops 2739142656 | bytes 21823488 | tf_op jit(solution)/shard_map/dot_general | solution.py:31
  192.1 3.1 convolution_convert_fusion.3
  198.5 2.7 fusion.7
  201.7 2.8 fusion.45
  204.5 3.8 copy.102
  208.3 2.4 reverse_select_fusion.7
  218.2 17.0 %collective-permute-done.5 = bf16[384,1152]{1,0:T(8,128)(2,1)} collective-permute-done((bf16[384,1152]{1,0:T(8,128)(2,1)}, bf16[384,1152]{1,0:T(8,128)(2,1)}, u32[]{:S(2)}, u32[]{:S(2)}) %collective-permute-start.5) | collective-permute-done | bytes 884768 | tf_op jit(solution)/shard_map/ppermute | solution.py:390
  235.3 6.8 %fusion.95 = (f32[384]{0:T(512)S(1)}, f32[384]{0:T(512)S(1)}, bf16[1152]{0:T(1024)(128)(2,1)S(1)}, bf16[1152]{0:T(1024)(128)(2,1)S(1)}, bf16[1152]{0:T(1024)(128...) fusion(f32[1152]{0:T(1024)S(1)} %copy-done.56, f32[384]{0:T(512)S(1)} %copy-done.68, ...), kind=kOutput, calls=%fused_computation.274 | convolution fusion | flops 1372663680 | bytes 14520064 | tf_op jit(solution)/shard_map/dot_general | solution.py:31
  242.2 3.1 multiply_convert_fusion.3
  246.7 2.7 convolution_convert_fusion.2
  250.5 2.7 convolution_convert_fusion.1
  253.8 2.8 convolution_convert_fusion
  258.3 6.6 %collective-permute-done.6 = bf16[384,1152]{1,0:T(8,128)(2,1)S(1)} collective-permute-done((bf16[384,1152]{1,0:T(8,128)(2,1)S(1)}, bf16[384,1152]{1,0:T(8,128)(2,1)S(1)}, u32[]{:S(2)}, u32[]{:S(2)}) %collective-permute-start.6) | collective-permute-done | bytes 884768 | tf_op jit(solution)/shard_map/ppermute | solution.py:390
  265.1 2.3 convolution_convert_fusion.5
  267.4 2.2 copy.91.grad_ref
  269.6 25.7 %attend_back.1 = (bf16[768,576]{1,0:T(8,128)(2,1)}, bf16[768,576]{1,0:T(8,128)(2,1)}, bf16[768,576]{1,0:T(8,128)(2,1)}, f32[8,128]{1,0:T(8,128)}) custom-call(s32[2,3]{1,0:T(2,128)} %pad_add_fusion.spans, bf16[768,576]{1,0:T(8,128)(2,1)} %copy.91.grad_ref, f32[8,768,128]{2,1,0:T(8,128)} %get-tuple-element.25.qpre_ref, ...), custom_call_target="tpu_custom_call" | custom-call | flops 1610612736 | bytes 25165824 | tf_op jit(solution)/shard_map/attend_back/pallas_call | solution.py:322
  310.0 2.8 copy.99
  318.3 2.2 convolution_add_fusion.3
  321.0 3.2 add_convert_fusion.2
  324.8 3.1 add_convert_fusion
  330.3 3.0 add_convert_fusion.1
  336.8 3.0 collective-permute-start.17
  348.4 5.4 %concatenate.29 = bf16[576,2304]{1,0:T(8,128)(2,1)} concatenate(bf16[576,576]{1,0:T(8,128)(2,1)S(1)} %add_convert_fusion.12, bf16[576,576]{1,0:T(8,128)(2,1)S(1)} %add_convert_fusion.11, bf16[576,576]{1,0:T(8,128)(2,1)} %add_convert_fusion.10, bf16[576,576]{1,0:T(8,128)(2,1)} %add_convert_fusion.9), dimensions={1} | concatenate | bytes 5308416 | tf_op jit(solution)/shard_map/concatenate | solution.py:555
  353.9 2.7 slice.456
  356.7 3.0 convert_add_fusion.2
  360.1 5.4 %multiply_reduce_fusion.11 = (bf16[1152]{0:T(1024)(128)(2,1)S(1)}, bf16[1152]{0:T(1024)(128)(2,1)S(1)}, bf16[1152]{0:T(1024)(128)(2,1)S(1)}, bf16[1152]{0:T(1024...) fusion(f32[384]{0:T(512)S(1)} %copy-done.66, ...), kind=kLoop, calls=%fused_computation.86 | loop fusion | flops 22542720 | bytes 12445440 | tf_op jit(solution)/shard_map/reduce_sum | solution.py:385
  368.9 4.8 collective-permute-start.18
  373.6 5.9 %collective-permute-done.21 = bf16[288,1536]{1,0:T(8,128)(2,1)} collective-permute-done((bf16[288,1536]{1,0:T(8,128)(2,1)}, bf16[288,1536]{1,0:T(8,128)(2,1)}, u32[]{:S(2)}, u32[]{:S(2)}) %collective-permute-start.21) | collective-permute-done | bytes 884768 | tf_op jit(solution)/shard_map/ppermute | solution.py:422
  381.8 4.8 collective-permute-start.22
  386.6 11.9 %collective-permute-done.25 = bf16[288,1536]{1,0:T(8,128)(2,1)} collective-permute-done((bf16[288,1536]{1,0:T(8,128)(2,1)}, bf16[288,1536]{1,0:T(8,128)(2,1)}, u32[]{:S(2)}, u32[]{:S(2)}) %collective-permute-start.25) | collective-permute-done | bytes 884768 | tf_op jit(solution)/shard_map/ppermute | solution.py:422
  401.7 4.8 collective-permute-start.26
  408.5 38.1 %all-gather.2 = bf16[16,4,6912]{2,1,0:T(4,128)(2,1)S(1)} all-gather(bf16[1,4,6912]{2,1,0:T(4,128)(2,1)S(1)} %fusion.63), channel_id=2, replica_groups=mesh['dp'=16,'tensor'=2] {'dp'}, dimensions={0}, use_global_device_ids=true | all-gather | bytes 940032 | tf_op jit(solution)/shard_map/all_gather | solution.py:585
  448.3 3.5 all-to-all-start.1
  451.9 2.6 fusion.94
  455.0 3.3 all-to-all-done.1
  463.6 2.3 collective-permute-start.23
  470.1 14.3 %collective-permute-done.19 = bf16[72,1536]{1,0:T(8,128)(2,1)S(1)} collective-permute-done((bf16[72,1536]{1,0:T(8,128)(2,1)S(1)}, bf16[72,1536]{1,0:T(8,128)(2,1)S(1)}, u32[]{:S(2)}, u32[]{:S(2)}) %collective-permute-start.19) | collective-permute-done | bytes 221216 | tf_op jit(solution)/shard_map/ppermute | solution.py:422
  485.1 3.9 collective-permute-done.23
  489.9 9.6 %collective-permute-done.14 = bf16[144,2304]{1,0:T(8,128)(2,1)S(1)} collective-permute-done((bf16[144,2304]{1,0:T(8,128)(2,1)S(1)}, bf16[144,2304]{1,0:T(8,128)(2,1)S(1)}, u32[]{:S(2)}, u32[]{:S(2)}) %collective-permute-start.14) | collective-permute-done | bytes 663584 | tf_op jit(solution)/shard_map/ppermute | solution.py:422
  500.6 14.1 %collective-permute-done.15 = bf16[72,2304]{1,0:T(8,128)(2,1)S(1)} collective-permute-done((bf16[72,2304]{1,0:T(8,128)(2,1)S(1)}, bf16[72,2304]{1,0:T(8,128)(2,1)S(1)}, u32[]{:S(2)}, u32[]{:S(2)}) %collective-permute-start.15) | collective-permute-done | bytes 331808 | tf_op jit(solution)/shard_map/ppermute | solution.py:422
  (433 shorter events, 109.9 us)
Async XLA Ops:
  0.6 183.5 %copy-start = (bf16[1536,1152]{1,0:T(8,128)(2,1)S(1)}, bf16[1536,1152]{1,0:T(8,128)(2,1)}, u32[]{:S(2)}) copy-start(bf16[1536,1152]{1,0:T(8,128)(2,1)} %param.26) | copy-start | bytes 10616836
  32.9 14.1 %copy-start.104 = (f32[72]{0:T(128)S(1)}, f32[72]{0:T(128)}, u32[]{:S(2)}) copy-start(f32[72]{0:T(128)} %param.23) | copy-start | bytes 868
  32.9 14.1 %copy-start.105 = (f32[72]{0:T(128)S(1)}, f32[72]{0:T(128)}, u32[]{:S(2)}) copy-start(f32[72]{0:T(128)} %param.22) | copy-start | bytes 868
  32.9 40.0 %all-to-all-start = ((f32[16,3,6912]{2,1,0:T(4,128)}), f32[16,3,6912]{2,1,0:T(4,128)}, u32[]{:S(2)}, u32[]{:S(2)}) async-start(f32[16,3,6912]{2,1,0:T(4,128)} %reshape.251), calls=%async_computation | async-start | bytes 3538944 | tf_op jit(solution)/shard_map/all_to_all | solution.py:470
  37.5 28.4 %collective-permute-start = (bf16[384,1152]{1,0:T(8,128)(2,1)}, bf16[384,1152]{1,0:T(8,128)(2,1)}, u32[]{:S(2)}, u32[]{:S(2)}) collective-permute-start(bf16[384,1152]{1,0:T(8,128)(2,1)} %param.14), channel_id=1, source_target_pairs={{0,1},{1,0},{2,3},{3,2},{4,5},{5,4},{6,7},{7,6},{8,9},{9,8},{10,11... | collective-permute-start | bytes 2654216 | tf_op jit(solution)/shard_map/ppermute | solution.py:390
  39.0 88.0 %collective-permute-start.4 = (bf16[384,1152]{1,0:T(8,128)(2,1)}, bf16[384,1152]{1,0:T(8,128)(2,1)}, u32[]{:S(2)}, u32[]{:S(2)}) collective-permute-start(bf16[384,1152]{1,0:T(8,128)(2,1)} %param.27), channel_id=1, source_target_pairs={{0,1},{1,0},{2,3},{3,2},{4,5},{5,4},{6,7},{7,6},{8,9},{9,8},{10,11... | collective-permute-start | bytes 2654216 | tf_op jit(solution)/shard_map/ppermute | solution.py:390
  87.5 25.3 %copy-start.111 = (bf16[576,1152]{1,0:T(8,128)(2,1)S(1)}, bf16[576,1152]{1,0:T(8,128)(2,1)}, u32[]{:S(2)}) copy-start(bf16[576,1152]{1,0:T(8,128)(2,1)} %param.21) | copy-start | bytes 3981316
  115.6 22.6 %collective-permute-start.1 = (bf16[384,1152]{1,0:T(8,128)(2,1)}, bf16[384,1152]{1,0:T(8,128)(2,1)}, u32[]{:S(2)}, u32[]{:S(2)}) collective-permute-start(bf16[384,1152]{1,0:T(8,128)(2,1)} %convolution_convert_fusion.4), channel_id=1, source_target_pairs={{0,1},{1,0},{2,3},{3,2},{4,5},{5,4},{6,7},{7,6},{8,9},{9,8},{10,11... | collective-permute-start | bytes 2654216 | tf_op jit(solution)/shard_map/ppermute | solution.py:390
  124.8 13.5 %copy-start.115 = (bf16[768,576]{1,0:T(8,128)(2,1)S(1)}, bf16[768,576]{1,0:T(8,128)(2,1)}, u32[]{:S(2)}) copy-start(bf16[768,576]{1,0:T(8,128)(2,1)} %get-tuple-element.24) | copy-start | bytes 2654212
  124.9 13.4 %copy-start.7 = (bf16[384,1152]{1,0:T(8,128)(2,1)S(1)}, bf16[384,1152]{1,0:T(8,128)(2,1)}, u32[]{:S(2)}) copy-start(bf16[384,1152]{1,0:T(8,128)(2,1)} %param.14) | copy-start | bytes 2654212
  124.9 13.4 %copy-start.25 = (bf16[384,1152]{1,0:T(8,128)(2,1)S(1)}, bf16[384,1152]{1,0:T(8,128)(2,1)}, u32[]{:S(2)}) copy-start(bf16[384,1152]{1,0:T(8,128)(2,1)} %param.27) | copy-start | bytes 2654212
  124.9 13.4 %copy-start.61 = (f32[384]{0:T(512)S(1)}, f32[384]{0:T(512)}, u32[]{:S(2)}) copy-start(f32[384]{0:T(512)} %get-tuple-element.77) | copy-start | bytes 4612
  149.5 21.8 %collective-permute-start.2 = (bf16[384,1152]{1,0:T(8,128)(2,1)}, bf16[384,1152]{1,0:T(8,128)(2,1)}, u32[]{:S(2)}, u32[]{:S(2)}) collective-permute-start(bf16[384,1152]{1,0:T(8,128)(2,1)} %add_convert_fusion.8), channel_id=1, source_target_pairs={{0,1},{1,0},{2,3},{3,2},{4,5},{5,4},{6,7},{7,6},{8,9},{9,8},{10,11... | collective-permute-start | bytes 2654216 | tf_op jit(solution)/shard_map/ppermute | solution.py:390
  162.3 15.3 %copy-start.109 = (bf16[1152,1536]{1,0:T(8,128)(2,1)S(1)}, bf16[1152,1536]{1,0:T(8,128)(2,1)}, u32[]{:S(2)}) copy-start(bf16[1152,1536]{1,0:T(8,128)(2,1)} %param.25) | copy-start | bytes 10616836
  195.3 22.9 %collective-permute-start.3 = (bf16[384,1152]{1,0:T(8,128)(2,1)}, bf16[384,1152]{1,0:T(8,128)(2,1)}, u32[]{:S(2)}, u32[]{:S(2)}) collective-permute-start(bf16[384,1152]{1,0:T(8,128)(2,1)} %convolution_convert_fusion.3), channel_id=1, source_target_pairs={{0,1},{1,0},{2,3},{3,2},{4,5},{5,4},{6,7},{7,6},{8,9},{9,8},{10,11... | collective-permute-start | bytes 2654216 | tf_op jit(solution)/shard_map/ppermute | solution.py:390
  201.2 34.0 %collective-permute-start.5 = (bf16[384,1152]{1,0:T(8,128)(2,1)}, bf16[384,1152]{1,0:T(8,128)(2,1)}, u32[]{:S(2)}, u32[]{:S(2)}) collective-permute-start(bf16[384,1152]{1,0:T(8,128)(2,1)} %fusion.7), channel_id=1, source_target_pairs={{0,1},{1,0},{2,3},{3,2},{4,5},{5,4},{6,7},{7,6},{8,9},{9,8},{10,11... | collective-permute-start | bytes 2654216 | tf_op jit(solution)/shard_map/ppermute | solution.py:390
  216.1 19.0 %copy-start.35 = (f32[384,1152]{1,0:T(8,128)}, f32[384,1152]{1,0:T(8,128)S(1)}, u32[]{:S(2)}) copy-start(f32[384,1152]{1,0:T(8,128)S(1)} %fusion.36) | copy-start | bytes 5308420
  216.1 19.0 %copy-start.3 = (f32[384,1152]{1,0:T(8,128)S(1)}, f32[384,1152]{1,0:T(8,128)}, u32[]{:S(2)}) copy-start(f32[384,1152]{1,0:T(8,128)} %copy-done.2) | copy-start | bytes 5308420
  216.1 19.1 %copy-start.56 = (f32[1152]{0:T(1024)S(1)}, f32[1152]{0:T(1024)}, u32[]{:S(2)}) copy-start(f32[1152]{0:T(1024)} %get-tuple-element.61) | copy-start | bytes 13828
  216.1 19.1 %copy-start.58 = (f32[1152]{0:T(1024)S(1)}, f32[1152]{0:T(1024)}, u32[]{:S(2)}) copy-start(f32[1152]{0:T(1024)} %get-tuple-element.62) | copy-start | bytes 13828
  216.1 19.1 %copy-start.60 = (f32[1152]{0:T(1024)S(1)}, f32[1152]{0:T(1024)}, u32[]{:S(2)}) copy-start(f32[1152]{0:T(1024)} %get-tuple-element.63) | copy-start | bytes 13828
  216.1 19.1 %copy-start.62 = (f32[384]{0:T(512)S(1)}, f32[384]{0:T(512)}, u32[]{:S(2)}) copy-start(f32[384]{0:T(512)} %get-tuple-element.77) | copy-start | bytes 4612
  216.1 19.1 %copy-start.65 = (f32[384]{0:T(512)S(1)}, f32[384]{0:T(512)}, u32[]{:S(2)}) copy-start(f32[384]{0:T(512)} %get-tuple-element.78) | copy-start | bytes 4612
  216.1 19.1 %copy-start.68 = (f32[384]{0:T(512)S(1)}, f32[384]{0:T(512)}, u32[]{:S(2)}) copy-start(f32[384]{0:T(512)} %get-tuple-element.80) | copy-start | bytes 4612
  216.1 19.1 %copy-start.82 = (f32[384]{0:T(512)S(1)}, f32[384]{0:T(512)}, u32[]{:S(2)}) copy-start(f32[384]{0:T(512)} %copy-done.81) | copy-start | bytes 4612
  216.2 19.1 %copy-start.90 = (f32[384]{0:T(512)S(1)}, f32[384]{0:T(512)}, u32[]{:S(2)}) copy-start(f32[384]{0:T(512)} %copy-done.89) | copy-start | bytes 4612
  216.2 19.1 %copy-start.92 = (f32[1152]{0:T(1024)S(1)}, f32[1152]{0:T(1024)}, u32[]{:S(2)}) copy-start(f32[1152]{0:T(1024)} %get-tuple-element.57) | copy-start | bytes 13828
  216.2 19.1 %copy-start.94 = (f32[1152]{0:T(1024)S(1)}, f32[1152]{0:T(1024)}, u32[]{:S(2)}) copy-start(f32[1152]{0:T(1024)} %get-tuple-element.64) | copy-start | bytes 13828
  216.2 19.1 %copy-start.96 = (f32[1152]{0:T(1024)S(1)}, f32[1152]{0:T(1024)}, u32[]{:S(2)}) copy-start(f32[1152]{0:T(1024)} %get-tuple-element.65) | copy-start | bytes 13828
  216.2 19.1 %copy-start.110 = (bf16[1152,1536]{1,0:T(8,128)(2,1)S(1)}, bf16[1152,1536]{1,0:T(8,128)(2,1)}, u32[]{:S(2)}) copy-start(bf16[1152,1536]{1,0:T(8,128)(2,1)} %param.25) | copy-start | bytes 10616836
  216.2 19.1 %copy-start.121 = (bf16[768,1536]{1,0:T(8,128)(2,1)S(1)}, bf16[768,1536]{1,0:T(8,128)(2,1)}, u32[]{:S(2)}) copy-start(bf16[768,1536]{1,0:T(8,128)(2,1)} %copy-done.120) | copy-start | bytes 7077892
  218.0 24.2 %copy-start.26 = (bf16[384,1152]{1,0:T(8,128)(2,1)S(1)}, bf16[384,1152]{1,0:T(8,128)(2,1)}, u32[]{:S(2)}) copy-start(bf16[384,1152]{1,0:T(8,128)(2,1)} %param.27) | copy-start | bytes 2654212
  218.0 24.2 %copy-start.76 = (f32[1152]{0:T(1024)S(1)}, f32[1152]{0:T(1024)}, u32[]{:S(2)}) copy-start(f32[1152]{0:T(1024)} %get-tuple-element.72) | copy-start | bytes 13828
  218.0 24.2 %copy-start.78 = (f32[1152]{0:T(1024)S(1)}, f32[1152]{0:T(1024)}, u32[]{:S(2)}) copy-start(f32[1152]{0:T(1024)} %get-tuple-element.73) | copy-start | bytes 13828
  218.0 24.2 %copy-start.80 = (f32[1152]{0:T(1024)S(1)}, f32[1152]{0:T(1024)}, u32[]{:S(2)}) copy-start(f32[1152]{0:T(1024)} %get-tuple-element.74) | copy-start | bytes 13828
  245.2 19.7 %collective-permute-start.6 = (bf16[384,1152]{1,0:T(8,128)(2,1)S(1)}, bf16[384,1152]{1,0:T(8,128)(2,1)S(1)}, u32[]{:S(2)}, u32[]{:S(2)}) collective-permute-start(bf16[384,1152]{1,0:T(8,128)(2,1)S(1)} %get-tuple-element.98), channel_id=1, source_target_pairs={{0,1},{1,0},{2,3},{3,2},{4,5},{5,4},{6,7},{7,6},{8,9},{9,8},{10,11... | collective-permute-start | bytes 2654216 | tf_op jit(solution)/shard_map/ppermute | solution.py:390
  249.5 71.0 %collective-permute-start.16 = (bf16[576,1536]{1,0:T(8,128)(2,1)}, bf16[576,1536]{1,0:T(8,128)(2,1)}, u32[]{:S(2)}, u32[]{:S(2)}) collective-permute-start(bf16[576,1536]{1,0:T(8,128)(2,1)} %convolution_convert_fusion.2), channel_id=1, source_target_pairs={{0,2},{2,0},{4,6},{6,4},{8,10},{10,8},{12,14},{14,12},{16,18},{18,... | collective-permute-start | bytes 5308424 | tf_op jit(solution)/shard_map/ppermute | solution.py:411
  253.2 75.6 %collective-permute-start.20 = (bf16[576,1536]{1,0:T(8,128)(2,1)}, bf16[576,1536]{1,0:T(8,128)(2,1)}, u32[]{:S(2)}, u32[]{:S(2)}) collective-permute-start(bf16[576,1536]{1,0:T(8,128)(2,1)} %convolution_convert_fusion.1), channel_id=1, source_target_pairs={{0,2},{2,0},{4,6},{6,4},{8,10},{10,8},{12,14},{14,12},{16,18},{18,... | collective-permute-start | bytes 5308424 | tf_op jit(solution)/shard_map/ppermute | solution.py:411
  256.5 67.7 %collective-permute-start.24 = (bf16[576,1536]{1,0:T(8,128)(2,1)}, bf16[576,1536]{1,0:T(8,128)(2,1)}, u32[]{:S(2)}, u32[]{:S(2)}) collective-permute-start(bf16[576,1536]{1,0:T(8,128)(2,1)} %convolution_convert_fusion), channel_id=1, source_target_pairs={{0,2},{2,0},{4,6},{6,4},{8,10},{10,8},{12,14},{14,12},{16,18},{18,... | collective-permute-start | bytes 5308424 | tf_op jit(solution)/shard_map/ppermute | solution.py:411
  269.6 25.7 %copy-start.13 = (bf16[1152,576]{0,1:T(8,128)(2,1)S(1)}, bf16[1152,576]{0,1:T(8,128)(2,1)}, u32[]{:S(2)}) copy-start(bf16[1152,576]{0,1:T(8,128)(2,1)} %param.18) | copy-start | bytes 3981316
  308.0 48.7 %collective-permute-start.7 = (bf16[384,1152]{1,0:T(8,128)(2,1)}, bf16[384,1152]{1,0:T(8,128)(2,1)}, u32[]{:S(2)}, u32[]{:S(2)}) collective-permute-start(bf16[384,1152]{1,0:T(8,128)(2,1)} %fusion.8), channel_id=1, source_target_pairs={{0,1},{1,0},{2,3},{3,2},{4,5},{5,4},{6,7},{7,6},{8,9},{9,8},{10,11... | collective-permute-start | bytes 2654216 | tf_op jit(solution)/shard_map/ppermute | solution.py:390
  310.0 26.8 %collective-permute-start.9 = (bf16[576,576]{1,0:T(8,128)(2,1)}, bf16[576,576]{1,0:T(8,128)(2,1)}, u32[]{:S(2)}, u32[]{:S(2)}) collective-permute-start(bf16[576,576]{1,0:T(8,128)(2,1)} %convolution_convert_fusion.9), channel_id=1, source_target_pairs={{0,2},{2,0},{4,6},{6,4},{8,10},{10,8},{12,14},{14,12},{16,18},{18,... | collective-permute-start | bytes 1990664 | tf_op jit(solution)/shard_map/ppermute | solution.py:411
  320.5 21.3 %collective-permute-start.10 = (bf16[576,576]{1,0:T(8,128)(2,1)S(1)}, bf16[576,576]{1,0:T(8,128)(2,1)S(1)}, u32[]{:S(2)}, u32[]{:S(2)}) collective-permute-start(bf16[576,576]{1,0:T(8,128)(2,1)S(1)} %copy-done.114), channel_id=1, source_target_pairs={{0,2},{2,0},{4,6},{6,4},{8,10},{10,8},{12,14},{14,12},{16,18},{18,... | collective-permute-start | bytes 1990664 | tf_op jit(solution)/shard_map/ppermute | solution.py:411
  324.3 18.5 %collective-permute-start.11 = (bf16[576,576]{1,0:T(8,128)(2,1)S(1)}, bf16[576,576]{1,0:T(8,128)(2,1)S(1)}, u32[]{:S(2)}, u32[]{:S(2)}) collective-permute-start(bf16[576,576]{1,0:T(8,128)(2,1)S(1)} %convolution_convert_fusion.7), channel_id=1, source_target_pairs={{0,2},{2,0},{4,6},{6,4},{8,10},{10,8},{12,14},{14,12},{16,18},{18,... | collective-permute-start | bytes 1990664 | tf_op jit(solution)/shard_map/ppermute | solution.py:411
  328.9 17.8 %collective-permute-start.12 = (bf16[576,576]{1,0:T(8,128)(2,1)S(1)}, bf16[576,576]{1,0:T(8,128)(2,1)S(1)}, u32[]{:S(2)}, u32[]{:S(2)}) collective-permute-start(bf16[576,576]{1,0:T(8,128)(2,1)S(1)} %convolution_convert_fusion.6), channel_id=1, source_target_pairs={{0,2},{2,0},{4,6},{6,4},{8,10},{10,8},{12,14},{14,12},{16,18},{18,... | collective-permute-start | bytes 1990664 | tf_op jit(solution)/shard_map/ppermute | solution.py:411
  336.8 29.8 %collective-permute-start.17 = (bf16[288,1536]{1,0:T(8,128)(2,1)}, bf16[288,1536]{1,0:T(8,128)(2,1)}, u32[]{:S(2)}, u32[]{:S(2)}) collective-permute-start(bf16[288,1536]{1,0:T(8,128)(2,1)} %slice.465), channel_id=1, source_target_pairs={{0,4},{2,6},{4,0},{6,2},{8,12},{10,14},{12,8},{14,10},{16,20},{18,... | collective-permute-start | bytes 2654216 | tf_op jit(solution)/shard_map/ppermute | solution.py:422
  341.8 37.8 %collective-permute-start.21 = (bf16[288,1536]{1,0:T(8,128)(2,1)}, bf16[288,1536]{1,0:T(8,128)(2,1)}, u32[]{:S(2)}, u32[]{:S(2)}) collective-permute-start(bf16[288,1536]{1,0:T(8,128)(2,1)} %slice.471), channel_id=1, source_target_pairs={{0,4},{2,6},{4,0},{6,2},{8,12},{10,14},{12,8},{14,10},{16,20},{18,... | collective-permute-start | bytes 2654216 | tf_op jit(solution)/shard_map/ppermute | solution.py:422
  342.8 55.8 %collective-permute-start.25 = (bf16[288,1536]{1,0:T(8,128)(2,1)}, bf16[288,1536]{1,0:T(8,128)(2,1)}, u32[]{:S(2)}, u32[]{:S(2)}) collective-permute-start(bf16[288,1536]{1,0:T(8,128)(2,1)} %slice.479), channel_id=1, source_target_pairs={{0,4},{2,6},{4,0},{6,2},{8,12},{10,14},{12,8},{14,10},{16,20},{18,... | collective-permute-start | bytes 2654216 | tf_op jit(solution)/shard_map/ppermute | solution.py:422
  356.6 111.2 %collective-permute-start.13 = (bf16[288,2304]{1,0:T(8,128)(2,1)}, bf16[288,2304]{1,0:T(8,128)(2,1)}, u32[]{:S(2)}, u32[]{:S(2)}) collective-permute-start(bf16[288,2304]{1,0:T(8,128)(2,1)} %slice.456), channel_id=1, source_target_pairs={{0,4},{2,6},{4,0},{6,2},{8,12},{10,14},{12,8},{14,10},{16,20},{18,... | collective-permute-start | bytes 3981320 | tf_op jit(solution)/shard_map/ppermute | solution.py:422
  366.0 13.6 %copy-start.33 = (bf16[576,1536]{1,0:T(8,128)(2,1)S(1)}, bf16[576,1536]{1,0:T(8,128)(2,1)}, u32[]{:S(2)}) copy-start(bf16[576,1536]{1,0:T(8,128)(2,1)} %copy-done.32) | copy-start | bytes 5308420
  366.1 42.4 %collective-permute-start.8 = (bf16[4,6912]{1,0:T(4,128)(2,1)S(1)}, bf16[4,6912]{1,0:T(4,128)(2,1)S(1)}, u32[]{:S(2)}, u32[]{:S(2)}) collective-permute-start(bf16[4,6912]{1,0:T(4,128)(2,1)S(1)} %fusion.62), channel_id=1, source_target_pairs={{0,1},{1,0},{2,3},{3,2},{4,5},{5,4},{6,7},{7,6},{8,9},{9,8},{10,11... | collective-permute-start | bytes 165896 | tf_op jit(solution)/shard_map/ppermute | solution.py:390
  368.9 29.7 %copy-start.29 = (bf16[576,1536]{1,0:T(8,128)(2,1)S(1)}, bf16[576,1536]{1,0:T(8,128)(2,1)}, u32[]{:S(2)}) copy-start(bf16[576,1536]{1,0:T(8,128)(2,1)} %copy-done.28) | copy-start | bytes 5308420
  368.9 91.5 %collective-permute-start.18 = (bf16[144,1536]{1,0:T(8,128)(2,1)}, bf16[144,1536]{1,0:T(8,128)(2,1)}, u32[]{:S(2)}, u32[]{:S(2)}) collective-permute-start(bf16[144,1536]{1,0:T(8,128)(2,1)} %slice.467), channel_id=1, source_target_pairs={{0,8},{2,10},{4,12},{6,14},{8,0},{10,2},{12,4},{14,6},{16,24},{18,... | collective-permute-start | bytes 1327112 | tf_op jit(solution)/shard_map/ppermute | solution.py:422
  381.0 19.0 %copy-start.22 = (bf16[288,1536]{1,0:T(8,128)(2,1)}, bf16[288,1536]{1,0:T(8,128)(2,1)S(1)}, u32[]{:S(2)}) copy-start(bf16[288,1536]{1,0:T(8,128)(2,1)S(1)} %add_convert_fusion.5) | copy-start | bytes 2654212
  381.8 80.3 %collective-permute-start.22 = (bf16[144,1536]{1,0:T(8,128)(2,1)}, bf16[144,1536]{1,0:T(8,128)(2,1)}, u32[]{:S(2)}, u32[]{:S(2)}) collective-permute-start(bf16[144,1536]{1,0:T(8,128)(2,1)} %slice.473), channel_id=1, source_target_pairs={{0,8},{2,10},{4,12},{6,14},{8,0},{10,2},{12,4},{14,6},{16,24},{18,... | collective-permute-start | bytes 1327112 | tf_op jit(solution)/shard_map/ppermute | solution.py:422
  401.7 44.8 %copy-start.17 = (bf16[72,6912]{1,0:T(8,128)(2,1)S(1)}, bf16[72,6912]{1,0:T(8,128)(2,1)}, u32[]{:S(2)}) copy-start(bf16[72,6912]{1,0:T(8,128)(2,1)} %param.17) | copy-start | bytes 2985988
  401.7 64.2 %collective-permute-start.26 = (bf16[144,1536]{1,0:T(8,128)(2,1)}, bf16[144,1536]{1,0:T(8,128)(2,1)}, u32[]{:S(2)}, u32[]{:S(2)}) collective-permute-start(bf16[144,1536]{1,0:T(8,128)(2,1)} %slice.481), channel_id=1, source_target_pairs={{0,8},{2,10},{4,12},{6,14},{8,0},{10,2},{12,4},{14,6},{16,24},{18,... | collective-permute-start | bytes 1327112 | tf_op jit(solution)/shard_map/ppermute | solution.py:422
  448.3 10.0 %all-to-all-start.1 = ((f32[16,1,216]{2,1,0:T(1,128)}), f32[16,1,216]{2,1,0:T(1,128)S(1)}, u32[]{:S(2)}, u32[]{:S(2)}) async-start(f32[16,1,216]{2,1,0:T(1,128)} %reshape.294), calls=%async_computation.1 | async-start | bytes 32768 | tf_op jit(solution)/shard_map/all_to_all | solution.py:590
  461.6 22.7 %collective-permute-start.19 = (bf16[72,1536]{1,0:T(8,128)(2,1)S(1)}, bf16[72,1536]{1,0:T(8,128)(2,1)S(1)}, u32[]{:S(2)}, u32[]{:S(2)}) collective-permute-start(bf16[72,1536]{1,0:T(8,128)(2,1)S(1)} %slice.469), channel_id=1, source_target_pairs={{0,16},{2,18},{4,20},{6,22},{8,24},{10,26},{12,28},{14,30},{16,0},... | collective-permute-start | bytes 663560 | tf_op jit(solution)/shard_map/ppermute | solution.py:422
  463.6 25.4 %collective-permute-start.23 = (bf16[72,1536]{1,0:T(8,128)(2,1)S(1)}, bf16[72,1536]{1,0:T(8,128)(2,1)S(1)}, u32[]{:S(2)}, u32[]{:S(2)}) collective-permute-start(bf16[72,1536]{1,0:T(8,128)(2,1)S(1)} %slice.475), channel_id=1, source_target_pairs={{0,16},{2,18},{4,20},{6,22},{8,24},{10,26},{12,28},{14,30},{16,0},... | collective-permute-start | bytes 663560 | tf_op jit(solution)/shard_map/ppermute | solution.py:422
  467.1 32.7 %collective-permute-start.27 = (bf16[72,1536]{1,0:T(8,128)(2,1)S(1)}, bf16[72,1536]{1,0:T(8,128)(2,1)S(1)}, u32[]{:S(2)}, u32[]{:S(2)}) collective-permute-start(bf16[72,1536]{1,0:T(8,128)(2,1)S(1)} %slice.483), channel_id=1, source_target_pairs={{0,16},{2,18},{4,20},{6,22},{8,24},{10,26},{12,28},{14,30},{16,0},... | collective-permute-start | bytes 663560 | tf_op jit(solution)/shard_map/ppermute | solution.py:422
  469.5 29.9 %collective-permute-start.14 = (bf16[144,2304]{1,0:T(8,128)(2,1)S(1)}, bf16[144,2304]{1,0:T(8,128)(2,1)S(1)}, u32[]{:S(2)}, u32[]{:S(2)}) collective-permute-start(bf16[144,2304]{1,0:T(8,128)(2,1)S(1)} %slice.458), channel_id=1, source_target_pairs={{0,8},{2,10},{4,12},{6,14},{8,0},{10,2},{12,4},{14,6},{16,24},{18,... | collective-permute-start | bytes 1990664 | tf_op jit(solution)/shard_map/ppermute | solution.py:422
  499.6 16.1 %copy-start.1 = (bf16[1536,1152]{1,0:T(8,128)(2,1)S(1)}, bf16[1536,1152]{1,0:T(8,128)(2,1)}, u32[]{:S(2)}) copy-start(bf16[1536,1152]{1,0:T(8,128)(2,1)} %param.26) | copy-start | bytes 10616836
  499.7 15.0 %collective-permute-start.15 = (bf16[72,2304]{1,0:T(8,128)(2,1)S(1)}, bf16[72,2304]{1,0:T(8,128)(2,1)S(1)}, u32[]{:S(2)}, u32[]{:S(2)}) collective-permute-start(bf16[72,2304]{1,0:T(8,128)(2,1)S(1)} %slice.460), channel_id=1, source_target_pairs={{0,16},{2,18},{4,20},{6,22},{8,24},{10,26},{12,28},{14,30},{16,0},... | collective-permute-start | bytes 995336 | tf_op jit(solution)/shard_map/ppermute | solution.py:422
  (92 other events, 484.7 us)

commit v2 on v1

--- a/solution.py
+++ b/solution.py
@@ -92,9 +92,7 @@
     items,
     spans,
     x_ref,
-    wq_ref,
-    wk_ref,
-    wv_ref,
+    w_ref,
     gq_ref,
     gk_ref,
     cos_ref,
@@ -120,12 +118,13 @@
         for first in range(0, length, TILE):
             rows = pl.ds(first, TILE)
             x = x_ref[rows, :]
-            for w_ref, raw in ((wq_ref, qraw), (wk_ref, kraw), (wv_ref, vraw)):
-
-                def store(h, part, raw=raw):
+            wide_in = dot(x, w_ref[...])
+            wide_in = jnp.concatenate([wide_in, jnp.zeros((TILE, LANES), F32)], axis=1)
+            for which, raw in enumerate((qraw, kraw, vraw)):
+                for h in range(heads):
+                    first_lane = (which * heads + h) * HD
+                    part = only_head(wide_in[:, first_lane : first_lane + LANES])
                     raw[h, rows, :] = part.astype(raw.dtype)
-
-                split_heads(dot(x, w_ref[...]), store, heads)
 
     for raw, pre_ref, low_ref, gain_ref in (
         (qraw, qpre_ref, q_ref, gq_ref),
@@ -181,9 +180,7 @@
     gk_ref,
     cos_ref,
     sin_ref,
-    dq_ref,
-    dk_ref,
-    dv_ref,
+    d_ref,
     gain_ref,
     graw,
     dqraw,
@@ -243,10 +240,11 @@
 
     @pl.when(head == heads - 1)
     def _():
-        for raw, o_ref in ((dqraw, dq_ref), (dkraw, dk_ref), (dvraw, dv_ref)):
+        for which, raw in enumerate((dqraw, dkraw, dvraw)):
             for h in range(heads):
-                wide[:, h * HD : h * HD + HD] = raw[h][:, :HD]
-            o_ref[...] = wide[...].astype(BF16)
+                first_lane = (which * heads + h) * HD
+                wide[:, first_lane : first_lane + HD] = raw[h][:, :HD]
+        d_ref[...] = wide[...].astype(BF16)
 
 
 def whole(shape):
@@ -257,9 +255,9 @@
     return pl.BlockSpec((1,) + shape, lambda h, spans: (h,) + (0,) * len(shape))
 
 
-def attend(spans, x, wq, wk, wv, gain_q, gain_k, cosine, sine):
+def attend(spans, x, w_qkv, gain_q, gain_k, cosine, sine):
     length, width = x.shape
-    heads = wq.shape[1] // HD
+    heads = w_qkv.shape[1] // HD // 3
     items = spans.shape[1]
     head_f32 = jax.ShapeDtypeStruct((heads, length, LANES), F32)
     head_low = jax.ShapeDtypeStruct((heads, length, LANES), BF16)
@@ -270,9 +268,7 @@
             grid=(heads,),
             in_specs=[
                 whole(x.shape),
-                whole(wq.shape),
-                whole(wk.shape),
-                whole(wv.shape),
+                whole(w_qkv.shape),
                 whole((1, LANES)),
                 whole((1, LANES)),
                 whole((length, LANES)),
@@ -311,14 +307,13 @@
             transcendentals=heads * items * SPAN * SPAN,
         ),
         name="attend",
-    )(spans, x, wq, wk, wv, gain_q, gain_k, cosine, sine)
+    )(spans, x, w_qkv, gain_q, gain_k, cosine, sine)
 
 
 def attend_back(spans, grad, saved, gain_q, gain_k, cosine, sine):
     length, width = grad.shape
     heads = width // HD
     items = spans.shape[1]
-    out = jax.ShapeDtypeStruct((length, width), BF16)
     return pl.pallas_call(
         functools.partial(attend_back_kernel, heads, items),
         grid_spec=pltpu.PrefetchScalarGridSpec(
@@ -338,9 +333,7 @@
                 whole((length, LANES)),
             ],
             out_specs=[
-                whole((length, width)),
-                whole((length, width)),
-                whole((length, width)),
+                whole((length, 3 * width)),
                 whole((8, LANES)),
             ],
             scratch_shapes=[
@@ -348,10 +341,13 @@
                 pltpu.VMEM((heads, length, LANES), F32),
                 pltpu.VMEM((heads, length, LANES), F32),
                 pltpu.VMEM((heads, length, LANES), F32),
-                pltpu.VMEM((length, width), F32),
+                pltpu.VMEM((length, 3 * width), F32),
             ],
         ),
-        out_shape=[out, out, out, jax.ShapeDtypeStruct((8, LANES), F32)],
+        out_shape=[
+            jax.ShapeDtypeStruct((length, 3 * width), BF16),
+            jax.ShapeDtypeStruct((8, LANES), F32),
+        ],
         compiler_params=pltpu.CompilerParams(vmem_limit_bytes=56 * 2**20),
         cost_estimate=pl.CostEstimate(
             flops=8 * heads * items * SPAN * SPAN * LANES,
@@ -424,6 +420,381 @@
         if bit < bits - 1:
             part = part.astype(BF16)
     return part.astype(F32)
+
+
+def remote(src, dst, send, recv, device):
+    return pltpu.make_async_remote_copy(
+        src_ref=src,
+        dst_ref=dst,
+        send_sem=send,
+        recv_sem=recv,
+        device_id=device,
+        device_id_type=pl.DeviceIdType.MESH,
+    )
+
+
+def block_at(position, me, bits):
+    block = 0
+    for bit in range(bits):
+        mine = (me // (1 << bit)) % 2
+        there = (position >> (bits - 1 - bit)) & 1
+        block = block + (1 << bit) * (1 - mine if there else mine)
+    return block
+
+
+def across(me, bit):
+    return me + (1 << bit) - 2 * (1 << bit) * ((me // (1 << bit)) % 2)
+
+
+def group_rows(count):
+    return -(-count // 16) * 16
+
+
+def greet(peers):
+    barrier = pltpu.get_barrier_semaphore()
+    for peer in peers:
+        pl.semaphore_signal(
+            barrier, inc=1, device_id=peer, device_id_type=pl.DeviceIdType.MESH
+        )
+    pl.semaphore_wait(barrier, len(peers))
+
+
+def tail_kernel(
+    dp,
+    items,
+    pieces,
+    d_ref,
+    attn_in_ref,
+    grad_attn_ref,
+    heads_ref,
+    w_ref,
+    tokens_ref,
+    resid_ref,
+    member_ref,
+    scale_ref,
+    early_ref,
+    gain_ref,
+    mod_ref,
+    grad_tokens_ref,
+    sums_ref,
+    all_ref,
+    gains_ref,
+    cond_ref,
+    part,
+    y_out,
+    y_in,
+    back,
+    core_out,
+    core_in,
+    core_keep,
+    x_out,
+    x_in,
+    x_keep,
+    z_out,
+    z_in,
+    z_keep,
+    w_out,
+    w_in,
+    early_in,
+    late_out,
+    late_in,
+    early_sum,
+    late_sum,
+    early_all,
+    late_all,
+    flat,
+    late_rows,
+    cond_out,
+    y_sems,
+    halving_sems,
+    early_send,
+    early_recv,
+    late_send,
+    late_recv,
+    cond_send,
+    cond_recv,
+):
+    bits = dp.bit_length() - 1
+    me = lax.axis_index("dp")
+    ten = lax.axis_index("tensor")
+    half = tokens_ref.shape[0]
+    width = tokens_ref.shape[1]
+    depth = width // dp
+    inner = d_ref.shape[1] // 3
+    piece = core_out.shape[2]
+    groups = width // LANES
+    early_groups = 4 * groups
+    late_groups = 2 * groups
+    early_span = early_ref.shape[0] // items
+    late_span = late_out.shape[0] // items
+    y_peer = (me, 1 - ten)
+    dp_peers = [((me + step) % dp, ten) for step in range(1, dp)]
+    greet([y_peer] + dp_peers)
+
+    def y_copy(which, src, dst):
+        return remote(src, dst, y_sems.at[0, which], y_sems.at[1, which], y_peer)
+
+    def halving(bit, which, src, dst):
+        return remote(
+            src,
+            dst,
+            halving_sems.at[0, bit, which],
+            halving_sems.at[1, bit, which],
+            (across(me, bit), ten),
+        )
+
+    def gather(src, all_there, send, recv):
+        copies = []
+        for step, peer in enumerate(dp_peers):
+            copies.append(remote(src, all_there.at[me], send.at[step], recv.at[me], peer))
+        return copies
+
+    def gathered(src, all_here, send, recv):
+        for step in range(1, dp):
+            source = (me + dp - step) % dp
+            remote(src, all_here.at[source], send.at[0], recv.at[source], y_peer).wait_recv()
+
+    early_copy = y_copy(0, early_ref, early_in)
+    early_copy.start()
+
+    other_rows = pl.ds(pl.multiple_of((1 - ten) * half, half), half)
+    own_rows = pl.ds(pl.multiple_of(ten * half, half), half)
+    y_out[...] = dot_t(d_ref[other_rows, :], w_ref[...]).astype(BF16)
+    back_copy = y_copy(1, y_out, y_in)
+    back_copy.start()
+
+    early_copy.wait_recv()
+    early_sum[...] = (early_ref[...].astype(F32) + early_in[...].astype(F32)).astype(BF16)
+    early_all[me] = early_sum[...]
+    early_copies = gather(early_sum, early_all, early_send, early_recv)
+    for copy in early_copies:
+        copy.start()
+
+    for first in range(0, width, LANES):
+        rows = pl.ds(first, LANES)
+        part[rows, : 3 * inner] = t_dot(attn_in_ref[:, rows], d_ref[...])
+        part[rows, 3 * inner :] = t_dot(grad_attn_ref[:, rows], heads_ref[...])
+
+    def packed(position, columns):
+        def rows_of(p):
+            return part[pl.ds(pl.multiple_of(block_at(p, me, bits) * depth, 8), depth), columns]
+
+        return jnp.concatenate([rows_of(position), rows_of(position + 1)]).astype(BF16)
+
+    core_copies = []
+    for p in range(pieces):
+        columns = pl.ds(p * piece, piece)
+        for position in range(0, dp // 2, 2):
+            rows = pl.ds(position * depth, 2 * depth)
+            core_out[p, rows, :] = packed(dp // 2 + position, columns)
+        core_copies.append(halving(0, p, core_out.at[p], core_in.at[p]))
+        core_copies[p].start()
+        for position in range(0, dp // 2, 2):
+            rows = pl.ds(position * depth, 2 * depth)
+            core_keep[p, rows, :] = packed(position, columns)
+
+    back[...] = dot_t(d_ref[own_rows, :], w_ref[...])
+
+    def level(bit, copies, keep, there, out, next_in, next_keep):
+        sent = []
+        size = keep.shape[1]
+        for p in range(pieces):
+            copies[p].wait_recv()
+            out[p] = (
+                keep[p, size // 2 :, :].astype(F32) + there[p, size // 2 :, :].astype(F32)
+            ).astype(BF16)
+            sent.append(halving(bit, p, out.at[p], next_in.at[p]))
+            sent[p].start()
+            next_keep[p] = (
+                keep[p, : size // 2, :].astype(F32) + there[p, : size // 2, :].astype(F32)
+            ).astype(BF16)
+        return sent
+
+    x_copies = level(1, core_copies, core_keep, core_in, x_out, x_in, x_keep)
+
+    back_copy.wait_recv()
+    shift_sums = [jnp.zeros((1, width), F32) for _ in range(items)]
+    scale_sums = [jnp.zeros((1, width), F32) for _ in range(items)]
+    for first in range(0, half, LANES):
+        rows = pl.ds(first, LANES)
+        values = tokens_ref[rows, :].astype(F32)
+        centred = values - jnp.mean(values, axis=1, keepdims=True)
+        inv = lax.rsqrt(jnp.mean(centred * centred, axis=1, keepdims=True) + EPSILON)
+        normed = centred * inv
+        grad = back[rows, :] + y_in[rows, :].astype(F32)
+        member = [member_ref[rows, item : item + 1] for item in range(items)]
+        scale = sum(member[item] * scale_ref[item : item + 1, :] for item in range(items))
+        product = grad * normed
+        for item in range(items):
+            shift_sums[item] += jnp.sum(member[item] * grad, axis=0, keepdims=True)
+            scale_sums[item] += jnp.sum(member[item] * product, axis=0, keepdims=True)
+        n = grad * (1.0 + scale)
+        mean_n = jnp.mean(n, axis=1, keepdims=True)
+        mean_along = jnp.mean(n * normed, axis=1, keepdims=True)
+        grad_tokens_ref[rows, :] = (
+            resid_ref[rows, :] + inv * (n - mean_n - normed * mean_along)
+        ).astype(BF16)
+    late_rows[...] = jnp.zeros_like(late_rows)
+    for item in range(items):
+        for group in range(groups):
+            lanes = slice(group * LANES, group * LANES + LANES)
+            row = item * late_span + group
+            late_rows[row : row + 1, :] = shift_sums[item][:, lanes]
+            late_rows[row + groups : row + groups + 1, :] = scale_sums[item][:, lanes]
+    late_rows[late_groups : late_groups + 2, :] = gain_ref[:2, :]
+    late_out[...] = late_rows[...].astype(BF16)
+    late_copy = y_copy(2, late_out, late_in)
+    late_copy.start()
+
+    z_copies = level(2, x_copies, x_keep, x_in, z_out, z_in, z_keep)
+
+    late_copy.wait_recv()
+    late_sum[...] = (late_out[...].astype(F32) + late_in[...].astype(F32)).astype(BF16)
+    late_all[me] = late_sum[...]
+    late_copies = gather(late_sum, late_all, late_send, late_recv)
+    for copy in late_copies:
+        copy.start()
+
+    last_copies = []
+    for p in range(pieces):
+        z_copies[p].wait_recv()
+        total = z_keep[p].astype(F32) + z_in[p].astype(F32)
+        w_out[p, depth:, :] = jnp.zeros((w_out.shape[1] - depth, piece), BF16)
+        w_out[p, :depth, :] = total[depth:].astype(BF16)
+        last_copies.append(halving(3, p, w_out.at[p], w_in.at[p]))
+        last_copies[p].start()
+        sums_ref[p] = total[:depth]
+
+    gathered(early_sum, early_all, early_send, early_recv)
+    count = dp * items
+    for source in range(dp):
+        flat[pl.ds(source * items * early_span, items * early_span), :] = early_all[
+            source
+        ].astype(F32)
+    for group in range(early_groups):
+        lanes = pl.ds((late_groups + group) * LANES, LANES)
+        all_ref[:, lanes] = flat[pl.ds(group, count, stride=early_span), :].astype(BF16)
+    gathered(late_sum, late_all, late_send, late_recv)
+    gains = jnp.zeros((2, LANES), F32)
+    for source in range(dp):
+        block = late_all[source].astype(F32)
+        gains += block[late_groups : late_groups + 2]
+        flat[pl.ds(source * items * late_span, items * late_span), :] = block
+    gains_ref[...] = jnp.zeros_like(gains_ref)
+    gains_ref[:2, :] = gains
+    for group in range(late_groups):
+        lanes = pl.ds(group * LANES, LANES)
+        all_ref[:, lanes] = flat[pl.ds(group, count, stride=late_span), :].astype(BF16)
+    cond_out[...] = jnp.zeros_like(cond_out)
+    flat[:count, :depth] = dot_t(all_ref[...], mod_ref[...])
+    for dest in range(dp):
+        cond_out[dest, :items, :] = flat[pl.ds(dest * items, items), :]
+    cond_ref[me] = cond_out[me]
+    cond_copies = []
+    for step, peer in enumerate(dp_peers):
+        cond_copies.append(
+            remote(cond_out.at[peer[0]], cond_ref.at[me], cond_send.at[step], cond_recv.at[me], peer)
+        )
+        cond_copies[-1].start()
+
+    for p in range(pieces):
+        last_copies[p].wait_recv()
+        sums_ref[p] += w_in[p, :depth, :].astype(F32)
+    gathered(cond_out.at[0], cond_ref, cond_send, cond_recv)
+    for copy in (
+        [early_copy, back_copy, late_copy]
+        + early_copies
+        + late_copies
+        + cond_copies
+        + core_copies
+        + x_copies
+        + z_copies
+        + last_copies
+    ):
+        copy.wait_send()
+
+
+def tail(dp, d, attn_in, grad_attn, heads_out, w_qkv, tokens, resid, member, scale, early, gains, mod):
+    half, width = tokens.shape
+    items = scale.shape[0]
+    length = 2 * half
+    inner = d.shape[1] // 3
+    depth = width // dp
+    pieces = 3
+    piece = 4 * inner // pieces
+    groups = width // LANES
+    early_rows = early.shape[0]
+    late_span = group_rows(2 * groups + 2)
+    late_rows = items * late_span
+    count = dp * items
+    columns = mod.shape[1]
+    vmem = pltpu.VMEM
+
+    def level(rows):
+        return [vmem((pieces, rows, piece), BF16)] * 3
+
+    dma = pltpu.SemaphoreType.DMA
+    return pl.pallas_call(
+        functools.partial(tail_kernel, dp, items, pieces),
+        out_shape=[
+            jax.ShapeDtypeStruct((half, width), BF16),
+            jax.ShapeDtypeStruct((pieces, depth, piece), F32),
+            jax.ShapeDtypeStruct((count, columns), BF16),
+            jax.ShapeDtypeStruct((8, LANES), F32),
+            jax.ShapeDtypeStruct((dp, 8, LANES), F32),
+        ],
+        in_specs=[pl.BlockSpec(memory_space=pltpu.VMEM)] * 12,
+        out_specs=[pl.BlockSpec(memory_space=pltpu.VMEM)] * 5,
+        scratch_shapes=[
+            vmem((width, 4 * inner), F32),
+            vmem((half, width), BF16),
+            vmem((half, width), BF16),
+            vmem((half, width), F32),
+            *level(width // 2),
+            *level(width // 4),
+            *level(width // 8),
+            vmem((pieces, group_rows(depth), piece), BF16),
+            vmem((pieces, group_rows(depth), piece), BF16),
+            vmem((early_rows, LANES), BF16),
+            vmem((late_rows, LANES), BF16),
+            vmem((late_rows, LANES), BF16),
+            vmem((early_rows, LANES), BF16),
+            vmem((late_rows, LANES), BF16),
+            vmem((dp, early_rows, LANES), BF16),
+            vmem((dp, late_rows, LANES), BF16),
+            vmem((dp * early_rows, LANES), F32),
+            vmem((late_rows, LANES), F32),
+            vmem((dp, 8, LANES), F32),
+            dma((2, 3)),
+            dma((2, 4, pieces)),
+            dma((dp,)),
+            dma((dp,)),
+            dma((dp,)),
+            dma((dp,)),
+            dma((dp,)),
+            dma((dp,)),
+        ],
+        compiler_params=pltpu.CompilerParams(
+            collective_id=1, has_side_effects=True, vmem_limit_bytes=60 * 2**20
+        ),
+        cost_estimate=pl.CostEstimate(
+            flops=4 * length * width * 4 * inner, bytes_accessed=20 * 2**20, transcendentals=0
+        ),
+        name="tail",
+    )(
+        d,
+        attn_in,
+        grad_attn,
+        heads_out,
+        w_qkv,
+        tokens,
+        resid,
+        member,
+        scale,
+        early,
+        gains,
+        mod,
+    )
 
 
 def shards(
@@ -482,9 +853,8 @@
         norm_all * (1.0 + per_token(member, scale_one)) + per_token(member, shift_one)
     ).astype(BF16)
 
-    heads_out, *saved = attend(
-        spans, attn_in, query_weight, key_weight, value_weight, gain_q, gain_k, cosine, sine
-    )
+    w_qkv = jnp.concatenate([query_weight, key_weight, value_weight], axis=1)
+    heads_out, *saved = attend(spans, attn_in, w_qkv, gain_q, gain_k, cosine, sine)
     heads_other = lax.dynamic_slice_in_dim(heads_out, other_first, half, 0)
     heads_own = lax.dynamic_slice_in_dim(heads_out, own_first, half, 0)
     attn_recv = swap(dot(heads_other, proj_weight).astype(BF16))
@@ -536,42 +906,15 @@
     grad_attn = (gate_one_own * grad_resid).astype(BF16)
     grad_attn_all = in_order(grad_attn, swap(grad_attn), second)
     grad_heads = dot_t(grad_attn_all, proj_weight).astype(BF16)
-    dq, dk, dv, gain_parts = attend_back(spans, grad_heads, saved, gain_q, gain_k, cosine, sine)
-
-    def attn_back(first):
-        def rows(array):
-            return lax.dynamic_slice_in_dim(array, first, half, 0)
-
-        return (
-            dot_t(rows(dq), query_weight)
-            + dot_t(rows(dk), key_weight)
-            + dot_t(rows(dv), value_weight)
-        )
-
-    attn_back_recv = swap(attn_back(other_first).astype(BF16))
-    grad_attn_in = attn_back(own_first) + attn_back_recv.astype(F32)
-    attn_in_rows = halving_rows(attn_in, bits)
-    grad_attn_rows = halving_rows(grad_attn_all, bits)
-    attn_parts = jnp.concatenate(
+    grad_heads, down_part, gate_part, up_part = lax.optimization_barrier(
+        (grad_heads, down_part, gate_part, up_part)
+    )
+    grad_down = rest_of_halving(down_part, bits).T
+    grad_gate = rest_of_halving(gate_part, bits)
+    grad_up = rest_of_halving(up_part, bits)
+    d, gain_parts = attend_back(spans, grad_heads, saved, gain_q, gain_k, cosine, sine)
+    early = jnp.concatenate(
         [
-            first_halving(attn_in_rows, dq),
-            first_halving(attn_in_rows, dk),
-            first_halving(attn_in_rows, dv),
-            first_halving(grad_attn_rows, heads_out),
-        ],
-        axis=1,
-    )
-
-    norm_one, inv_one = layer_norm(tokens_float)
-    scale_one_own = per_token(member_own, scale_one)
-    grad_tokens = (
-        grad_resid + norm_back(grad_attn_in * (1.0 + scale_one_own), norm_one, inv_one)
-    ).astype(BF16)
-
-    part_mod = jnp.concatenate(
-        [
-            per_item(member_own, grad_attn_in),
-            per_item(member_own, grad_attn_in * norm_one),
             per_item(member_own, grad_resid * attn_out),
             per_item(member_own, grad_mlp_in),
             per_item(member_own, grad_mlp_in * norm_two),
@@ -579,25 +922,75 @@
         ],
         axis=1,
     )
-    gains = jnp.pad(gain_parts[:2].reshape(1, 2 * LANES), ((0, 0), (0, 6 * width - 2 * LANES)))
-    part_small = jnp.concatenate([part_mod, gains]).astype(BF16)
-    small = part_small.astype(F32) + swap(part_small).astype(F32)
-    small_all = lax.all_gather(small.astype(BF16), "dp", axis=0, tiled=False)
-    grad_mod_all = small_all[:, :items].reshape(dp * items, 6 * width)
-    grad_gains = jnp.sum(small_all[:, items, : 2 * LANES].astype(F32), axis=0)
+    inner = heads_out.shape[1]
+
+    if dp == 16 and owned % 8 == 0:
+        groups = 4 * width // LANES
+        early = early.reshape(items, groups, LANES)
+        early = jnp.pad(early, ((0, 0), (0, group_rows(groups) - groups), (0, 0)))
+        grad_tokens, attn_sum, grad_mod_all, gain_sums, cond_parts = tail(
+            dp,
+            d,
+            attn_in,
+            grad_attn_all,
+            heads_out,
+            w_qkv,
+            tokens,
+            grad_resid,
+            member_own,
+            scale_one,
+            early.reshape(-1, LANES).astype(BF16),
+            gain_parts,
+            mod_weight,
+        )
+        attn_sum = jnp.concatenate(list(attn_sum), axis=1)
+        cond_parts = cond_parts[:, :items, :owned]
+    else:
+
+        def attn_back(first):
+            return dot_t(lax.dynamic_slice_in_dim(d, first, half, 0), w_qkv)
+
+        attn_back_recv = swap(attn_back(other_first).astype(BF16))
+        grad_attn_in = attn_back(own_first) + attn_back_recv.astype(F32)
+        attn_sum = rest_of_halving(
+            jnp.concatenate(
+                [
+                    first_halving(halving_rows(attn_in, bits), d),
+                    first_halving(halving_rows(grad_attn_all, bits), heads_out),
+                ],
+                axis=1,
+            ),
+            bits,
+        )
+        norm_one, inv_one = layer_norm(tokens_float)
+        scale_one_own = per_token(member_own, scale_one)
+        grad_tokens = (
+            grad_resid + norm_back(grad_attn_in * (1.0 + scale_one_own), norm_one, inv_one)
+        ).astype(BF16)
+        part_mod = jnp.concatenate(
+            [per_item(member_own, grad_attn_in), per_item(member_own, grad_attn_in * norm_one), early],
+            axis=1,
+        )
+        gains = jnp.pad(gain_parts[:2].reshape(1, 2 * LANES), ((0, 0), (0, 6 * width - 2 * LANES)))
+        part_small = jnp.concatenate([part_mod, gains]).astype(BF16)
+        small = part_small.astype(F32) + swap(part_small).astype(F32)
+        small_all = lax.all_gather(small.astype(BF16), "dp", axis=0, tiled=False)
+        grad_mod_all = small_all[:, :items].reshape(dp * items, 6 * width)
+        gain_sums = jnp.sum(small_all[:, items, : 2 * LANES].astype(F32), axis=0).reshape(2, LANES)
+        cond_parts = lax.all_to_all(
+            dot_t(grad_mod_all, mod_weight).reshape(dp, items, owned),
+            "dp",
+            split_axis=0,
+            concat_axis=0,
+            tiled=True,
+        )
+
     grad_mod_weight = t_dot(mod_in_own, grad_mod_all)
-    cond_part = dot_t(grad_mod_all, mod_weight)
-    cond_parts = lax.all_to_all(
-        cond_part.reshape(dp, items, owned), "dp", split_axis=0, concat_axis=0, tiled=True
-    )
     grad_mod_in = cond_parts.transpose(1, 0, 2).reshape(items, dp * owned)
     grad_conditions = silu_grad(conditions.astype(F32)) * grad_mod_in
-
-    grad_down = rest_of_halving(down_part, bits).T
-    grad_gate = rest_of_halving(gate_part, bits)
-    grad_up = rest_of_halving(up_part, bits)
-    attn_sum = rest_of_halving(attn_parts, bits)
-    grad_q, grad_k, grad_v, grad_proj = jnp.split(attn_sum, 4, axis=1)
+    grad_q, grad_k, grad_v, grad_proj = (
+        attn_sum[:, which * inner : (which + 1) * inner] for which in range(4)
+    )
     return (
         block_out,
         grad_tokens,
@@ -607,8 +1000,8 @@
         grad_k,
         grad_v,
         grad_proj.T,
-        grad_gains[:HD],
-        grad_gains[LANES : LANES + HD],
+        gain_sums[0, :HD],
+        gain_sums[1, :HD],
         grad_gate,
         grad_up,
         grad_down,

time: 525 us -> 502 us (0.956)
  Pallas kernels: 51 us -> 134 us
  blocking collectives: 63.3 us -> 25.2 us
  matrix products: 96 us -> 72.8 us
  starting transfers between devices: 44.7 us -> 22.7 us
  other arithmetic: 76.3 us -> 59.5 us
  local copies, waits for them, and re-layouts: 69.8 us -> 58.8 us
  waiting for transfers between devices: 110 us -> 117 us
    pallas_call x0 -> x1, Pallas kernels: none -> 82.8 us  [tail(): pl.pallas_call(functools.partial(tail_kernel, dp, items, pieces), out_sha...]
    all_gather x1 -> x0, blocking collectives: 38.1 us -> none  [shards(): small_all = lax.all_gather(small.astype(BF16), 'dp', axis=0, tiled=False)]
    dot_general x13 -> x6, matrix products: 35.7 us -> 20.5 us  [dot_t(): lax.dot_general(left, right, (((1,), (1,)), ((), ())), preferred_element_...]
    ppermute x12 -> x9, starting transfers between devices: 23.7 us -> 8.98 us  [rest_of_halving(): sent = lax.ppermute(part[half:], 'dp', partners(bit))]
    ppermute x12 -> x9, waiting for transfers between devices: 59.8 us -> 74.4 us  [rest_of_halving(): sent = lax.ppermute(part[half:], 'dp', partners(bit))]
    convert_element_type x8 -> x6, other arithmetic: 9.8 us -> 0.98 us  [rest_of_halving(): part = part.astype(BF16)]
    dot_general x21 -> x13, matrix products: 57.7 us -> 49.8 us  [dot(): return jnp.dot(left, right, preferred_element_type=F32)]
    slice x12 -> x9, local copies, waits for them, and re-layouts: 8.34 us -> 1.61 us  [rest_of_halving(): sent = lax.ppermute(part[half:], 'dp', partners(bit))]
  transfers between devices with their start and end apart: 30 -> 20, of which waited for: 13 -> 11; matrix products, arithmetic and copies ran while one was open for 35% -> 27% of each run, Pallas kernels for 10% -> 5%
where the time goes in v2:
time: 502 us; the launch traced here: 494 us
  Pallas kernels  134 us (27%)
  waiting for transfers between devices  117 us (23%)
  matrix products  72.8 us (15%)
  other arithmetic  59.5 us (12%)
  local copies, waits for them, and re-layouts  58.8 us (12%)
  blocking collectives  25.2 us (5%)
  starting transfers between devices  22.7 us (5%)
    pallas_call x1, Pallas kernels, tail(): pl.pallas_call(functools.partial(tail_kernel, dp, items, pieces), out_sha...  82.8 us
    ppermute x9, waiting for transfers between devices, rest_of_halving(): sent = lax.ppermute(part[half:], 'dp', partners(bit))  74.4 us
    dot_general x13, matrix products, dot(): return jnp.dot(left, right, preferred_element_type=F32)  49.8 us
    ppermute x7, waiting for transfers between devices, swap(): return lax.ppermute(values, 'tensor', [(0, 1), (1, 0)])  42.1 us
    pallas_call x1, Pallas kernels, attend_back(): pl.pallas_call(functools.partial(attend_back_kernel, heads, items), grid_...  25.9 us
    pallas_call x1, Pallas kernels, attend(): pl.pallas_call(functools.partial(attend_kernel, heads, items), grid_spec=...  25.4 us
    all_gather x1, blocking collectives, shards(): cond_all = lax.all_gather(conditions, 'dp', axis=0, tiled=True)  25.2 us
    dot_general x6, matrix products, dot_t(): lax.dot_general(left, right, (((1,), (1,)), ((), ())), preferred_element_...  20.5 us
  transfers between devices with their start and end apart: 20, of which 11 were waited for; matrix products, arithmetic and copies ran while one was open for 27% of the time, Pallas kernels for 5%

profile of v2, /device:TPU:0, one launch (start us, length us, event | category | flops | bytes accessed | tf_op | source)
XLA Modules:
  0.0 493.8 jit_solution(16772763869923489644)
XLA Ops:
  0.7 25.2 %all-gather = bf16[16,3,1152]{2,1,0:T(4,128)(2,1)} all-gather(bf16[1,3,1152]{2,1,0:T(4,128)(2,1)} %bitcast.82), channel_id=1, replica_groups=mesh['dp'=16,'tensor'=2] {'dp'}, dimensions={0}, use_global_device_ids=true | all-gather | bytes 117504 | tf_op jit(solution)/shard_map/all_gather | solution.py:837
  25.9 1.7 reshape.221
  27.6 2.7 fusion.52
  30.3 2.6 reshape.214
  32.9 4.5 all-to-all-start
  37.4 1.6 collective-permute-start.4
  45.9 1.7 convert_element_type.190
  47.6 2.6 copy.43
  50.1 2.6 copy.44
  52.7 2.6 copy.45
  55.4 7.9 %concatenate.27.w_ref = bf16[1152,1728]{1,0:T(8,128)(2,1)} concatenate(bf16[1152,576]{1,0:T(8,128)(2,1)} %copy.43, bf16[1152,576]{1,0:T(8,128)(2,1)} %copy.44, bf16[1152,576]{1,0:T(8,128)(2,1)} %copy.45), dimensions={1} | concatenate | bytes 7962624 | tf_op jit(solution)/shard_map/concatenate | solution.py:856
  65.8 2.7 add_select_fusion
  68.5 2.7 slice_reduce_fusion.2
  71.2 3.4 sine_select_fusion
  74.5 4.0 collective-permute-done
  82.3 2.4 reduce_sum.171
  84.7 1.8 slice_reduce_fusion.11
  86.5 10.4 %fusion.6.x_ref.attn_in_ref = bf16[768,1152]{1,0:T(8,128)(2,1)} fusion(f32[1152]{0:T(1024)S(1)} %get-tuple-element.81, f32[1152]{0:T(1024)S(1)} %get-tuple-element.82, f32[1152]{0:T(1024)S(1)} %get-tuple-element.83, f32[1152]{0:T(1024)S(1)} %get-tuple-element.84, f32[768]{0:T(1024)} %get-tuple-element.70, f32[1152]{0:T(1024)S(1)} %get-tuple-element.85, ...), kind=kLoop, calls=%fused_computation.12 | loop fusion | flops 17694720 | bytes 3581952 | tf_op jit(solution)/shard_map/convert_element_type | solution.py:854
  96.9 25.4 %attend.1 = (bf16[768,576]{1,0:T(8,128)(2,1)}, f32[8,768,128]{2,1,0:T(8,128)}, f32[8,768,128]{2,1,0:T(8,128)}, bf16[8,768,128]{2,1,0:T(8,128)(2,1)}, bf16[8,768,...) custom-call(s32[2,3]{1,0:T(2,128)} %pad_add_fusion.1.spans, ...), custom_call_target="tpu_custom_call" | custom-call | flops 3862953984 | bytes 25165824 | tf_op jit(solution)/shard_map/attend/pallas_call | solution.py:264
  122.3 2.9 convolution_convert_fusion.4
  125.2 1.5 collective-permute-start.1
  126.7 2.1 dynamic-slice_reduce_fusion.2
  128.8 1.6 constant_dynamic-slice_fusion.member_ref
  131.8 14.7 %collective-permute-done.1 = bf16[384,1152]{1,0:T(8,128)(2,1)} collective-permute-done((bf16[384,1152]{1,0:T(8,128)(2,1)}, bf16[384,1152]{1,0:T(8,128)(2,1)}, u32[]{:S(2)}, u32[]{:S(2)}) %collective-permute-start.1) | collective-permute-done | bytes 884768 | tf_op jit(solution)/shard_map/ppermute | solution.py:386
  146.4 5.5 %fusion.8 = (bf16[384,1152]{1,0:T(8,128)(2,1)S(1)}, bf16[384,1152]{1,0:T(8,128)(2,1)S(1)}, f32[384]{0:T(512)S(1)}, f32[384,1152]{1,0:T(8,128)S(1)}, f32[384,1152]{1,0:T(8,128)}) fusion(bf16[384,1152]{1,0:T(8,128)(2,1)} %param.27, f32[1152]{0:T(1024)} %get-tuple-element.79, f32[1152]{0:T(1024)} %get-tuple-element.80, f32[1152]{0:T(1024)} %get-tuple-element.72, ...), kind=kOutput, calls=%fused_computation.35 | convolution fusion | flops 521551488 | bytes 10725892 | tf_op jit(solution)/shard_map/dot_general | solution.py:27
  152.9 4.8 add_convert_fusion.7
  160.5 3.9 copy.47
  164.4 2.4 reverse_select_fusion.7
  169.0 9.1 %collective-permute-done.2 = bf16[384,1152]{1,0:T(8,128)(2,1)} collective-permute-done((bf16[384,1152]{1,0:T(8,128)(2,1)}, bf16[384,1152]{1,0:T(8,128)(2,1)}, u32[]{:S(2)}, u32[]{:S(2)}) %collective-permute-start.2) | collective-permute-done | bytes 884768 | tf_op jit(solution)/shard_map/ppermute | solution.py:386
  178.1 6.3 %fusion.29 = f32[768,1536]{1,0:T(8,128)} fusion(bf16[1152,1536]{1,0:T(8,128)(2,1)S(1)} %copy-done.47, bf16[384,1152]{1,0:T(8,128)(2,1)} %collective-permute-done.2, bf16[384,1152]{1,0:T(8,128)(2,1)} %add_convert_fusion.7), kind=kOutput, calls=%fused_computation.95 | convolution fusion | flops 2721447936 | bytes 10027008 | tf_op jit(solution)/shard_map/dot_general | solution.py:27
  184.4 6.6 %fusion.28 = f32[768,1536]{1,0:T(8,128)} fusion(bf16[1152,1536]{1,0:T(8,128)(2,1)S(1)} %copy-done.49, bf16[384,1152]{1,0:T(8,128)(2,1)} %collective-permute-done.2, bf16[384,1152]{1,0:T(8,128)(2,1)} %add_convert_fusion.7), kind=kOutput, calls=%fused_computation.94 | convolution fusion | flops 2721447936 | bytes 10027008 | tf_op jit(solution)/shard_map/dot_general | solution.py:27
  190.9 8.0 %multiply_convert_fusion = (bf16[768,1536]{1,0:T(8,128)(2,1)S(1)}, bf16[768,1536]{1,0:T(8,128)(2,1)S(1)}, bf16[768,1536]{1,0:T(8,128)(2,1)S(1)}) fusion(f32[768,1536]{1,0:T(8,128)} %fusion.29, f32[768,1536]{1,0:T(8,128)} %fusion.28, bf16[1536,1152]{1,0:T(8,128)(2,1)S(1)} %copy-done, bf16[384,1152]{1,0:T(8,128)(2,1)S(1)} %copy-done.14, ...), kind=kOutput, calls=%fused_computation | convolution fusion | flops 2739142656 | bytes 21823488 | tf_op jit(solution)/shard_map/dot_general | solution.py:31
  199.0 1.7 fusion.14
  201.1 2.6 fusion.7
  205.2 2.6 convolution_convert_fusion.3
  208.4 2.8 convolution_convert_fusion.2
  211.2 2.9 fusion.27
  214.1 4.3 copy.50
  218.4 2.5 reverse_select_fusion.3
  223.5 2.8 convolution_convert_fusion.1
  227.7 1.7 fusion.19
  229.5 1.7 fusion.22
  232.8 3.7 fusion.54
  236.6 2.5 fusion.12
  239.1 3.0 collective-permute-done.3
  242.2 4.6 multiply_reduce_fusion.5
  246.8 1.5 collective-permute-start.6
  248.4 2.7 convolution_convert_fusion
  254.7 11.3 %collective-permute-done.6 = bf16[384,1152]{1,0:T(8,128)(2,1)} collective-permute-done((bf16[384,1152]{1,0:T(8,128)(2,1)}, bf16[384,1152]{1,0:T(8,128)(2,1)}, u32[]{:S(2)}, u32[]{:S(2)}) %collective-permute-start.6) | collective-permute-done | bytes 884768 | tf_op jit(solution)/shard_map/ppermute | solution.py:386
  266.1 1.6 broadcast_select_fusion.1
  269.6 2.7 convolution_convert_fusion.5.grad_ref
  272.3 4.4 add_convert_fusion.1
  276.7 4.4 add_convert_fusion
  281.1 4.3 add_convert_fusion.2
  285.5 25.9 %attend_back.1 = (bf16[768,1728]{1,0:T(8,128)(2,1)}, f32[8,128]{1,0:T(8,128)}) custom-call(s32[2,3]{1,0:T(2,128)} %pad_add_fusion.1.spans, bf16[768,576]{1,0:T(8,128)(2,1)} %convolution_convert_fusion.5.grad_ref, f32[8,768,128]{2,1,0:T(8,128)} %get-tuple-element.33.qpre_ref, f32[8,768,128]{2,1,0:T(8,128)} %get-tuple-element.34.kpre_ref, ...), custom_call_target="tpu_custom_call" | custom-call | flops 1610612736 | bytes 25165824 | tf_op jit(solution)/shard_map/attend_back/pallas_call | solution.py:317
  311.4 82.8 %tail.1 = (bf16[384,1152]{1,0:T(8,128)(2,1)}, f32[3,72,768]{2,1,0:T(8,128)}, bf16[48,6912]{1,0:T(8,128)(2,1)}, f32[8,128]{1,0:T(8,128)}, f32[16,8,128]{2,1,0:T(8,128)}) custom-call(bf16[768,1728]{1,0:T(8,128)(2,1)} %get-tuple-element.39.d_ref, bf16[768,1152]{1,0:T(8,128)(2,1)} %fusion.6.x_ref.attn_in_ref, bf16[768,1152]{1,0:T(8,128)(2,1)} %pad_maximum_fusion.3.grad_attn_ref, ...), custom_call_target="tpu_custom_call" | custom-call | flops 8153726976 | bytes 20971520 | tf_op jit(solution)/shard_map/tail/pallas_call | solution.py:737
  405.7 2.6 fusion.53
  408.3 14.0 %collective-permute-done.10 = bf16[288,1536]{1,0:T(8,128)(2,1)S(1)} collective-permute-done((bf16[288,1536]{1,0:T(8,128)(2,1)S(1)}, bf16[288,1536]{1,0:T(8,128)(2,1)S(1)}, u32[]{:S(2)}, u32[]{:S(2)}) %collective-permute-start.10) | collective-permute-done | bytes 884768 | tf_op jit(solution)/shard_map/ppermute | solution.py:418
  423.4 17.9 %collective-permute-done.13 = bf16[288,1536]{1,0:T(8,128)(2,1)S(1)} collective-permute-done((bf16[288,1536]{1,0:T(8,128)(2,1)S(1)}, bf16[288,1536]{1,0:T(8,128)(2,1)S(1)}, u32[]{:S(2)}, u32[]{:S(2)}) %collective-permute-start.13) | collective-permute-done | bytes 884768 | tf_op jit(solution)/shard_map/ppermute | solution.py:418
  442.3 17.1 %collective-permute-done.16 = bf16[288,1536]{1,0:T(8,128)(2,1)S(1)} collective-permute-done((bf16[288,1536]{1,0:T(8,128)(2,1)S(1)}, bf16[288,1536]{1,0:T(8,128)(2,1)S(1)}, u32[]{:S(2)}, u32[]{:S(2)}) %collective-permute-start.16) | collective-permute-done | bytes 884768 | tf_op jit(solution)/shard_map/ppermute | solution.py:418
  460.6 1.9 collective-permute-start.12
  463.8 15.6 %collective-permute-done.17 = bf16[144,1536]{1,0:T(8,128)(2,1)S(1)} collective-permute-done((bf16[144,1536]{1,0:T(8,128)(2,1)S(1)}, bf16[144,1536]{1,0:T(8,128)(2,1)S(1)}, u32[]{:S(2)}, u32[]{:S(2)}) %collective-permute-start.17) | collective-permute-done | bytes 442400 | tf_op jit(solution)/shard_map/ppermute | solution.py:418
  481.0 6.4 %collective-permute-done.15 = bf16[72,1536]{1,0:T(8,128)(2,1)S(1)} collective-permute-done((bf16[72,1536]{1,0:T(8,128)(2,1)S(1)}, bf16[72,1536]{1,0:T(8,128)(2,1)S(1)}, u32[]{:S(2)}, u32[]{:S(2)}) %collective-permute-start.15) | collective-permute-done | bytes 221216 | tf_op jit(solution)/shard_map/ppermute | solution.py:418
  488.3 3.4 collective-permute-done.18
  (227 shorter events, 52.0 us)
Async XLA Ops:
  0.6 190.3 %copy-start = (bf16[1536,1152]{1,0:T(8,128)(2,1)S(1)}, bf16[1536,1152]{1,0:T(8,128)(2,1)}, u32[]{:S(2)}) copy-start(bf16[1536,1152]{1,0:T(8,128)(2,1)} %param.26) | copy-start | bytes 10616836
  32.9 6.6 %copy-start.44 = (s32[3,2]{0,1:T(2,128)S(1)}, s32[3,2]{0,1:T(2,128)}, u32[]{:S(2)}) copy-start(s32[3,2]{0,1:T(2,128)} %param.16) | copy-start | bytes 76
  32.9 49.4 %all-to-all-start = ((f32[16,3,6912]{2,1,0:T(4,128)}), f32[16,3,6912]{2,1,0:T(4,128)}, u32[]{:S(2)}, u32[]{:S(2)}) async-start(f32[16,3,6912]{2,1,0:T(4,128)} %reshape.214), calls=%async_computation | async-start | bytes 3538944 | tf_op jit(solution)/shard_map/all_to_all | solution.py:841
  37.4 94.3 %collective-permute-start.4 = (bf16[384,1152]{1,0:T(8,128)(2,1)}, bf16[384,1152]{1,0:T(8,128)(2,1)}, u32[]{:S(2)}, u32[]{:S(2)}) collective-permute-start(bf16[384,1152]{1,0:T(8,128)(2,1)} %param.27), channel_id=1, source_target_pairs={{0,1},{1,0},{2,3},{3,2},{4,5},{5,4},{6,7},{7,6},{8,9},{9,8},{10,11... | collective-permute-start | bytes 2654216 | tf_op jit(solution)/shard_map/ppermute | solution.py:386
  39.0 39.5 %collective-permute-start = (bf16[384,1152]{1,0:T(8,128)(2,1)}, bf16[384,1152]{1,0:T(8,128)(2,1)}, u32[]{:S(2)}, u32[]{:S(2)}) collective-permute-start(bf16[384,1152]{1,0:T(8,128)(2,1)} %tokens_ref.1), channel_id=1, source_target_pairs={{0,1},{1,0},{2,3},{3,2},{4,5},{5,4},{6,7},{7,6},{8,9},{9,8},{10,11... | collective-permute-start | bytes 2654216 | tf_op jit(solution)/shard_map/ppermute | solution.py:386
  55.4 9.2 %copy-start.45 = (f32[72]{0:T(128)S(1)}, f32[72]{0:T(128)}, u32[]{:S(2)}) copy-start(f32[72]{0:T(128)} %param.23) | copy-start | bytes 868
  55.4 9.2 %copy-start.46 = (f32[72]{0:T(128)S(1)}, f32[72]{0:T(128)}, u32[]{:S(2)}) copy-start(f32[72]{0:T(128)} %param.22) | copy-start | bytes 868
  63.3 15.3 %copy-start.18 = (bf16[384,1152]{1,0:T(8,128)(2,1)S(1)}, bf16[384,1152]{1,0:T(8,128)(2,1)}, u32[]{:S(2)}) copy-start(bf16[384,1152]{1,0:T(8,128)(2,1)} %tokens_ref.1) | copy-start | bytes 2654212
  96.9 25.4 %copy-start.51 = (bf16[576,1152]{1,0:T(8,128)(2,1)S(1)}, bf16[576,1152]{1,0:T(8,128)(2,1)}, u32[]{:S(2)}) copy-start(bf16[576,1152]{1,0:T(8,128)(2,1)} %param.21) | copy-start | bytes 3981316
  125.2 21.3 %collective-permute-start.1 = (bf16[384,1152]{1,0:T(8,128)(2,1)}, bf16[384,1152]{1,0:T(8,128)(2,1)}, u32[]{:S(2)}, u32[]{:S(2)}) collective-permute-start(bf16[384,1152]{1,0:T(8,128)(2,1)} %convolution_convert_fusion.4), channel_id=1, source_target_pairs={{0,1},{1,0},{2,3},{3,2},{4,5},{5,4},{6,7},{7,6},{8,9},{9,8},{10,11... | collective-permute-start | bytes 2654216 | tf_op jit(solution)/shard_map/ppermute | solution.py:386
  128.8 23.6 %copy-start.25 = (f32[384]{0:T(512)}, f32[384]{0:T(512)S(1)}, u32[]{:S(2)}) copy-start(f32[384]{0:T(512)S(1)} %get-tuple-element.65) | copy-start | bytes 4612
  128.8 23.6 %copy-start.27 = (f32[384]{0:T(512)}, f32[384]{0:T(512)S(1)}, u32[]{:S(2)}) copy-start(f32[384]{0:T(512)S(1)} %get-tuple-element.66) | copy-start | bytes 4612
  128.8 23.6 %copy-start.29 = (f32[384]{0:T(512)}, f32[384]{0:T(512)S(1)}, u32[]{:S(2)}) copy-start(f32[384]{0:T(512)S(1)} %get-tuple-element.67) | copy-start | bytes 4612
  152.0 5.7 %copy-start.1 = (f32[384,1152]{1,0:T(8,128)}, f32[384,1152]{1,0:T(8,128)S(1)}, u32[]{:S(2)}) copy-start(f32[384,1152]{1,0:T(8,128)S(1)} %get-tuple-element.126) | copy-start | bytes 5308420
  152.0 7.2 %copy-start.11 = (bf16[384,1152]{1,0:T(8,128)(2,1)}, bf16[384,1152]{1,0:T(8,128)(2,1)S(1)}, u32[]{:S(2)}) copy-start(bf16[384,1152]{1,0:T(8,128)(2,1)S(1)} %get-tuple-element.120) | copy-start | bytes 2654212
  152.0 7.2 %copy-start.13 = (bf16[384,1152]{1,0:T(8,128)(2,1)}, bf16[384,1152]{1,0:T(8,128)(2,1)S(1)}, u32[]{:S(2)}) copy-start(bf16[384,1152]{1,0:T(8,128)(2,1)S(1)} %get-tuple-element.121) | copy-start | bytes 2654212
  152.0 5.6 %copy-start.31 = (f32[384]{0:T(512)}, f32[384]{0:T(512)S(1)}, u32[]{:S(2)}) copy-start(f32[384]{0:T(512)S(1)} %broadcast_multiply_fusion.3) | copy-start | bytes 4612
  152.4 6.8 %copy-start.42 = (f32[384]{0:T(512)}, f32[384]{0:T(512)S(1)}, u32[]{:S(2)}) copy-start(f32[384]{0:T(512)S(1)} %add_rsqrt_fusion.1) | copy-start | bytes 4612
  157.7 20.4 %collective-permute-start.2 = (bf16[384,1152]{1,0:T(8,128)(2,1)}, bf16[384,1152]{1,0:T(8,128)(2,1)}, u32[]{:S(2)}, u32[]{:S(2)}) collective-permute-start(bf16[384,1152]{1,0:T(8,128)(2,1)} %add_convert_fusion.7), channel_id=1, source_target_pairs={{0,1},{1,0},{2,3},{3,2},{4,5},{5,4},{6,7},{7,6},{8,9},{9,8},{10,11... | collective-permute-start | bytes 2654216 | tf_op jit(solution)/shard_map/ppermute | solution.py:386
  167.9 10.1 %copy-start.47 = (bf16[1152,1536]{1,0:T(8,128)(2,1)S(1)}, bf16[1152,1536]{1,0:T(8,128)(2,1)}, u32[]{:S(2)}) copy-start(bf16[1152,1536]{1,0:T(8,128)(2,1)} %param.24) | copy-start | bytes 10616836
  169.0 15.4 %copy-start.49 = (bf16[1152,1536]{1,0:T(8,128)(2,1)S(1)}, bf16[1152,1536]{1,0:T(8,128)(2,1)}, u32[]{:S(2)}) copy-start(bf16[1152,1536]{1,0:T(8,128)(2,1)} %param.25) | copy-start | bytes 10616836
  184.4 6.6 %copy-start.12 = (bf16[384,1152]{1,0:T(8,128)(2,1)S(1)}, bf16[384,1152]{1,0:T(8,128)(2,1)}, u32[]{:S(2)}) copy-start(bf16[384,1152]{1,0:T(8,128)(2,1)} %copy-done.11) | copy-start | bytes 2654212
  184.4 6.6 %copy-start.14 = (bf16[384,1152]{1,0:T(8,128)(2,1)S(1)}, bf16[384,1152]{1,0:T(8,128)(2,1)}, u32[]{:S(2)}) copy-start(bf16[384,1152]{1,0:T(8,128)(2,1)} %copy-done.13) | copy-start | bytes 2654212
  199.0 2.1 copy-start.56
  199.0 9.4 %copy-start.53 = (bf16[768,1536]{1,0:T(8,128)(2,1)}, bf16[768,1536]{1,0:T(8,128)(2,1)S(1)}, u32[]{:S(2)}) copy-start(bf16[768,1536]{1,0:T(8,128)(2,1)S(1)} %get-tuple-element.102) | copy-start | bytes 7077892
  203.7 27.5 %collective-permute-start.5 = (bf16[384,1152]{1,0:T(8,128)(2,1)}, bf16[384,1152]{1,0:T(8,128)(2,1)}, u32[]{:S(2)}, u32[]{:S(2)}) collective-permute-start(bf16[384,1152]{1,0:T(8,128)(2,1)} %fusion.7), channel_id=1, source_target_pairs={{0,1},{1,0},{2,3},{3,2},{4,5},{5,4},{6,7},{7,6},{8,9},{9,8},{10,11... | collective-permute-start | bytes 2654216 | tf_op jit(solution)/shard_map/ppermute | solution.py:386
  207.8 34.3 %collective-permute-start.3 = (bf16[384,1152]{1,0:T(8,128)(2,1)}, bf16[384,1152]{1,0:T(8,128)(2,1)}, u32[]{:S(2)}, u32[]{:S(2)}) collective-permute-start(bf16[384,1152]{1,0:T(8,128)(2,1)} %convolution_convert_fusion.3), channel_id=1, source_target_pairs={{0,1},{1,0},{2,3},{3,2},{4,5},{5,4},{6,7},{7,6},{8,9},{9,8},{10,11... | collective-permute-start | bytes 2654216 | tf_op jit(solution)/shard_map/ppermute | solution.py:386
  211.2 69.9 %collective-permute-start.7 = (bf16[576,1536]{1,0:T(8,128)(2,1)}, bf16[576,1536]{1,0:T(8,128)(2,1)}, u32[]{:S(2)}, u32[]{:S(2)}) collective-permute-start(bf16[576,1536]{1,0:T(8,128)(2,1)} %convolution_convert_fusion.2), channel_id=1, source_target_pairs={{0,2},{2,0},{4,6},{6,4},{8,10},{10,8},{12,14},{14,12},{16,18},{18,... | collective-permute-start | bytes 5308424 | tf_op jit(solution)/shard_map/ppermute | solution.py:407
  223.5 4.3 copy-start.48
  226.2 46.1 %collective-permute-start.8 = (bf16[576,1536]{1,0:T(8,128)(2,1)}, bf16[576,1536]{1,0:T(8,128)(2,1)}, u32[]{:S(2)}, u32[]{:S(2)}) collective-permute-start(bf16[576,1536]{1,0:T(8,128)(2,1)} %convolution_convert_fusion.1), channel_id=1, source_target_pairs={{0,2},{2,0},{4,6},{6,4},{8,10},{10,8},{12,14},{14,12},{16,18},{18,... | collective-permute-start | bytes 5308424 | tf_op jit(solution)/shard_map/ppermute | solution.py:407
  229.5 2.5 copy-start.50
  229.5 3.3 copy-start.57
  231.3 5.3 %copy-start.6 = (bf16[384,1152]{1,0:T(8,128)(2,1)S(1)}, bf16[384,1152]{1,0:T(8,128)(2,1)}, u32[]{:S(2)}) copy-start(bf16[384,1152]{1,0:T(8,128)(2,1)} %param.27) | copy-start | bytes 2654212
  231.3 5.3 %copy-start.7 = (f32[384,1152]{1,0:T(8,128)S(1)}, f32[384,1152]{1,0:T(8,128)}, u32[]{:S(2)}) copy-start(f32[384,1152]{1,0:T(8,128)} %get-tuple-element.135) | copy-start | bytes 5308420
  236.6 5.6 %copy-start.36 = (f32[1152]{0:T(1024)S(1)}, f32[1152]{0:T(1024)}, u32[]{:S(2)}) copy-start(f32[1152]{0:T(1024)} %get-tuple-element.72) | copy-start | bytes 13828
  236.6 5.6 %copy-start.37 = (f32[1152]{0:T(1024)S(1)}, f32[1152]{0:T(1024)}, u32[]{:S(2)}) copy-start(f32[1152]{0:T(1024)} %get-tuple-element.79) | copy-start | bytes 13828
  236.6 5.6 %copy-start.38 = (f32[1152]{0:T(1024)S(1)}, f32[1152]{0:T(1024)}, u32[]{:S(2)}) copy-start(f32[1152]{0:T(1024)} %get-tuple-element.80) | copy-start | bytes 13828
  236.6 5.6 %copy-start.39 = (f32[1152]{0:T(1024)S(1)}, f32[1152]{0:T(1024)}, u32[]{:S(2)}) copy-start(f32[1152]{0:T(1024)} %get-tuple-element.87) | copy-start | bytes 13828
  236.6 5.6 %copy-start.40 = (f32[1152]{0:T(1024)S(1)}, f32[1152]{0:T(1024)}, u32[]{:S(2)}) copy-start(f32[1152]{0:T(1024)} %get-tuple-element.88) | copy-start | bytes 13828
  236.6 5.6 %copy-start.41 = (f32[1152]{0:T(1024)S(1)}, f32[1152]{0:T(1024)}, u32[]{:S(2)}) copy-start(f32[1152]{0:T(1024)} %get-tuple-element.89) | copy-start | bytes 13828
  239.1 7.7 %copy-start.5 = (f32[384,1152]{1,0:T(8,128)}, f32[384,1152]{1,0:T(8,128)S(1)}, u32[]{:S(2)}) copy-start(f32[384,1152]{1,0:T(8,128)S(1)} %get-tuple-element.97.resid_ref) | copy-start | bytes 5308420
  246.8 19.3 %collective-permute-start.6 = (bf16[384,1152]{1,0:T(8,128)(2,1)}, bf16[384,1152]{1,0:T(8,128)(2,1)}, u32[]{:S(2)}, u32[]{:S(2)}) collective-permute-start(bf16[384,1152]{1,0:T(8,128)(2,1)} %get-tuple-element.124), channel_id=1, source_target_pairs={{0,1},{1,0},{2,3},{3,2},{4,5},{5,4},{6,7},{7,6},{8,9},{9,8},{10,11... | collective-permute-start | bytes 2654216 | tf_op jit(solution)/shard_map/ppermute | solution.py:386
  251.1 25.6 %collective-permute-start.9 = (bf16[576,1536]{1,0:T(8,128)(2,1)}, bf16[576,1536]{1,0:T(8,128)(2,1)}, u32[]{:S(2)}, u32[]{:S(2)}) collective-permute-start(bf16[576,1536]{1,0:T(8,128)(2,1)} %convolution_convert_fusion), channel_id=1, source_target_pairs={{0,2},{2,0},{4,6},{6,4},{8,10},{10,8},{12,14},{14,12},{16,18},{18,... | collective-permute-start | bytes 5308424 | tf_op jit(solution)/shard_map/ppermute | solution.py:407
  269.6 2.7 copy-start.17
  269.6 2.7 copy-start.61
  272.3 4.4 copy-start.58
  276.7 4.4 copy-start.15
  276.7 4.4 copy-start.55
  397.0 3.4 copy-start.9
  398.4 3.6 copy-start.8
  399.7 22.6 %collective-permute-start.10 = (bf16[288,1536]{1,0:T(8,128)(2,1)S(1)}, bf16[288,1536]{1,0:T(8,128)(2,1)S(1)}, u32[]{:S(2)}, u32[]{:S(2)}) collective-permute-start(bf16[288,1536]{1,0:T(8,128)(2,1)S(1)} %slice.343), channel_id=1, source_target_pairs={{0,4},{2,6},{4,0},{6,2},{8,12},{10,14},{12,8},{14,10},{16,20},{18,... | collective-permute-start | bytes 2654216 | tf_op jit(solution)/shard_map/ppermute | solution.py:418
  400.5 3.2 copy-start.22
  400.5 3.2 copy-start.23
  400.6 5.1 %copy-start.19 = (bf16[48,6912]{1,0:T(8,128)(2,1)S(1)}, bf16[48,6912]{1,0:T(8,128)(2,1)}, u32[]{:S(2)}) copy-start(bf16[48,6912]{1,0:T(8,128)(2,1)} %get-tuple-element.43) | copy-start | bytes 1990660
  400.6 40.7 %collective-permute-start.13 = (bf16[288,1536]{1,0:T(8,128)(2,1)S(1)}, bf16[288,1536]{1,0:T(8,128)(2,1)S(1)}, u32[]{:S(2)}, u32[]{:S(2)}) collective-permute-start(bf16[288,1536]{1,0:T(8,128)(2,1)S(1)} %slice.349), channel_id=1, source_target_pairs={{0,4},{2,6},{4,0},{6,2},{8,12},{10,14},{12,8},{14,10},{16,20},{18,... | collective-permute-start | bytes 2654216 | tf_op jit(solution)/shard_map/ppermute | solution.py:418
  402.1 57.3 %collective-permute-start.16 = (bf16[288,1536]{1,0:T(8,128)(2,1)S(1)}, bf16[288,1536]{1,0:T(8,128)(2,1)S(1)}, u32[]{:S(2)}, u32[]{:S(2)}) collective-permute-start(bf16[288,1536]{1,0:T(8,128)(2,1)S(1)} %slice.355), channel_id=1, source_target_pairs={{0,4},{2,6},{4,0},{6,2},{8,12},{10,14},{12,8},{14,10},{16,20},{18,... | collective-permute-start | bytes 2654216 | tf_op jit(solution)/shard_map/ppermute | solution.py:418
  403.8 18.6 %copy-start.10 = (bf16[576,1536]{1,0:T(8,128)(2,1)S(1)}, bf16[576,1536]{1,0:T(8,128)(2,1)}, u32[]{:S(2)}) copy-start(bf16[576,1536]{1,0:T(8,128)(2,1)} %add_convert_fusion.1) | copy-start | bytes 5308420
  422.6 37.9 %collective-permute-start.11 = (bf16[144,1536]{1,0:T(8,128)(2,1)S(1)}, bf16[144,1536]{1,0:T(8,128)(2,1)S(1)}, u32[]{:S(2)}, u32[]{:S(2)}) collective-permute-start(bf16[144,1536]{1,0:T(8,128)(2,1)S(1)} %slice.394), channel_id=1, source_target_pairs={{0,8},{2,10},{4,12},{6,14},{8,0},{10,2},{12,4},{14,6},{16,24},{18,... | collective-permute-start | bytes 1327112 | tf_op jit(solution)/shard_map/ppermute | solution.py:418
  441.5 20.9 %collective-permute-start.14 = (bf16[144,1536]{1,0:T(8,128)(2,1)S(1)}, bf16[144,1536]{1,0:T(8,128)(2,1)S(1)}, u32[]{:S(2)}, u32[]{:S(2)}) collective-permute-start(bf16[144,1536]{1,0:T(8,128)(2,1)S(1)} %slice.398), channel_id=1, source_target_pairs={{0,8},{2,10},{4,12},{6,14},{8,0},{10,2},{12,4},{14,6},{16,24},{18,... | collective-permute-start | bytes 1327112 | tf_op jit(solution)/shard_map/ppermute | solution.py:418
  459.7 19.7 %collective-permute-start.17 = (bf16[144,1536]{1,0:T(8,128)(2,1)S(1)}, bf16[144,1536]{1,0:T(8,128)(2,1)S(1)}, u32[]{:S(2)}, u32[]{:S(2)}) collective-permute-start(bf16[144,1536]{1,0:T(8,128)(2,1)S(1)} %slice.402), channel_id=1, source_target_pairs={{0,8},{2,10},{4,12},{6,14},{8,0},{10,2},{12,4},{14,6},{16,24},{18,... | collective-permute-start | bytes 1327112 | tf_op jit(solution)/shard_map/ppermute | solution.py:418
  460.6 19.6 %collective-permute-start.12 = (bf16[72,1536]{1,0:T(8,128)(2,1)S(1)}, bf16[72,1536]{1,0:T(8,128)(2,1)S(1)}, u32[]{:S(2)}, u32[]{:S(2)}) collective-permute-start(bf16[72,1536]{1,0:T(8,128)(2,1)S(1)} %slice.396), channel_id=1, source_target_pairs={{0,16},{2,18},{4,20},{6,22},{8,24},{10,26},{12,28},{14,30},{16,0},... | collective-permute-start | bytes 663560 | tf_op jit(solution)/shard_map/ppermute | solution.py:418
  462.6 24.9 %collective-permute-start.15 = (bf16[72,1536]{1,0:T(8,128)(2,1)S(1)}, bf16[72,1536]{1,0:T(8,128)(2,1)S(1)}, u32[]{:S(2)}, u32[]{:S(2)}) collective-permute-start(bf16[72,1536]{1,0:T(8,128)(2,1)S(1)} %slice.400), channel_id=1, source_target_pairs={{0,16},{2,18},{4,20},{6,22},{8,24},{10,26},{12,28},{14,30},{16,0},... | collective-permute-start | bytes 663560 | tf_op jit(solution)/shard_map/ppermute | solution.py:418
  479.5 12.9 %copy-start.16 = (bf16[384,1152]{1,0:T(8,128)(2,1)S(1)}, bf16[384,1152]{1,0:T(8,128)(2,1)}, u32[]{:S(2)}) copy-start(bf16[384,1152]{1,0:T(8,128)(2,1)} %get-tuple-element.159) | copy-start | bytes 2654212
  479.6 12.1 %collective-permute-start.18 = (bf16[72,1536]{1,0:T(8,128)(2,1)S(1)}, bf16[72,1536]{1,0:T(8,128)(2,1)S(1)}, u32[]{:S(2)}, u32[]{:S(2)}) collective-permute-start(bf16[72,1536]{1,0:T(8,128)(2,1)S(1)} %slice.404), channel_id=1, source_target_pairs={{0,16},{2,18},{4,20},{6,22},{8,24},{10,26},{12,28},{14,30},{16,0},... | collective-permute-start | bytes 663560 | tf_op jit(solution)/shard_map/ppermute | solution.py:418
  (18 other events, 27.7 us)

commit v3 on v2

--- a/solution.py
+++ b/solution.py
@@ -475,6 +475,8 @@
     early_ref,
     gain_ref,
     mod_ref,
+    paired_ref,
+    crossed_ref,
     grad_tokens_ref,
     sums_ref,
     all_ref,
@@ -557,6 +559,26 @@
     early_copy = y_copy(0, early_ref, early_in)
     early_copy.start()
 
+    paired = paired_ref.shape[0]
+    crossed = crossed_ref.shape[0]
+    last_copies = {}
+
+    def last_level(p, total):
+        w_out[p, depth:, :] = jnp.zeros((w_out.shape[1] - depth, piece), BF16)
+        w_out[p, :depth, :] = total[depth:].astype(BF16)
+        last_copies[p] = halving(3, p, w_out.at[p], w_in.at[p])
+        last_copies[p].start()
+        sums_ref[p] = total[:depth]
+
+    for p in range(crossed):
+        last_level(pieces + paired + p, crossed_ref[p].astype(F32))
+    paired_copies = []
+    for p in range(paired):
+        paired_copies.append(
+            halving(2, pieces + p, paired_ref.at[p, pl.ds(2 * depth, 2 * depth), :], z_in.at[pieces + p])
+        )
+        paired_copies[p].start()
+
     other_rows = pl.ds(pl.multiple_of((1 - ten) * half, half), half)
     own_rows = pl.ds(pl.multiple_of(ten * half, half), half)
     y_out[...] = dot_t(d_ref[other_rows, :], w_ref[...]).astype(BF16)
@@ -611,6 +633,13 @@
         return sent
 
     x_copies = level(1, core_copies, core_keep, core_in, x_out, x_in, x_keep)
+
+    for p in range(paired):
+        paired_copies[p].wait_recv()
+        last_level(
+            pieces + p,
+            paired_ref[p, : 2 * depth, :].astype(F32) + z_in[pieces + p].astype(F32),
+        )
 
     back_copy.wait_recv()
     shift_sums = [jnp.zeros((1, width), F32) for _ in range(items)]
@@ -655,15 +684,9 @@
     for copy in late_copies:
         copy.start()
 
-    last_copies = []
     for p in range(pieces):
         z_copies[p].wait_recv()
-        total = z_keep[p].astype(F32) + z_in[p].astype(F32)
-        w_out[p, depth:, :] = jnp.zeros((w_out.shape[1] - depth, piece), BF16)
-        w_out[p, :depth, :] = total[depth:].astype(BF16)
-        last_copies.append(halving(3, p, w_out.at[p], w_in.at[p]))
-        last_copies[p].start()
-        sums_ref[p] = total[:depth]
+        last_level(p, z_keep[p].astype(F32) + z_in[p].astype(F32))
 
     gathered(early_sum, early_all, early_send, early_recv)
     count = dp * items
@@ -697,7 +720,7 @@
         )
         cond_copies[-1].start()
 
-    for p in range(pieces):
+    for p in last_copies:
         last_copies[p].wait_recv()
         sums_ref[p] += w_in[p, :depth, :].astype(F32)
     gathered(cond_out.at[0], cond_ref, cond_send, cond_recv)
@@ -709,12 +732,15 @@
         + core_copies
         + x_copies
         + z_copies
-        + last_copies
+        + paired_copies
+        + list(last_copies.values())
     ):
         copy.wait_send()
 
 
-def tail(dp, d, attn_in, grad_attn, heads_out, w_qkv, tokens, resid, member, scale, early, gains, mod):
+def tail(
+    dp, d, attn_in, grad_attn, heads_out, w_qkv, tokens, resid, member, scale, early, gains, mod, paired, crossed
+):
     half, width = tokens.shape
     items = scale.shape[0]
     length = 2 * half
@@ -728,6 +754,7 @@
     late_rows = items * late_span
     count = dp * items
     columns = mod.shape[1]
+    total = pieces + paired.shape[0] + crossed.shape[0]
     vmem = pltpu.VMEM
 
     def level(rows):
@@ -738,12 +765,12 @@
         functools.partial(tail_kernel, dp, items, pieces),
         out_shape=[
             jax.ShapeDtypeStruct((half, width), BF16),
-            jax.ShapeDtypeStruct((pieces, depth, piece), F32),
+            jax.ShapeDtypeStruct((total, depth, piece), F32),
             jax.ShapeDtypeStruct((count, columns), BF16),
             jax.ShapeDtypeStruct((8, LANES), F32),
             jax.ShapeDtypeStruct((dp, 8, LANES), F32),
         ],
-        in_specs=[pl.BlockSpec(memory_space=pltpu.VMEM)] * 12,
+        in_specs=[pl.BlockSpec(memory_space=pltpu.VMEM)] * 14,
         out_specs=[pl.BlockSpec(memory_space=pltpu.VMEM)] * 5,
         scratch_shapes=[
             vmem((width, 4 * inner), F32),
@@ -752,9 +779,11 @@
             vmem((half, width), F32),
             *level(width // 2),
             *level(width // 4),
-            *level(width // 8),
-            vmem((pieces, group_rows(depth), piece), BF16),
-            vmem((pieces, group_rows(depth), piece), BF16),
+            vmem((pieces, width // 8, piece), BF16),
+            vmem((pieces + paired.shape[0], width // 8, piece), BF16),
+            vmem((pieces, width // 8, piece), BF16),
+            vmem((total, group_rows(depth), piece), BF16),
+            vmem((total, group_rows(depth), piece), BF16),
             vmem((early_rows, LANES), BF16),
             vmem((late_rows, LANES), BF16),
             vmem((late_rows, LANES), BF16),
@@ -766,7 +795,7 @@
             vmem((late_rows, LANES), F32),
             vmem((dp, 8, LANES), F32),
             dma((2, 3)),
-            dma((2, 4, pieces)),
+            dma((2, 4, total)),
             dma((dp,)),
             dma((dp,)),
             dma((dp,)),
@@ -794,7 +823,353 @@
         early,
         gains,
         mod,
+        paired,
+        crossed,
     )
+
+
+def middle_kernel(
+    items,
+    chunk,
+    step,
+    heads_ref,
+    proj_ref,
+    tokens_ref,
+    own_grad_ref,
+    other_grad_ref,
+    own_member_ref,
+    other_member_ref,
+    mod_ref,
+    gate_hbm,
+    up_hbm,
+    down_hbm,
+    grad_heads_ref,
+    grad_attn_ref,
+    grad_resid_ref,
+    resid_ref,
+    early_ref,
+    mlp_other_ref,
+    mlp_own_ref,
+    crossed_ref,
+    paired_ref,
+    gate_ref,
+    up_ref,
+    down_ref,
+    attn,
+    grad_mlp,
+    mlp_in,
+    hidden,
+    grad_gate,
+    grad_up,
+    y_out,
+    y_in,
+    part,
+    core_out,
+    core_keep,
+    core_in,
+    x_out,
+    x_in,
+    y_sems,
+    core_sems,
+    x_sems,
+    load_sems,
+):
+    dp = lax.axis_size("dp")
+    bits = dp.bit_length() - 1
+    me = lax.axis_index("dp")
+    ten = lax.axis_index("tensor")
+    half, width = tokens_ref.shape
+    depth = width // dp
+    units = gate_ref.shape[1]
+    piece = part.shape[1]
+    per_weight = units // piece
+    chunks = half // chunk
+    y_peer = (me, 1 - ten)
+    core_peer = (across(me, 0), ten)
+    x_peer = (across(me, 1), ten)
+    loads = [
+        pltpu.make_async_copy(source, there, load_sems.at[which])
+        for which, (source, there) in enumerate(
+            ((gate_hbm, gate_ref), (up_hbm, up_ref), (down_hbm, down_ref))
+        )
+    ]
+    for load in loads:
+        load.start()
+    greet([y_peer, core_peer, x_peer])
+
+    def rows_at(first, count=chunk):
+        return pl.ds(pl.multiple_of(first, 16), count)
+
+    def y_copy(kind, c, src, dst):
+        return remote(
+            src, dst, y_sems.at[0, kind, c], y_sems.at[1, kind, c], y_peer
+        )
+
+    def mod_row(kind, item):
+        return mod_ref[item : item + 1, kind * width : (kind + 1) * width]
+
+    def token_values(member_ref, rows, kind):
+        return sum(member_ref[rows, item : item + 1] * mod_row(kind, item) for item in range(items))
+
+    def in_steps(c, body):
+        def one(index, carry):
+            body(pl.ds(pl.multiple_of(c * chunk + index * step, step), step))
+            return carry
+
+        lax.fori_loop(0, chunk // step, one, 0)
+
+    proj_copies = []
+    for c in range(chunks):
+        rows = pl.ds(c * chunk, chunk)
+        y_out[rows, :] = dot(
+            heads_ref[rows_at((1 - ten) * half + c * chunk), :], proj_ref[...]
+        ).astype(BF16)
+        proj_copies.append(y_copy(0, c, y_out.at[rows, :], y_in.at[rows, :]))
+        proj_copies[c].start()
+    for c in range(chunks):
+        attn[pl.ds(c * chunk, chunk), :] = dot(
+            heads_ref[rows_at(ten * half + c * chunk), :], proj_ref[...]
+        )
+    for c in range(chunks):
+
+        def scale_grads(rows):
+            later = pl.ds(pl.multiple_of(rows.start + half, step), step)
+            grad_mlp[rows, :] = (
+                token_values(own_member_ref, rows, 5) * own_grad_ref[rows, :].astype(F32)
+            ).astype(BF16)
+            grad_mlp[later, :] = (
+                token_values(other_member_ref, rows, 5) * other_grad_ref[rows, :].astype(F32)
+            ).astype(BF16)
+
+        in_steps(c, scale_grads)
+
+    for load in loads:
+        load.wait()
+
+    def mlp(c):
+        rows = pl.ds(c * chunk, chunk)
+        for first in range(0, units, 256):
+            columns = pl.ds(first, 256)
+            gate = dot(mlp_in[rows, :], gate_ref[:, columns])
+            up = dot(mlp_in[rows, :], up_ref[:, columns])
+            grad = dot_t(grad_mlp[rows, :], down_ref[columns, :])
+            sigma = 1.0 / (1.0 + jnp.exp(-gate))
+            silu = gate * sigma
+            hidden[rows, columns] = (silu * up).astype(BF16)
+            grad_gate[rows, columns] = (
+                grad * up * (sigma * (1.0 + gate * (1.0 - sigma)))
+            ).astype(BF16)
+            grad_up[rows, columns] = (grad * silu).astype(BF16)
+
+    mlp_copies = []
+    for c in range(chunks):
+        proj_copies[c].wait_recv()
+
+        def norm(rows):
+            mixed = attn[rows, :] + y_in[rows, :].astype(F32)
+            attn[rows, :] = mixed
+            resid = tokens_ref[rows, :].astype(F32) + token_values(own_member_ref, rows, 2) * mixed
+            resid_ref[rows, :] = resid
+            normed, _ = layer_norm(resid)
+            mlp_in[rows, :] = (
+                normed * (1.0 + token_values(own_member_ref, rows, 4))
+                + token_values(own_member_ref, rows, 3)
+            ).astype(BF16)
+
+        in_steps(c, norm)
+        mlp_copies.append(
+            y_copy(
+                1, c, mlp_in.at[pl.ds(c * chunk, chunk), :], mlp_in.at[pl.ds(half + c * chunk, chunk), :]
+            )
+        )
+        mlp_copies[c].start()
+    for c in range(chunks):
+        mlp(c)
+    for c in range(chunks):
+        mlp_copies[c].wait_recv()
+        mlp(chunks + c)
+
+    def back(first):
+        rows = pl.ds(first, chunk)
+        return dot_t(grad_gate[rows, :], gate_ref[...]) + dot_t(grad_up[rows, :], up_ref[...])
+
+    back_copies = []
+    for c in range(chunks):
+        rows = pl.ds(c * chunk, chunk)
+        proj_copies[c].wait_send()
+        y_out[rows, :] = back(half + c * chunk).astype(BF16)
+        back_copies.append(y_copy(2, c, y_out.at[rows, :], y_in.at[rows, :]))
+        back_copies[c].start()
+
+    def packed(position):
+        def rows_of(p):
+            return part[pl.ds(pl.multiple_of(block_at(p, me, bits) * depth, 8), depth), :]
+
+        return jnp.concatenate([rows_of(position), rows_of(position + 1)]).astype(BF16)
+
+    core_copies = []
+    x_copies = []
+
+    def weight_grad(p):
+        which, column = divmod(p, per_weight)
+        columns = pl.ds(column * piece, piece)
+        left, right = ((grad_mlp, hidden), (mlp_in, grad_gate), (mlp_in, grad_up))[which]
+        slot = p % 2
+        for first in range(0, width, LANES):
+            rows = pl.ds(first, LANES)
+            part[rows, :] = t_dot(left[:, rows], right[:, columns])
+        if p >= 2:
+            core_copies[p - 2].wait_send()
+        for position in range(0, dp // 2, 2):
+            rows = pl.ds(position * depth, 2 * depth)
+            core_out[slot, rows, :] = packed(dp // 2 + position)
+        core_copies.append(
+            remote(
+                core_out.at[slot], core_in.at[p], core_sems.at[0, p], core_sems.at[1, p], core_peer
+            )
+        )
+        core_copies[p].start()
+        for position in range(0, dp // 2, 2):
+            rows = pl.ds(position * depth, 2 * depth)
+            core_keep[slot, rows, :] = packed(position)
+
+    quarter = width // 4
+
+    def cross(p):
+        slot = p % 2
+        core_copies[p].wait_recv()
+
+        def total(rows):
+            return (core_keep[slot, rows, :].astype(F32) + core_in[p, rows, :].astype(F32)).astype(
+                BF16
+            )
+
+        if p < 2 * per_weight:
+            x_out[p] = total(pl.ds(quarter, quarter))
+            x_copies.append(
+                remote(x_out.at[p], x_in.at[p], x_sems.at[0, p], x_sems.at[1, p], x_peer)
+            )
+            x_copies[p].start()
+            crossed_ref[p] = total(pl.ds(0, quarter))
+        else:
+            paired_ref[p - 2 * per_weight] = total(pl.ds(0, 2 * quarter))
+
+    pieces = 3 * per_weight
+    weight_grad(0)
+    for p in range(1, pieces - 1):
+        weight_grad(p)
+        cross(p - 1)
+    for c in range(chunks):
+        grad_resid_ref[pl.ds(c * chunk, chunk), :] = back(c * chunk)
+
+    early_ref[...] = jnp.zeros_like(early_ref)
+    grad_copies = []
+    for c in range(chunks):
+        back_copies[c].wait_recv()
+
+        def norm_grad(rows):
+            grad = grad_resid_ref[rows, :] + y_in[rows, :].astype(F32)
+            normed, inv = layer_norm(resid_ref[rows, :])
+            n = grad * (1.0 + token_values(own_member_ref, rows, 4))
+            grad_resid = own_grad_ref[rows, :].astype(F32) + norm_back(n, normed, inv)
+            grad_resid_ref[rows, :] = grad_resid
+            there = pl.ds(pl.multiple_of(rows.start + ten * half, step), step)
+            grad_attn_ref[there, :] = (token_values(own_member_ref, rows, 2) * grad_resid).astype(
+                BF16
+            )
+            for kind, values in enumerate((grad_resid * attn[rows, :], grad, grad * normed)):
+                lanes = slice(kind * width, (kind + 1) * width)
+                for item in range(items):
+                    early_ref[item : item + 1, lanes] += jnp.sum(
+                        own_member_ref[rows, item : item + 1] * values, axis=0, keepdims=True
+                    )
+
+        in_steps(c, norm_grad)
+        rows = rows_at(ten * half + c * chunk)
+        grad_copies.append(y_copy(3, c, grad_attn_ref.at[rows, :], grad_attn_ref.at[rows, :]))
+        grad_copies[c].start()
+
+    weight_grad(pieces - 1)
+    cross(pieces - 2)
+    for c in range(chunks):
+        rows = pl.ds(c * chunk, chunk)
+        mlp_other_ref[rows, :] = dot(
+            hidden[pl.ds(half + c * chunk, chunk), :], down_ref[...]
+        ).astype(BF16)
+        mlp_own_ref[rows, :] = dot(hidden[rows, :], down_ref[...])
+        own_rows = rows_at(ten * half + c * chunk)
+        grad_heads_ref[own_rows, :] = dot_t(grad_attn_ref[own_rows, :], proj_ref[...]).astype(BF16)
+    cross(pieces - 1)
+    for c in range(chunks):
+        rows = rows_at((1 - ten) * half + c * chunk)
+        y_copy(3, c, grad_attn_ref.at[rows, :], grad_attn_ref.at[rows, :]).wait_recv()
+        grad_heads_ref[rows, :] = dot_t(grad_attn_ref[rows, :], proj_ref[...]).astype(BF16)
+    for p in range(2 * per_weight):
+        x_copies[p].wait_recv()
+        crossed_ref[p] = (crossed_ref[p].astype(F32) + x_in[p].astype(F32)).astype(BF16)
+    for copy in mlp_copies + back_copies + grad_copies + core_copies[-2:] + x_copies:
+        copy.wait_send()
+
+
+def middle(heads_out, proj, tokens, own_grad, other_grad, own_member, other_member, mod, gate, up, down):
+    half, width = tokens.shape
+    length = 2 * half
+    units = gate.shape[1]
+    inner = heads_out.shape[1]
+    items = mod.shape[0]
+    chunk = half // 2
+    chunks = half // chunk
+    piece = units // 2
+    pieces = 6
+    vmem = pltpu.VMEM
+    dma = pltpu.SemaphoreType.DMA
+    anywhere = pl.BlockSpec(memory_space=pl.ANY)
+    return pl.pallas_call(
+        functools.partial(middle_kernel, items, chunk, 32),
+        out_shape=[
+            jax.ShapeDtypeStruct((length, inner), BF16),
+            jax.ShapeDtypeStruct((length, width), BF16),
+            jax.ShapeDtypeStruct((half, width), F32),
+            jax.ShapeDtypeStruct((half, width), F32),
+            jax.ShapeDtypeStruct((8, 3 * width), F32),
+            jax.ShapeDtypeStruct((half, width), BF16),
+            jax.ShapeDtypeStruct((half, width), F32),
+            jax.ShapeDtypeStruct((4, width // 4, piece), BF16),
+            jax.ShapeDtypeStruct((2, width // 2, piece), BF16),
+        ],
+        in_specs=[pl.BlockSpec(memory_space=pltpu.VMEM)] * 8 + [anywhere] * 3,
+        out_specs=[pl.BlockSpec(memory_space=pltpu.VMEM)] * 9,
+        scratch_shapes=[
+            vmem((width, units), BF16),
+            vmem((width, units), BF16),
+            vmem((units, width), BF16),
+            vmem((half, width), F32),
+            vmem((length, width), BF16),
+            vmem((length, width), BF16),
+            vmem((length, units), BF16),
+            vmem((length, units), BF16),
+            vmem((length, units), BF16),
+            vmem((half, width), BF16),
+            vmem((half, width), BF16),
+            vmem((width, piece), F32),
+            vmem((2, width // 2, piece), BF16),
+            vmem((2, width // 2, piece), BF16),
+            vmem((pieces, width // 2, piece), BF16),
+            vmem((4, width // 4, piece), BF16),
+            vmem((4, width // 4, piece), BF16),
+            dma((2, 4, chunks)),
+            dma((2, pieces)),
+            dma((2, 4)),
+            dma((3,)),
+        ],
+        compiler_params=pltpu.CompilerParams(
+            collective_id=2, has_side_effects=True, vmem_limit_bytes=62 * 2**20
+        ),
+        cost_estimate=pl.CostEstimate(
+            flops=18 * length * width * units, bytes_accessed=30 * 2**20, transcendentals=0
+        ),
+        name="middle",
+    )(heads_out, proj, tokens, own_grad, other_grad, own_member, other_member, mod, gate, up, down)
 
 
 def shards(
@@ -855,80 +1230,47 @@
 
     w_qkv = jnp.concatenate([query_weight, key_weight, value_weight], axis=1)
     heads_out, *saved = attend(spans, attn_in, w_qkv, gain_q, gain_k, cosine, sine)
-    heads_other = lax.dynamic_slice_in_dim(heads_out, other_first, half, 0)
-    heads_own = lax.dynamic_slice_in_dim(heads_out, own_first, half, 0)
-    attn_recv = swap(dot(heads_other, proj_weight).astype(BF16))
-    attn_out = dot(heads_own, proj_weight) + attn_recv.astype(F32)
-
-    gate_one_own = per_token(member_own, gate_one)
-    scale_two_own = per_token(member_own, scale_two)
-    resid = tokens_float + gate_one_own * attn_out
-    norm_two, inv_two = layer_norm(resid)
-    mlp_in = (norm_two * (1.0 + scale_two_own) + per_token(member_own, shift_two)).astype(BF16)
-    mlp_in_all = jnp.concatenate([mlp_in, swap(mlp_in)])
-
+    inner = heads_out.shape[1]
     grad_out = out_grad.astype(F32)
     gate_two_own = per_token(member_own, gate_two)
-    grad_mlp_all = jnp.concatenate(
-        [
-            (gate_two_own * grad_out).astype(BF16),
-            (per_token(member_other, gate_two) * out_grad_other.astype(F32)).astype(BF16),
-        ]
-    )
-    grad_hidden = dot_t(grad_mlp_all, down_weight)
-
-    gate_pre = dot(mlp_in_all, gate_weight)
-    up_pre = dot(mlp_in_all, up_weight)
-    silu_gate = jax.nn.silu(gate_pre)
-    hidden = (silu_gate * up_pre).astype(BF16)
-    grad_gate_pre = (grad_hidden * up_pre * silu_grad(gate_pre)).astype(BF16)
-    grad_up_pre = (grad_hidden * silu_gate).astype(BF16)
-
-    back_other = dot_t(grad_gate_pre[half:], gate_weight) + dot_t(grad_up_pre[half:], up_weight)
-    back_recv = swap(back_other.astype(BF16))
-    mlp_recv = swap(dot(hidden[half:], down_weight).astype(BF16))
-    grad_mlp_in = (
-        dot_t(grad_gate_pre[:half], gate_weight)
-        + dot_t(grad_up_pre[:half], up_weight)
-        + back_recv.astype(F32)
-    )
-
-    grad_mlp_rows = halving_rows(grad_mlp_all, bits)
-    mlp_in_rows = halving_rows(mlp_in_all, bits)
-    down_part = first_halving(grad_mlp_rows, hidden)
-    gate_part = first_halving(mlp_in_rows, grad_gate_pre)
-    up_part = first_halving(mlp_in_rows, grad_up_pre)
-
-    mlp_out = dot(hidden[:half], down_weight) + mlp_recv.astype(F32)
-    block_out = (resid + gate_two_own * mlp_out).astype(BF16)
-
-    grad_resid = grad_out + norm_back(grad_mlp_in * (1.0 + scale_two_own), norm_two, inv_two)
-    grad_attn = (gate_one_own * grad_resid).astype(BF16)
-    grad_attn_all = in_order(grad_attn, swap(grad_attn), second)
-    grad_heads = dot_t(grad_attn_all, proj_weight).astype(BF16)
-    grad_heads, down_part, gate_part, up_part = lax.optimization_barrier(
-        (grad_heads, down_part, gate_part, up_part)
-    )
-    grad_down = rest_of_halving(down_part, bits).T
-    grad_gate = rest_of_halving(gate_part, bits)
-    grad_up = rest_of_halving(up_part, bits)
-    d, gain_parts = attend_back(spans, grad_heads, saved, gain_q, gain_k, cosine, sine)
-    early = jnp.concatenate(
-        [
-            per_item(member_own, grad_resid * attn_out),
-            per_item(member_own, grad_mlp_in),
-            per_item(member_own, grad_mlp_in * norm_two),
-            per_item(member_own, grad_out * mlp_out),
-        ],
-        axis=1,
-    )
-    inner = heads_out.shape[1]
 
     if dp == 16 and owned % 8 == 0:
+        (
+            grad_heads,
+            grad_attn_all,
+            grad_resid,
+            resid,
+            early,
+            mlp_other,
+            mlp_own,
+            crossed,
+            paired,
+        ) = middle(
+            heads_out,
+            proj_weight,
+            tokens,
+            out_grad,
+            out_grad_other,
+            member_own,
+            member_other,
+            modulation,
+            gate_weight,
+            up_weight,
+            down_weight,
+        )
+        mlp_recv = swap(mlp_other)
+        fifth = crossed.shape[1] // 2
+        crossed_recv = lax.ppermute(crossed[:, fifth:], "dp", partners(2))
+        sixth = paired.shape[1] // 2
+        paired_recv = lax.ppermute(paired[:, sixth:], "dp", partners(1))
+        d, gain_parts = attend_back(spans, grad_heads, saved, gain_q, gain_k, cosine, sine)
+        mlp_out = mlp_own + mlp_recv.astype(F32)
+        block_out = (resid + gate_two_own * mlp_out).astype(BF16)
+        early = jnp.concatenate([early[:items], per_item(member_own, grad_out * mlp_out)], axis=1)
         groups = 4 * width // LANES
         early = early.reshape(items, groups, LANES)
         early = jnp.pad(early, ((0, 0), (0, group_rows(groups) - groups), (0, 0)))
-        grad_tokens, attn_sum, grad_mod_all, gain_sums, cond_parts = tail(
+        grad_tokens, sums, grad_mod_all, gain_sums, cond_parts = tail(
             dp,
             d,
             attn_in,
@@ -942,11 +1284,81 @@
             early.reshape(-1, LANES).astype(BF16),
             gain_parts,
             mod_weight,
-        )
-        attn_sum = jnp.concatenate(list(attn_sum), axis=1)
+            (paired[:, :sixth].astype(F32) + paired_recv.astype(F32)).astype(BF16),
+            (crossed[:, :fifth].astype(F32) + crossed_recv.astype(F32)).astype(BF16),
+        )
+        attn_sum = jnp.concatenate(list(sums[:3]), axis=1)
+        grad_up = jnp.concatenate(list(sums[3:5]), axis=1)
+        grad_down = jnp.concatenate(list(sums[5:7]), axis=1).T
+        grad_gate = jnp.concatenate(list(sums[7:9]), axis=1)
         cond_parts = cond_parts[:, :items, :owned]
     else:
-
+        heads_other = lax.dynamic_slice_in_dim(heads_out, other_first, half, 0)
+        heads_own = lax.dynamic_slice_in_dim(heads_out, own_first, half, 0)
+        attn_recv = swap(dot(heads_other, proj_weight).astype(BF16))
+        attn_out = dot(heads_own, proj_weight) + attn_recv.astype(F32)
+
+        gate_one_own = per_token(member_own, gate_one)
+        scale_two_own = per_token(member_own, scale_two)
+        resid = tokens_float + gate_one_own * attn_out
+        norm_two, inv_two = layer_norm(resid)
+        mlp_in = (norm_two * (1.0 + scale_two_own) + per_token(member_own, shift_two)).astype(BF16)
+        mlp_in_all = jnp.concatenate([mlp_in, swap(mlp_in)])
+
+        grad_mlp_all = jnp.concatenate(
+            [
+                (gate_two_own * grad_out).astype(BF16),
+                (per_token(member_other, gate_two) * out_grad_other.astype(F32)).astype(BF16),
+            ]
+        )
+        grad_hidden = dot_t(grad_mlp_all, down_weight)
+
+        gate_pre = dot(mlp_in_all, gate_weight)
+        up_pre = dot(mlp_in_all, up_weight)
+        silu_gate = jax.nn.silu(gate_pre)
+        hidden = (silu_gate * up_pre).astype(BF16)
+        grad_gate_pre = (grad_hidden * up_pre * silu_grad(gate_pre)).astype(BF16)
+        grad_up_pre = (grad_hidden * silu_gate).astype(BF16)
+
+        back_other = dot_t(grad_gate_pre[half:], gate_weight) + dot_t(grad_up_pre[half:], up_weight)
+        back_recv = swap(back_other.astype(BF16))
+        mlp_recv = swap(dot(hidden[half:], down_weight).astype(BF16))
+        grad_mlp_in = (
+            dot_t(grad_gate_pre[:half], gate_weight)
+            + dot_t(grad_up_pre[:half], up_weight)
+            + back_recv.astype(F32)
+        )
+
+        grad_mlp_rows = halving_rows(grad_mlp_all, bits)
+        mlp_in_rows = halving_rows(mlp_in_all, bits)
+        down_part = first_halving(grad_mlp_rows, hidden)
+        gate_part = first_halving(mlp_in_rows, grad_gate_pre)
+        up_part = first_halving(mlp_in_rows, grad_up_pre)
+
+        mlp_out = dot(hidden[:half], down_weight) + mlp_recv.astype(F32)
+        block_out = (resid + gate_two_own * mlp_out).astype(BF16)
+
+        grad_resid = grad_out + norm_back(grad_mlp_in * (1.0 + scale_two_own), norm_two, inv_two)
+        grad_attn = (gate_one_own * grad_resid).astype(BF16)
+        grad_attn_all = in_order(grad_attn, swap(grad_attn), second)
+        grad_heads = dot_t(grad_attn_all, proj_weight).astype(BF16)
+        grad_heads, down_part, gate_part, up_part = lax.optimization_barrier(
+            (grad_heads, down_part, gate_part, up_part)
+        )
+        grad_down = rest_of_halving(down_part, bits).T
+        grad_gate = rest_of_halving(gate_part, bits)
+        grad_up = rest_of_halving(up_part, bits)
+        d, gain_parts = attend_back(spans, grad_heads, saved, gain_q, gain_k, cosine, sine)
+
+        early = jnp.concatenate(
+            [
+                per_item(member_own, grad_resid * attn_out),
+                per_item(member_own, grad_mlp_in),
+                per_item(member_own, grad_mlp_in * norm_two),
+                per_item(member_own, grad_out * mlp_out),
+            ],
+            axis=1,
+        )
         def attn_back(first):
             return dot_t(lax.dynamic_slice_in_dim(d, first, half, 0), w_qkv)
 

time: 502 us -> 361 us (0.72)
  waiting for transfers between devices: 117 us -> 4.97 us
  Pallas kernels: 134 us -> 240 us
  matrix products: 72.8 us -> 4.62 us
  local copies, waits for them, and re-layouts: 58.8 us -> 30.6 us
  other arithmetic: 59.5 us -> 32.8 us
  starting transfers between devices: 22.7 us -> 13.9 us
    pallas_call x0 -> x1, Pallas kernels: none -> 104 us  [middle(): pl.pallas_call(functools.partial(middle_kernel, items, chunk, 32), out_sh...]
    ppermute x12 -> x2, waiting for transfers between devices: 74.4 us -> 0.01 us  [the longest x1 0.01 us: shards(): crossed_recv = lax.ppermute(crossed[:, fifth:], 'dp', partners(2))]
    dot_general x13 -> x1, matrix products: 49.8 us -> 1.7 us  [dot(): return jnp.dot(left, right, preferred_element_type=F32)]
    ppermute x7 -> x3, waiting for transfers between devices: 42.1 us -> 0.01 us  [swap(): return lax.ppermute(values, 'tensor', [(0, 1), (1, 0)])]
    dot_general x6 -> x0, matrix products: 20.5 us -> none  [dot_t(): lax.dot_general(left, right, (((1,), (1,)), ((), ())), preferred_element_...]
    transpose x2 -> x0, local copies, waits for them, and re-layouts: 8.12 us -> none  [halving_rows(): blocks = values.T.reshape((2,) * bits + (depth, values.shape[0]))]
    unnamed x128 -> x34, local copies, waits for them, and re-layouts: 14.1 us -> 6.82 us
    select_n x6 -> x0, other arithmetic: 6.16 us -> none  [halving_rows(): blocks = jnp.where(me >> bit & 1 == 1, jnp.flip(blocks, axis), blocks)]
  transfers between devices with their start and end apart: 20 -> 6, of which waited for: 11 -> 1; matrix products, arithmetic and copies ran while one was open for 27% -> 15% of each run, Pallas kernels for 5% -> 14%
where the time goes in v3:
time: 361 us; the launch traced here: 354 us
  Pallas kernels  240 us (66%)
  other arithmetic  32.8 us (9%)
  local copies, waits for them, and re-layouts  30.6 us (8%)
  blocking collectives  23.7 us (7%)
  starting transfers between devices  13.9 us (4%)
  waiting for transfers between devices  4.97 us (1%)
  matrix products  4.62 us (1%)
    pallas_call x1, Pallas kernels, middle(): pl.pallas_call(functools.partial(middle_kernel, items, chunk, 32), out_sh...  104 us
    pallas_call x1, Pallas kernels, tail(): pl.pallas_call(functools.partial(tail_kernel, dp, items, pieces), out_sha...  85.1 us
    pallas_call x1, Pallas kernels, attend_back(): pl.pallas_call(functools.partial(attend_back_kernel, heads, items), grid_...  26.1 us
    pallas_call x1, Pallas kernels, attend(): pl.pallas_call(functools.partial(attend_kernel, heads, items), grid_spec=...  24.7 us
    all_gather x1, blocking collectives, shards(): cond_all = lax.all_gather(conditions, 'dp', axis=0, tiled=True)  23.7 us
    convert_element_type x1, other arithmetic, shards(): attn_in = (norm_all * (1.0 + per_token(member, scale_one)) + per_token(me...  8.27 us
  transfers between devices with their start and end apart: 6, of which 1 were waited for; matrix products, arithmetic and copies ran while one was open for 15% of the time, Pallas kernels for 14%

profile of v3, /device:TPU:0, one launch (start us, length us, event | category | flops | bytes accessed | tf_op | source)
XLA Modules:
  0.0 353.8 jit_solution(13451958693396418657)
XLA Ops:
  0.6 23.7 %all-gather = bf16[16,3,1152]{2,1,0:T(4,128)(2,1)S(1)} all-gather(bf16[1,3,1152]{2,1,0:T(4,128)(2,1)} %bitcast.48), channel_id=1, replica_groups=mesh['dp'=16,'tensor'=2] {'dp'}, dimensions={0}, use_global_device_ids=true | all-gather | bytes 117504 | tf_op jit(solution)/shard_map/all_gather | solution.py:1212
  24.4 0.1 reshape.187
  24.4 0.0 copy-start.8
  24.5 1.7 fusion.20
  26.2 1.5 reshape.182
  27.7 4.6 %all-to-all-start = ((f32[16,3,6912]{2,1,0:T(4,128)}), f32[16,3,6912]{2,1,0:T(4,128)}, u32[]{:S(2)}, u32[]{:S(2)}) async-start(f32[16,3,6912]{2,1,0:T(4,128)} %reshape.182), calls=%async_computation | async-start | bytes 3538944 | tf_op jit(solution)/shard_map/all_to_all | solution.py:1216
  32.2 1.6 collective-permute-start
  33.8 0.5 collective-permute-start.1
  34.4 0.6 fusion.23
  36.3 0.7 compare_and_fusion.1
  37.6 0.7 add_bitcast_fusion
  38.3 0.6 pad_add_fusion.1.spans
  38.9 0.2 copy.34
  39.2 1.1 copy.35
  40.4 2.1 copy.36
  42.5 2.6 copy.37
  45.1 7.0 %concatenate.27.w_ref = bf16[1152,1728]{1,0:T(8,128)(2,1)} concatenate(bf16[1152,576]{1,0:T(8,128)(2,1)S(1)} %copy.35, bf16[1152,576]{1,0:T(8,128)(2,1)S(1)} %copy.36, bf16[1152,576]{1,0:T(8,128)(2,1)} %copy.37), dimensions={1} | concatenate | bytes 7962624 | tf_op jit(solution)/shard_map/concatenate | solution.py:1231
  52.1 0.5 pad_bitcast_fusion
  52.6 0.6 fusion.22
  53.2 2.7 add_select_fusion
  55.9 0.8 constant_dynamic-slice_fusion
  56.7 0.6 slice_reduce_fusion.2
  57.3 2.8 sine_select_fusion
  60.1 0.0 collective-permute-done
  60.1 1.6 broadcast_select_fusion.1
  61.7 0.3 convert_reduce_fusion
  62.1 0.6 fusion.2
  62.7 5.0 %all-to-all-done = f32[16,3,6912]{2,1,0:T(4,128)} async-done(((f32[16,3,6912]{2,1,0:T(4,128)}), f32[16,3,6912]{2,1,0:T(4,128)}, u32[]{:S(2)}, u32[]{:S(2)}) %all-to-all-start) | async-done | bytes 1327136 | tf_op jit(solution)/shard_map/all_to_all | solution.py:1216
  67.6 1.7 reduce_sum.56.mod_ref
  69.4 0.0 copy-start.9
  69.4 0.7 slice_reduce_fusion.5
  70.1 8.3 %fusion.5.x_ref.attn_in_ref = bf16[768,1152]{1,0:T(8,128)(2,1)} fusion(f32[1152]{0:T(1024)S(1)} %get-tuple-element.71, f32[1152]{0:T(1024)S(1)} %get-tuple-element.72, f32[1152]{0:T(1024)S(1)} %get-tuple-element.73, f32[1152]{0:T(1024)S(1)} %get-tuple-element.74, f32[768]{0:T(1024)S(1)} %get-tuple-element.66, f32[1152]{0:T(1024)S(1)} %get-tuple-element.75, ...), kind=kLoop, calls=%fused_computation.7 | loop fusion | flops 17694720 | bytes 3581952 | tf_op jit(solution)/shard_map/convert_element_type | solution.py:1229
  78.3 24.7 %attend.1 = (bf16[768,576]{1,0:T(8,128)(2,1)}, f32[8,768,128]{2,1,0:T(8,128)}, f32[8,768,128]{2,1,0:T(8,128)}, bf16[8,768,128]{2,1,0:T(8,128)(2,1)}, bf16[8,768,...) custom-call(s32[2,3]{1,0:T(2,128)} %pad_add_fusion.1.spans, ...), custom_call_target="tpu_custom_call" | custom-call | flops 3862953984 | bytes 25165824 | tf_op jit(solution)/shard_map/attend/pallas_call | solution.py:264
  103.0 0.0 collective-permute-done.1.other_grad_ref
  103.0 104.3 %middle.1 = (bf16[768,576]{1,0:T(8,128)(2,1)}, bf16[768,1152]{1,0:T(8,128)(2,1)}, f32[384,1152]{1,0:T(8,128)}, f32[384,1152]{1,0:T(8,128)}, f32[8,3456]{1,0:T(8,...) custom-call(bf16[768,576]{1,0:T(8,128)(2,1)} %get-tuple-element.36.h, ...), custom_call_target="tpu_custom_call" | custom-call | flops 24461180928 | bytes 31457280 | tf_op jit(solution)/shard_map/middle/pallas_call | solution.py:1127
  207.3 1.6 collective-permute-start.2
  208.9 0.4 dynamic-slice_reduce_fusion.2
  209.2 1.5 split.6.scale_ref
  210.7 0.9 slice.222
  211.6 2.1 slice.176
  213.8 0.5 collective-permute-start.3
  214.3 1.0 slice.178
  215.3 5.1 %collective-permute-start.4 = (bf16[4,144,768]{2,1,0:T(8,128)(2,1)}, bf16[4,144,768]{2,1,0:T(8,128)(2,1)}, u32[]{:S(2)}, u32[]{:S(2)}) collective-permute-start(bf16[4,144,768]{2,1,0:T(8,128)(2,1)} %slice.178), channel_id=1, source_target_pairs={{0,8},{2,10},{4,12},{6,14},{8,0},{10,2},{12,4},{14,6},{16,24},{18,... | collective-permute-start | bytes 2654216 | tf_op jit(solution)/shard_map/ppermute | solution.py:1263
  220.4 26.1 %attend_back.1 = (bf16[768,1728]{1,0:T(8,128)(2,1)}, f32[8,128]{1,0:T(8,128)}) custom-call(s32[2,3]{1,0:T(2,128)} %pad_add_fusion.1.spans, bf16[768,576]{1,0:T(8,128)(2,1)} %get-tuple-element.40.grad_ref, f32[8,768,128]{2,1,0:T(8,128)} %get-tuple-element.41.qpre_ref, f32[8,768,128]{2,1,0:T(8,128)} %get-tuple-element.42.kpre_ref, ...), custom_call_target="tpu_custom_call" | custom-call | flops 1610612736 | bytes 25165824 | tf_op jit(solution)/shard_map/attend_back/pallas_call | solution.py:317
  246.6 0.0 collective-permute-done.2
  246.6 3.4 multiply_reduce_fusion.2
  250.0 0.7 maximum_maximum_fusion
  250.7 1.4 reshape.183
  252.1 1.4 pad.14
  253.5 2.3 add_convert_fusion.1.paired_ref
  255.8 0.0 collective-permute-done.4
  255.8 2.3 add_convert_fusion.crossed_ref
  258.1 85.1 %tail.1 = (bf16[384,1152]{1,0:T(8,128)(2,1)}, f32[9,72,768]{2,1,0:T(8,128)}, bf16[48,6912]{1,0:T(8,128)(2,1)}, f32[8,128]{1,0:T(8,128)}, f32[16,8,128]{2,1,0:T(8,128)}) custom-call(bf16[768,1728]{1,0:T(8,128)(2,1)} %get-tuple-element.47.d_ref, bf16[768,1152]{1,0:T(8,128)(2,1)} %fusion.5.x_ref.attn_in_ref, bf16[768,1152]{1,0:T(8,128)(2,1)} %get-tuple-element.48.grad_attn_ref, ...), custom_call_target="tpu_custom_call" | custom-call | flops 8153726976 | bytes 20971520 | tf_op jit(solution)/shard_map/tail/pallas_call | solution.py:764
  343.2 1.0 slice_bitcast_fusion.10
  344.2 0.1 reshape.184
  344.3 0.6 fusion.11
  344.9 2.9 fusion.21
  347.9 0.1 slice_bitcast_fusion.1
  348.0 1.3 slice_bitcast_fusion.11
  349.3 0.8 pad_maximum_fusion.1
  350.1 0.8 pad_maximum_fusion.2
  350.9 0.8 maximum_bitcast_fusion
  351.7 1.0 slice_bitcast_fusion.9
  352.6 0.9 copy.40
  (42 shorter events, 0.2 us)
Async XLA Ops:
  24.4 3.2 copy-start.8
  27.7 6.7 %copy-start.12 = (s32[3,2]{0,1:T(2,128)S(1)}, s32[3,2]{0,1:T(2,128)}, u32[]{:S(2)}) copy-start(s32[3,2]{0,1:T(2,128)} %param.16) | copy-start | bytes 76
  27.7 11.5 %copy-start.6 = (bf16[1152,576]{0,1:T(8,128)(2,1)S(1)}, bf16[1152,576]{0,1:T(8,128)(2,1)}, u32[]{:S(2)}) copy-start(bf16[1152,576]{0,1:T(8,128)(2,1)} %param.18) | copy-start | bytes 3981316
  27.7 39.9 %all-to-all-start = ((f32[16,3,6912]{2,1,0:T(4,128)}), f32[16,3,6912]{2,1,0:T(4,128)}, u32[]{:S(2)}, u32[]{:S(2)}) async-start(f32[16,3,6912]{2,1,0:T(4,128)} %reshape.182), calls=%async_computation | async-start | bytes 3538944 | tf_op jit(solution)/shard_map/all_to_all | solution.py:1216
  32.2 27.9 %collective-permute-start = (bf16[384,1152]{1,0:T(8,128)(2,1)}, bf16[384,1152]{1,0:T(8,128)(2,1)}, u32[]{:S(2)}, u32[]{:S(2)}) collective-permute-start(bf16[384,1152]{1,0:T(8,128)(2,1)} %tokens_ref.3), channel_id=1, source_target_pairs={{0,1},{1,0},{2,3},{3,2},{4,5},{5,4},{6,7},{7,6},{8,9},{9,8},{10,11... | collective-permute-start | bytes 2654216 | tf_op jit(solution)/shard_map/ppermute | solution.py:386
  33.8 69.2 %collective-permute-start.1 = (bf16[384,1152]{1,0:T(8,128)(2,1)}, bf16[384,1152]{1,0:T(8,128)(2,1)}, u32[]{:S(2)}, u32[]{:S(2)}) collective-permute-start(bf16[384,1152]{1,0:T(8,128)(2,1)} %own_grad_ref.1), channel_id=1, source_target_pairs={{0,1},{1,0},{2,3},{3,2},{4,5},{5,4},{6,7},{7,6},{8,9},{9,8},{10,11... | collective-permute-start | bytes 2654216 | tf_op jit(solution)/shard_map/ppermute | solution.py:386
  45.1 7.0 %copy-start.13 = (f32[72]{0:T(128)S(1)}, f32[72]{0:T(128)}, u32[]{:S(2)}) copy-start(f32[72]{0:T(128)} %param.23) | copy-start | bytes 868
  45.1 7.0 %copy-start.14 = (f32[72]{0:T(128)S(1)}, f32[72]{0:T(128)}, u32[]{:S(2)}) copy-start(f32[72]{0:T(128)} %param.22) | copy-start | bytes 868
  69.4 8.9 %copy-start.9 = (f32[3,6912]{1,0:T(4,128)}, f32[3,6912]{1,0:T(4,128)S(1)}, u32[]{:S(2)}) copy-start(f32[3,6912]{1,0:T(4,128)S(1)} %reduce_sum.56.mod_ref) | copy-start | bytes 248836
  207.3 39.2 %collective-permute-start.2 = (bf16[384,1152]{1,0:T(8,128)(2,1)}, bf16[384,1152]{1,0:T(8,128)(2,1)S(1)}, u32[]{:S(2)}, u32[]{:S(2)}) collective-permute-start(bf16[384,1152]{1,0:T(8,128)(2,1)} %get-tuple-element.39), channel_id=1, source_target_pairs={{0,1},{1,0},{2,3},{3,2},{4,5},{5,4},{6,7},{7,6},{8,9},{9,8},{10,11... | collective-permute-start | bytes 2654216 | tf_op jit(solution)/shard_map/ppermute | solution.py:386
  208.9 5.5 %copy-start.3 = (bf16[4,288,768]{2,1,0:T(8,128)(2,1)S(1)}, bf16[4,288,768]{2,1,0:T(8,128)(2,1)}, u32[]{:S(2)}) copy-start(bf16[4,288,768]{2,1,0:T(8,128)(2,1)} %get-tuple-element.53) | copy-start | bytes 5308420
  213.8 39.7 %collective-permute-start.3 = (bf16[2,288,768]{2,1,0:T(8,128)(2,1)}, bf16[2,288,768]{2,1,0:T(8,128)(2,1)}, u32[]{:S(2)}, u32[]{:S(2)}) collective-permute-start(bf16[2,288,768]{2,1,0:T(8,128)(2,1)} %slice.176), channel_id=1, source_target_pairs={{0,4},{2,6},{4,0},{6,2},{8,12},{10,14},{12,8},{14,10},{16,20},{18,... | collective-permute-start | bytes 2654216 | tf_op jit(solution)/shard_map/ppermute | solution.py:1265
  215.3 40.5 %collective-permute-start.4 = (bf16[4,144,768]{2,1,0:T(8,128)(2,1)}, bf16[4,144,768]{2,1,0:T(8,128)(2,1)}, u32[]{:S(2)}, u32[]{:S(2)}) collective-permute-start(bf16[4,144,768]{2,1,0:T(8,128)(2,1)} %slice.178), channel_id=1, source_target_pairs={{0,8},{2,10},{4,12},{6,14},{8,0},{10,2},{12,4},{14,6},{16,24},{18,... | collective-permute-start | bytes 2654216 | tf_op jit(solution)/shard_map/ppermute | solution.py:1263
  220.4 26.1 %copy-start.1 = (f32[384,1152]{1,0:T(8,128)S(1)}, f32[384,1152]{1,0:T(8,128)}, u32[]{:S(2)}) copy-start(f32[384,1152]{1,0:T(8,128)} %get-tuple-element.37) | copy-start | bytes 5308420
  220.4 26.1 %copy-start.2 = (f32[384,1152]{1,0:T(8,128)S(1)}, f32[384,1152]{1,0:T(8,128)}, u32[]{:S(2)}) copy-start(f32[384,1152]{1,0:T(8,128)} %get-tuple-element.38) | copy-start | bytes 5308420
  220.4 26.1 %copy-start.11 = (f32[1152]{0:T(1024)S(1)}, f32[1152]{0:T(1024)}, u32[]{:S(2)}) copy-start(f32[1152]{0:T(1024)} %get-tuple-element.70) | copy-start | bytes 13828
  246.6 6.9 %copy-start.5 = (bf16[2,576,768]{2,1,0:T(8,128)(2,1)S(1)}, bf16[2,576,768]{2,1,0:T(8,128)(2,1)}, u32[]{:S(2)}) copy-start(bf16[2,576,768]{2,1,0:T(8,128)(2,1)} %get-tuple-element.52) | copy-start | bytes 5308420
  250.0 5.8 %copy-start.4 = (bf16[4,288,768]{2,1,0:T(8,128)(2,1)S(1)}, bf16[4,288,768]{2,1,0:T(8,128)(2,1)}, u32[]{:S(2)}) copy-start(bf16[4,288,768]{2,1,0:T(8,128)(2,1)} %get-tuple-element.53) | copy-start | bytes 5308420
  258.1 86.2 %copy-start.10 = (bf16[3,1152]{1,0:T(4,128)(2,1)S(1)}, bf16[3,1152]{1,0:T(4,128)(2,1)}, u32[]{:S(2)}) copy-start(bf16[3,1152]{1,0:T(4,128)(2,1)} %param.15) | copy-start | bytes 20740
  343.2 4.7 %copy-start = (f32[9,72,768]{2,1,0:T(8,128)S(1)}, f32[9,72,768]{2,1,0:T(8,128)}, u32[]{:S(2)}) copy-start(f32[9,72,768]{2,1,0:T(8,128)} %get-tuple-element.57) | copy-start | bytes 5971972
  350.1 2.6 copy-start.7
